TPU v7x, 32 devices: a whole 2x2x4 slice. The times are simulated.
32 devices in a mesh: clus: 8 (over z, x), sub: 4 (over y, core).
Axes of the slice: x: 2, y: 2, z: 4, core: 2. Of those that a mesh axis runs over, the one named last changes fastest.
Arguments:
- forward_rhs: bfloat16 [256, 32, 256], P('clus', 'sub'), may hold values from -6 to 6
- adjoint_rhs: bfloat16 [256, 32, 256], P('clus', 'sub'), may hold values from -6 to 6
- far_clusters: int32 [2, 4096], P(None, ('clus', 'sub')), may hold values from 0 to 255, as said below
- far_ranks: int32 [4096], P(('clus', 'sub')), may hold values from 0 to 32, as said below
- far_left: bfloat16 [4096, 2, 32, 128], P(('clus', 'sub')), may hold values from -0.25 to 0.25
- far_right: bfloat16 [4096, 2, 32, 128], P(('clus', 'sub')), may hold values from -0.5 to 0.5
- near_clusters: int32 [2, 1024], P(None, ('clus', 'sub')), may hold values from 0 to 255, as said below
- near_blocks: bfloat16 [1024, 2, 128, 128], P(('clus', 'sub')), may hold values from -0.125 to 0.125
- panel_params: int32 [4, 32768], P(None, 'clus'), may hold values from 0 to 4095, as said below
- panel_weights: float32 [4, 32768], P(None, 'clus'), may hold values from -6 to 6
- panel_counts: int32 [32768], P('clus'), may hold values from 1 to 4
Outputs:
- forward_field: float32 [256, 32, 256], P('clus', 'sub')
- adjoint_field: float32 [256, 32, 256], P('clus', 'sub')
- param_gradient: float32 [4096], P(('clus', 'sub'))
Inputs may be any that keep to these rules, and one draw needn't show every extreme that they name: `far_clusters`: block slot b belongs to device b // 128; its row cluster lies in row group g = (b // 128) // 4, among clusters 32 * g to 32 * g + 31; its column cluster is the row cluster plus d modulo 256 with 2 <= |d| <= 32. `far_ranks`: 0 marks an empty slot; on each device the live slots come first. `near_clusters`: block slot b belongs to device b // 32; its row cluster lies in row group (b // 32) // 4; its column cluster is the row cluster plus d modulo 256 with |d| <= 1. panel_params[0,p] equals p // 8 plus an offset of -3 to 3, modulo 4096; the other slots may name any shape parameter.
All inputs are finite; a program needn't handle non-finite values.
Results may differ from a plain program's by a relative error of at most 0.0036.
Values may be sent and summed in bfloat16 or wider, within the bound.
No kernel may reach another device: no remote copies, remote signals or barrier semaphores. Data moves between devices by JAX's collectives and lax.ppermute only.
A program may use at most 128 MiB of HBM per device.

v0:
```python
import jax
import jax.numpy as jnp
from jax import lax
from jax.sharding import PartitionSpec as P

PAR_DEV = 128


def extended(x, sides, width):
    for axis, dim in sides:
        devices, length = (lax.axis_size(axis), x.shape[dim])
        up = [(i, (i + 1) % devices) for i in range(devices)]
        down = [(j, i) for i, j in up]
        last = lax.slice_in_dim(x, length - width, length, axis=dim)
        leading = lax.slice_in_dim(x, 0, width, axis=dim)
        before = lax.ppermute(last, axis, up)
        after = lax.ppermute(leading, axis, down)
        x = jnp.concatenate([before, x, after], axis=dim)
    return x


def shifted(x, axis, by):
    devices = lax.axis_size(axis)
    return lax.ppermute(x, axis, [(i, (i + by) % devices) for i in range(devices)])


def complex_mix(lhs_data, rhs_factor, einsum_form):
    width = lhs_data.shape[-1] // 2
    real_lhs = lhs_data[..., :width]
    imag_lhs = lhs_data[..., width:]
    real_rhs = rhs_factor[:, 0]
    imag_rhs = rhs_factor[:, 1]
    real_out = jnp.einsum(
        einsum_form, real_lhs, real_rhs, preferred_element_type=jnp.float32
    ) - jnp.einsum(einsum_form, imag_lhs, imag_rhs, preferred_element_type=jnp.float32)
    imag_out = jnp.einsum(
        einsum_form, real_lhs, imag_rhs, preferred_element_type=jnp.float32
    ) + jnp.einsum(einsum_form, imag_lhs, real_rhs, preferred_element_type=jnp.float32)
    return jnp.concatenate([real_out, imag_out], axis=-1)


def rank_columns(rank_list, width):
    column_ids = lax.broadcasted_iota(jnp.int32, (rank_list.shape[0], width), 1)
    kept = (column_ids < rank_list[:, None]).astype(jnp.float32)
    return jnp.concatenate([kept, kept], axis=1)[:, None, :]


def shards(
    forward_rhs,
    adjoint_rhs,
    far_clusters,
    far_ranks,
    far_left,
    far_right,
    near_clusters,
    near_blocks,
    panel_params,
    panel_weights,
    panel_counts,
):
    groups = lax.axis_size("clus")
    members = lax.axis_size("sub")
    clusters = forward_rhs.shape[0]
    total_clusters = clusters * groups
    first_cluster = lax.axis_index("clus") * clusters
    whole_rhs, whole_adj = (
        lax.all_gather(forward_rhs, "sub", axis=1, tiled=True),
        lax.all_gather(adjoint_rhs, "sub", axis=1, tiled=True),
    )
    widened = extended(whole_rhs, (("clus", 0),), clusters)
    far_rows = far_clusters[0] - first_cluster
    far_cols = (far_clusters[1] - first_cluster + clusters) % total_clusters
    near_rows = near_clusters[0] - first_cluster
    near_cols = (near_clusters[1] - first_cluster + clusters) % total_clusters
    rank_keep = rank_columns(far_ranks, far_left.shape[2])
    adj_far = jnp.take(whole_adj, far_rows, axis=0)
    coeff_adj = (complex_mix(adj_far, far_left, "bkp,bjp->bkj") * rank_keep).astype(jnp.bfloat16)
    far_back = complex_mix(coeff_adj, far_right, "bkj,bjq->bkq")
    near_back = complex_mix(jnp.take(whole_adj, near_rows, axis=0), near_blocks, "bkp,bpq->bkq")
    wide_back = jax.ops.segment_sum(
        far_back, far_cols, num_segments=3 * clusters
    ) + jax.ops.segment_sum(near_back, near_cols, num_segments=3 * clusters)
    rhs_far = jnp.take(widened, far_cols, axis=0)
    coeff_fwd = (complex_mix(rhs_far, far_right, "bkq,bjq->bkj") * rank_keep).astype(jnp.bfloat16)
    far_out = complex_mix(coeff_fwd, far_left, "bkj,bjp->bkp")
    near_out = complex_mix(jnp.take(widened, near_cols, axis=0), near_blocks, "bkq,bpq->bkp")
    forward_part = jax.ops.segment_sum(
        far_out, far_rows, num_segments=clusters
    ) + jax.ops.segment_sum(near_out, near_rows, num_segments=clusters)
    forward_field = lax.psum_scatter(forward_part, "sub", scatter_dimension=1, tiled=True)
    reduced = lax.psum_scatter(wide_back, "sub", scatter_dimension=1, tiled=True)
    right_part = shifted(reduced[:clusters], "clus", -1)
    left_part = shifted(reduced[2 * clusters :], "clus", 1)
    adjoint_field = reduced[clusters : 2 * clusters] + right_part + left_part
    half_width = forward_field.shape[-1] // 2
    column_total = forward_rhs.shape[1] * members
    sensitivity = (
        jnp.sum(
            forward_field[..., :half_width] * adjoint_field[..., :half_width]
            - forward_field[..., half_width:] * adjoint_field[..., half_width:],
            axis=1,
        ).reshape(-1)
        / column_total
    )
    param_total = PAR_DEV * groups * members
    slot_ids = lax.broadcasted_iota(jnp.int32, panel_params.shape, 0)
    live_slots = slot_ids < panel_counts[None, :]
    weighted = jnp.where(
        live_slots,
        panel_weights * sensitivity[None, :],
        jnp.zeros(panel_weights.shape, jnp.float32),
    )
    param_gradient = lax.psum_scatter(
        jax.ops.segment_sum(
            weighted.reshape(-1), panel_params.reshape(-1), num_segments=param_total
        ),
        ("clus", "sub"),
        scatter_dimension=0,
        tiled=True,
    )
    return (forward_field, adjoint_field, param_gradient)


def solution(mesh):
    in_specs = (
        P("clus", "sub", None),
        P("clus", "sub", None),
        P(None, ("clus", "sub")),
        P(("clus", "sub")),
        P(("clus", "sub"), None, None, None),
        P(("clus", "sub"), None, None, None),
        P(None, ("clus", "sub")),
        P(("clus", "sub"), None, None, None),
        P(None, "clus"),
        P(None, "clus"),
        P("clus"),
    )
    out_specs = (P("clus", "sub", None), P("clus", "sub", None), P(("clus", "sub")))
    return jax.shard_map(shards, mesh=mesh, in_specs=in_specs, out_specs=out_specs, check_vma=False)
```

profile of v0, /device:TPU:0, one launch (start us, length us, event | category | flops | bytes accessed | tf_op | source)
XLA Modules:
  0.0 299.0 jit_solution(8539972881946359026)
XLA Ops:
  7.2 10.2 %all_gather.6 = bf16[32,32,256]{2,1,0:T(8,128)(2,1)} all-gather(bf16[32,8,256]{2,1,0:T(8,128)(2,1)} %param.11), channel_id=1, replica_groups=mesh['clus'=8,'sub'=4] {'sub'}, dimensions={1}, use_global_device_ids=true | all-gather | bytes 655360 | tf_op jit(solution)/shard_map/all_gather | solution.py:67
  17.4 1.5 collective-permute-start
  18.9 3.2 %collective-permute-start.1 = (bf16[32,32,256]{2,1,0:T(8,128)(2,1)}, bf16[32,32,256]{2,1,0:T(8,128)(2,1)}, u32[]{:S(2)}, u32[]{:S(2)}) collective-permute-start(bf16[32,32,256]{2,1,0:T(8,128)(2,1)} %all_gather.6), channel_id=1, source_target_pairs={{4,0},{8,4},{12,8},{16,12},{20,16},{24,20},{28,24},{0,28},{5,1},{9... | collective-permute-start | bytes 1572872 | tf_op jit(solution)/shard_map/ppermute | solution.py:17
  22.2 0.8 fusion.95
  22.9 0.8 compare_and_fusion.1
  23.7 0.8 fusion.96
  24.5 7.0 %all_gather.7 = bf16[32,32,256]{2,1,0:T(8,128)(2,1)S(1)} all-gather(bf16[32,8,256]{2,1,0:T(8,128)(2,1)} %param.12), channel_id=1, replica_groups=mesh['clus'=8,'sub'=4] {'sub'}, dimensions={1}, use_global_device_ids=true | all-gather | bytes 655360 | tf_op jit(solution)/shard_map/all_gather | solution.py:68
  31.5 0.7 gather_fusion.2
  32.5 1.3 copy-done.3
  33.8 2.0 fusion.21
  35.8 2.0 fusion.14
  37.8 0.6 gather_fusion.3
  38.5 0.9 copy-done
  40.2 0.8 copy-done.4
  41.0 3.9 %convolution_subtract_fusion.1 = f32[128,32,32]{2,1,0:T(8,128)} fusion(f32[128,32,32]{2,1,0:T(8,128)} %fusion.21, bf16[128,32,256]{2,1,0:T(8,128)(2,1)} %copy-done.8, bf16[128,2,32,128]{3,2,1,0:T(8,128)(2,1)S(1)} %copy-done.4), kind=kOutput, calls=%fused_computation.20 | convolution fusion | flops 33685504 | bytes 4718592 | tf_op jit(solution)/shard_map/bkp,bjp->bkj/dot_general | solution.py:35
  45.9 2.0 broadcast.357.clone.1
  47.9 5.0 %scatter_fusion.3 = f32[96,32,256]{2,1,0:T(8,128)} fusion(f32[96,32,256]{2,1,0:T(8,128)} %broadcast.357.clone.1, s32[32]{0:T(128)S(1)} %bitcast.107, f32[32,32,256]{2,1,0:T(8,128)S(1)} %pad_maximum_fusion.3), kind=kCustom, calls=%fused_computation.7 | custom fusion | flops 262144 | bytes 3145856 | tf_op jit(solution)/shard_map/scatter-add | solution.py:82
  53.0 3.9 %convolution_add_fusion.1 = f32[128,32,32]{2,1,0:T(8,128)} fusion(f32[128,32,32]{2,1,0:T(8,128)} %fusion.14, bf16[128,32,256]{2,1,0:T(8,128)(2,1)} %copy-done.8, bf16[128,2,32,128]{3,2,1,0:T(8,128)(2,1)S(1)} %copy-done.5), kind=kOutput, calls=%fused_computation.19 | convolution fusion | flops 33685504 | bytes 4718592 | tf_op jit(solution)/shard_map/bkp,bjp->bkj/dot_general | solution.py:38
  56.9 1.1 constant_dynamic-update-slice_fusion.2
  58.0 1.1 constant_dynamic-update-slice_fusion.1
  59.1 1.1 constant_dynamic-update-slice_fusion
  60.2 1.2 copy-done.11
  61.5 2.1 gather_fusion
  63.8 1.3 copy-done.2
  65.1 0.7 fusion.35
  65.8 0.7 fusion.30
  66.5 0.7 convolution_add_fusion.3
  67.2 0.7 convolution_subtract_fusion.3
  67.9 0.9 copy-done.9
  68.8 0.6 copy-done.10
  69.4 2.2 fusion.1
  71.5 0.4 fusion.33
  72.0 0.4 fusion.26
  72.4 0.5 convolution_subtract_fusion
  72.9 0.5 convolution_add_fusion
  73.5 2.4 pad_maximum_fusion.1
  76.3 13.5 %scatter_fusion.2 = f32[96,32,256]{2,1,0:T(8,128)S(1)} fusion(f32[96,32,256]{2,1,0:T(8,128)S(1)} %broadcast.357.clone, s32[128]{0:T(128)S(1)} %bitcast.106, f32[128,32,256]{2,1,0:T(8,128)} %pad_maximum_fusion.1), kind=kCustom, calls=%fused_computation.6 | custom fusion | flops 1048576 | bytes 12583424 | tf_op jit(solution)/shard_map/scatter-add | solution.py:80
  89.7 4.2 %add.257 = f32[96,32,256]{2,1,0:T(8,128)} add(f32[96,32,256]{2,1,0:T(8,128)S(1)} %scatter_fusion.2, f32[96,32,256]{2,1,0:T(8,128)} %scatter_fusion.3) | non-fusion elementwise | flops 786432 | bytes 9437184 | tf_op jit(solution)/shard_map/add | solution.py:80
  94.1 0.6 copy-done.16
  94.7 3.1 %gather_fusion.1 = bf16[32,32,256]{2,1,0:T(8,128)(2,1)} fusion(bf16[96,32,256]{2,1,0:T(8,128)(2,1)} %copy-done.11, s32[1024]{0:T(1024)S(1)} %get-tuple-element.19), kind=kCustom, calls=%fused_computation.1 | custom fusion | bytes 1048704 | tf_op jit(solution)/shard_map/jit(_take)/gather | solution.py:86
  97.7 0.4 fusion.24
  98.1 0.4 fusion.17
  98.6 0.5 convolution_subtract_fusion.2
  99.1 0.5 convolution_add_fusion.2
  99.6 2.5 pad_maximum_fusion
  102.3 13.8 %scatter_fusion = f32[32,32,256]{2,1,0:T(8,128)S(1)} fusion(f32[32,32,256]{2,1,0:T(8,128)S(1)} %broadcast.352.clone, s32[128]{0:T(128)S(1)} %fusion.99, f32[128,32,256]{2,1,0:T(8,128)} %pad_maximum_fusion), kind=kCustom, calls=%fused_computation.4 | custom fusion | flops 1048576 | bytes 12583424 | tf_op jit(solution)/shard_map/scatter-add | solution.py:87
  116.1 1.2 broadcast_select_fusion.3
  117.3 0.6 fusion.11
  117.9 0.7 fusion.6
  118.6 0.7 convolution_add_fusion.5
  119.3 0.7 convolution_subtract_fusion.5
  120.1 2.1 scatter_fusion.1
  122.3 1.1 add.245
  123.4 6.7 %reduce-scatter.5.cloned.1.call-done = f32[96,8,256]{2,1,0:T(8,128)} async-done(((f32[96,32,256]{2,1,0:T(8,128)}), f32[96,8,256]{2,1,0:T(8,128)}) %reduce-scatter.5.cloned.1.call-update) | async-done | bytes 786448 | tf_op jit(solution)/shard_map/reduce_scatter | solution.py:91
  130.1 1.1 fusion.101
  131.2 4.3 %collective-permute-start.2 = (f32[32,8,256]{2,1,0:T(8,128)S(1)}, f32[32,8,256]{2,1,0:T(8,128)S(1)}, u32[]{:S(2)}, u32[]{:S(2)}) collective-permute-start(f32[32,8,256]{2,1,0:T(8,128)S(1)} %get-tuple-element.7), channel_id=1, source_target_pairs={{0,28},{4,0},{8,4},{12,8},{16,12},{20,16},{24,20},{28,24},{1,29},{... | collective-permute-start | bytes 786440 | tf_op jit(solution)/shard_map/ppermute | solution.py:24
  135.5 5.5 %collective-permute-done.2 = f32[32,8,256]{2,1,0:T(8,128)S(1)} collective-permute-done((f32[32,8,256]{2,1,0:T(8,128)S(1)}, f32[32,8,256]{2,1,0:T(8,128)S(1)}, u32[]{:S(2)}, u32[]{:S(2)}) %collective-permute-start.2) | collective-permute-done | bytes 262176 | tf_op jit(solution)/shard_map/ppermute | solution.py:24
  141.0 4.9 %collective-permute-done.3 = f32[32,8,256]{2,1,0:T(8,128)S(1)} collective-permute-done((f32[32,8,256]{2,1,0:T(8,128)S(1)}, f32[32,8,256]{2,1,0:T(8,128)S(1)}, u32[]{:S(2)}, u32[]{:S(2)}) %collective-permute-start.3) | collective-permute-done | bytes 262176 | tf_op jit(solution)/shard_map/ppermute | solution.py:24
  145.9 1.0 fusion.78
  147.0 11.3 %reduce-scatter.3.cloned.1.call-done = f32[32,8,256]{2,1,0:T(8,128)} async-done(((f32[32,32,256]{2,1,0:T(8,128)}), f32[32,8,256]{2,1,0:T(8,128)}) %reduce-scatter.3.cloned.1.call-update) | async-done | bytes 262160 | tf_op jit(solution)/shard_map/reduce_scatter | solution.py:90
  158.3 1.0 fusion.88
  159.4 92.7 %scatter_custom_fusion.4 = f32[4096]{0:T(1024)S(1)} fusion(s32[16384]{0:T(1024)S(1)} %bitcast.104, f32[16384]{0:T(1024)S(1)} %bitcast.105, f32[]{:T(128)} %constant.86.clone.1), kind=kCustom, calls=%fused_computation.128 | custom fusion | flops 16384 | bytes 16388 | tf_op jit(solution)/shard_map/scatter-add | solution.py:114
  252.1 39.4 %all-reduce = f32[4096]{0:T(1024)S(1)} all-reduce(f32[4096]{0:T(1024)S(1)} %scatter_custom_fusion.4), channel_id=4, replica_groups=mesh['clus'=8,'sub'=4] {'clus','sub'}, use_global_device_ids=true, to_apply=%region_8.9.clone | all-reduce | flops 4096 | bytes 32768
  291.5 0.6 dynamic-slice
  (60 shorter events, 3.4 us)
Async XLA Ops:
  7.2 122.9 %reduce-scatter.5.cloned.1.call-start = ((), (), s32[]{:S(2)}) async-start(), calls=%async_computation.3 | async-start | bytes 3932160 | tf_op jit(solution)/shard_map/reduce_scatter | solution.py:91
  17.4 39.5 %collective-permute-start = (bf16[32,32,256]{2,1,0:T(8,128)(2,1)}, bf16[32,32,256]{2,1,0:T(8,128)(2,1)}, u32[]{:S(2)}, u32[]{:S(2)}) collective-permute-start(bf16[32,32,256]{2,1,0:T(8,128)(2,1)} %all_gather.6), channel_id=1, source_target_pairs={{0,4},{4,8},{8,12},{12,16},{16,20},{20,24},{24,28},{28,0},{1,5},{5... | collective-permute-start | bytes 1572872 | tf_op jit(solution)/shard_map/ppermute | solution.py:16
  18.9 40.2 %collective-permute-start.1 = (bf16[32,32,256]{2,1,0:T(8,128)(2,1)}, bf16[32,32,256]{2,1,0:T(8,128)(2,1)}, u32[]{:S(2)}, u32[]{:S(2)}) collective-permute-start(bf16[32,32,256]{2,1,0:T(8,128)(2,1)} %all_gather.6), channel_id=1, source_target_pairs={{4,0},{8,4},{12,8},{16,12},{20,16},{24,20},{28,24},{0,28},{5,1},{9... | collective-permute-start | bytes 1572872 | tf_op jit(solution)/shard_map/ppermute | solution.py:17
  32.2 1.6 copy-start.3
  33.8 4.0 %copy-start.8 = (bf16[128,32,256]{2,1,0:T(8,128)(2,1)}, bf16[128,32,256]{2,1,0:T(8,128)(2,1)S(1)}, u32[]{:S(2)}) copy-start(bf16[128,32,256]{2,1,0:T(8,128)(2,1)S(1)} %broadcast_select_fusion) | copy-start | bytes 6291460
  35.8 2.0 copy-start.17
  37.8 1.6 copy-start
  39.4 1.6 copy-start.4
  41.0 3.9 %copy-start.18 = (s32[128]{0:T(128)S(1)}, s32[128]{0:T(128)}, u32[]{:S(2)}) copy-start(s32[128]{0:T(128)} %param.14) | copy-start | bytes 1540
  47.9 5.1 %copy-start.5 = (bf16[128,2,32,128]{3,2,1,0:T(8,128)(2,1)S(1)}, bf16[128,2,32,128]{3,2,1,0:T(8,128)(2,1)}, u32[]{:S(2)}) copy-start(bf16[128,2,32,128]{3,2,1,0:T(8,128)(2,1)} %param.15) | copy-start | bytes 6291460
  60.2 1.2 copy-start.11
  63.5 1.6 copy-start.2
  67.2 1.6 copy-start.9
  67.2 2.2 copy-start.10
  94.0 0.7 copy-start.16
  94.0 3.7 %copy-start.6 = (bf16[128,2,32,128]{3,2,1,0:T(8,128)(2,1)S(1)}, bf16[128,2,32,128]{3,2,1,0:T(8,128)(2,1)}, u32[]{:S(2)}) copy-start(bf16[128,2,32,128]{3,2,1,0:T(8,128)(2,1)} %param.15) | copy-start | bytes 6291460
  94.0 3.7 %copy-start.7 = (bf16[128,32,64]{2,1,0:T(8,128)(2,1)S(1)}, bf16[128,32,64]{2,1,0:T(8,128)(2,1)}, u32[]{:S(2)}) copy-start(bf16[128,32,64]{2,1,0:T(8,128)(2,1)} %get-tuple-element.10) | copy-start | bytes 1572868
  94.0 64.3 %reduce-scatter.3.cloned.1.call-start = ((), (), s32[]{:S(2)}) async-start(), calls=%async_computation.2 | async-start | bytes 1310720 | tf_op jit(solution)/shard_map/reduce_scatter | solution.py:90
  102.2 15.0 %copy-start.1 = (bf16[32,2,128,128]{3,2,1,0:T(8,128)(2,1)S(1)}, bf16[32,2,128,128]{3,2,1,0:T(8,128)(2,1)}, u32[]{:S(2)}) copy-start(bf16[32,2,128,128]{3,2,1,0:T(8,128)(2,1)} %param.18) | copy-start | bytes 6291460
  122.3 13.2 %copy-start.13 = (s32[4,4096]{1,0:T(4,128)S(1)}, s32[4,4096]{1,0:T(4,128)}, u32[]{:S(2)}) copy-start(s32[4,4096]{1,0:T(4,128)} %param.19) | copy-start | bytes 196612
  123.4 35.9 %copy-start.14 = (f32[4,4096]{1,0:T(4,128)S(1)}, f32[4,4096]{1,0:T(4,128)}, u32[]{:S(2)}) copy-start(f32[4,4096]{1,0:T(4,128)} %param.20) | copy-start | bytes 196612
  123.4 36.0 %copy-start.15 = (s32[4096]{0:T(1024)S(1)}, s32[4096]{0:T(1024)}, u32[]{:S(2)}) copy-start(s32[4096]{0:T(1024)} %param.21) | copy-start | bytes 49156
  131.2 9.9 %collective-permute-start.2 = (f32[32,8,256]{2,1,0:T(8,128)S(1)}, f32[32,8,256]{2,1,0:T(8,128)S(1)}, u32[]{:S(2)}, u32[]{:S(2)}) collective-permute-start(f32[32,8,256]{2,1,0:T(8,128)S(1)} %get-tuple-element.7), channel_id=1, source_target_pairs={{0,28},{4,0},{8,4},{12,8},{16,12},{20,16},{24,20},{28,24},{1,29},{... | collective-permute-start | bytes 786440 | tf_op jit(solution)/shard_map/ppermute | solution.py:24
  135.5 10.5 %collective-permute-start.3 = (f32[32,8,256]{2,1,0:T(8,128)S(1)}, f32[32,8,256]{2,1,0:T(8,128)S(1)}, u32[]{:S(2)}, u32[]{:S(2)}) collective-permute-start(f32[32,8,256]{2,1,0:T(8,128)S(1)} %get-tuple-element.8), channel_id=1, source_target_pairs={{0,4},{4,8},{8,12},{12,16},{16,20},{20,24},{24,28},{28,0},{1,5},{5... | collective-permute-start | bytes 786440 | tf_op jit(solution)/shard_map/ppermute | solution.py:24
  146.9 145.2 %copy-start.12 = (f32[32,8,256]{2,1,0:T(8,128)}, f32[32,8,256]{2,1,0:T(8,128)S(1)}, u32[]{:S(2)}) copy-start(f32[32,8,256]{2,1,0:T(8,128)S(1)} %fusion.78) | copy-start | bytes 786436
Sparse Core Ops, SparseCore 0:
  94.1 35.9 reduce-scatter.4
  133.4 24.8 reduce-scatter.2
where the time goes:
time: 301 us; the launch traced here: 299 us
  other arithmetic  146 us (49%)
  blocking collectives  56.7 us (19%)
  waiting for transfers between devices  28.5 us (9%)
  matrix products  22.6 us (8%)
  local copies, waits for them, and re-layouts  21.6 us (7%)
  between operations  14.4 us (5%)
  starting transfers between devices  9.11 us (3%)
    scatter-add x1, other arithmetic, shards(): jax.ops.segment_sum(weighted.reshape(-1), panel_params.reshape(-1), num_s...  92.7 us
    unnamed x1, blocking collectives  39.4 us
    scatter-add x1, other arithmetic, shards(): jax.ops.segment_sum(far_out, far_rows, num_segments=clusters)  13.8 us
    scatter-add x1, other arithmetic, shards(): jax.ops.segment_sum(far_back, far_cols, num_segments=3 * clusters)  13.5 us
    reduce_scatter x1, waiting for transfers between devices, shards(): lax.psum_scatter(forward_part, 'sub', scatter_dimension=1, tiled=True)  11.3 us
    unnamed x43, local copies, waits for them, and re-layouts  10.5 us
    ppermute x2, waiting for transfers between devices, shifted(): lax.ppermute(x, axis, [(i, (i + by) % devices) for i in range(devices)])  10.4 us
    all_gather x1, blocking collectives, shards(): lax.all_gather(forward_rhs, 'sub', axis=1, tiled=True)  10.2 us
  transfers between devices with their start and end apart: 6, of which 4 were waited for; matrix products, arithmetic and copies ran while one was open for 19% of the time, Pallas kernels for 0%

commit v1 on v0

v1 whole, which is shorter than its diff:
```python
import functools

import jax
import jax.numpy as jnp
from jax import lax
from jax.experimental import pallas as pl
from jax.experimental.pallas import tpu as pltpu
from jax.sharding import PartitionSpec as P

PAR_DEV = 128
AXES = ("clus", "sub")
FAR_UNROLL = 16
NEAR_UNROLL = 4
VMEM_BYTES = 40 * 1024 * 1024


def moved(x, by, mask):
    groups, members = lax.axis_size("clus"), lax.axis_size("sub")
    pairs = [
        (g * members + s, ((g + by) % groups) * members + (s ^ mask))
        for g in range(groups)
        for s in range(members)
    ]
    return lax.ppermute(x, AXES, pairs)


def wide_place(cluster, row, clusters, total):
    first = row - lax.rem(row, clusters)
    place = lax.rem(cluster - first + total, total)
    return jnp.where(place >= 2 * clusters, place - (total - 3 * clusters), place)


def block_kernel(transposed, total, members, *refs):
    far_ids, ranks, near_ids = refs[:3]
    halves = 1 if transposed else 3
    pieces = refs[3 : 3 + halves * members]
    first, second, near = refs[3 + halves * members : 6 + halves * members]
    outs = refs[6 + halves * members : 6 + halves * members + members]
    lhs, coeffs = refs[6 + halves * members + members :]
    clusters, height, _ = pieces[0].shape
    far, _, rank, width = first.shape
    near_total = near.shape[0]
    rows = lhs.shape[1]
    part = 2 * height
    for out in outs:
        out[...] = jnp.zeros_like(out)
    for g in range(halves):

        @pl.loop(0, clusters, unroll=2)
        def _(c):
            left, right = [], []
            for piece in pieces[g * members : (g + 1) * members]:
                x = piece[c].astype(jnp.float32)
                re, im = x[:, :width], x[:, width:]
                left += [re, im]
                right += [-im, re]
            both = [jnp.concatenate(left, axis=0), jnp.concatenate(right, axis=0)]
            lhs[g * clusters + c] = jnp.concatenate(both, axis=1).astype(jnp.bfloat16)

    def add(place, value):
        for i, out in enumerate(outs):
            out[place] += value[i * part : (i + 1) * part]

    def places(ids, b):
        row = ids[0, b]
        column = wide_place(ids[1, b], row, clusters, total)
        row = lax.rem(row, clusters)
        return (row, column) if transposed else (column, row)

    rank_ids = lax.broadcasted_iota(jnp.int32, (rows, 2 * rank), 1)
    rank_ids = jnp.where(rank_ids >= rank, rank_ids - rank, rank_ids)

    far_unroll = min(FAR_UNROLL, far)
    near_unroll = min(NEAR_UNROLL, near_total)

    @pl.loop(0, far // far_unroll)
    def _(t):
        for i in range(far_unroll):
            b = t * far_unroll + i
            re, im = first[b, 0], first[b, 1]
            factor = jnp.concatenate(
                [jnp.concatenate([re, im], axis=1), jnp.concatenate([-im, re], axis=1)], axis=0
            )
            coeff = lax.dot_general(
                lhs[places(far_ids, b)[0]],
                factor,
                (((1,), (1,)), ((), ())),
                preferred_element_type=jnp.float32,
            )
            coeffs[i] = jnp.where(rank_ids < ranks[b], coeff, 0.0).astype(jnp.bfloat16)
        for i in range(far_unroll):
            b = t * far_unroll + i
            value = jnp.dot(
                coeffs[i], second[b].reshape(2 * rank, width), preferred_element_type=jnp.float32
            )
            add(places(far_ids, b)[1], value)

    @pl.loop(0, near_total // near_unroll)
    def _(t):
        for i in range(near_unroll):
            b = t * near_unroll + i
            source, place = places(near_ids, b)
            if transposed:
                value = jnp.dot(
                    lhs[source],
                    near[b].reshape(2 * width, width),
                    preferred_element_type=jnp.float32,
                )
            else:
                value = lax.dot_general(
                    lhs[source],
                    jnp.concatenate([near[b, 0], near[b, 1]], axis=1),
                    (((1,), (1,)), ((), ())),
                    preferred_element_type=jnp.float32,
                )
            add(place, value)


def apply_blocks(transposed, total, members, far_ids, ranks, near_ids, pieces, first, second, near):
    clusters, height, double = pieces[0].shape
    halves = len(pieces) // members
    out_clusters = 3 * clusters if transposed else clusters
    rows = members * 2 * height
    rank, width = first.shape[2:]
    smem = pl.BlockSpec(memory_space=pltpu.SMEM)
    vmem = pl.BlockSpec(memory_space=pltpu.VMEM)
    flops = 2 * rows * (first.shape[0] * 2 * 2 * rank * 2 * width + near.shape[0] * 2 * width * width)
    return pl.pallas_call(
        functools.partial(block_kernel, transposed, total, members),
        in_specs=[smem] * 3 + [vmem] * (len(pieces) + 3),
        out_specs=[vmem] * members,
        out_shape=[
            jax.ShapeDtypeStruct((out_clusters, 2 * height, width), jnp.float32)
        ] * members,
        scratch_shapes=[
            pltpu.VMEM((halves * clusters, rows, double), jnp.bfloat16),
            pltpu.VMEM((min(FAR_UNROLL, first.shape[0]), rows, 2 * rank), jnp.bfloat16),
        ],
        compiler_params=pltpu.CompilerParams(vmem_limit_bytes=VMEM_BYTES),
        cost_estimate=pl.CostEstimate(flops=flops, bytes_accessed=20_000_000, transcendentals=0),
    )(far_ids, ranks, near_ids, *pieces, first, second, near)


def final_kernel(column_total, n_fwd, n_adj, *refs):
    fwd_terms = refs[:n_fwd]
    adj_terms = refs[n_fwd : n_fwd + n_adj]
    params, weights, counts = refs[n_fwd + n_adj : n_fwd + n_adj + 3]
    fwd_out, adj_out, grad = refs[n_fwd + n_adj + 3 :]
    clusters, height, _ = fwd_out.shape
    slots = params.shape[0]
    high, width = grad.shape
    high_ids = lax.broadcasted_iota(jnp.int32, (high, width), 0)
    low_ids = lax.broadcasted_iota(jnp.int32, (width, width), 0)
    shift = width.bit_length() - 1
    grad[...] = jnp.zeros_like(grad)

    def panels(c):
        fwd = sum(t[c].astype(jnp.float32) for t in fwd_terms)
        adj = sum(t[c].astype(jnp.float32) for t in adj_terms)
        for out, value in ((fwd_out, fwd), (adj_out, adj)):
            out[c, :, :width] = value[:height]
            out[c, :, width:] = value[height:]
        product = fwd * adj
        sens = jnp.sum(product[:height] - product[height:], axis=0, keepdims=True) / column_total
        at = pl.ds(pl.multiple_of(c * width, width), width)
        slot_ids = lax.broadcasted_iota(jnp.int32, (slots, width), 0)
        value = jnp.where(slot_ids < counts[:, at], weights[:, at] * sens, 0.0)
        ids = params[:, at]
        high_of, low_of = ids >> shift, ids & (width - 1)
        top = value.astype(jnp.bfloat16).astype(jnp.float32)
        rest = value - top
        middle = rest.astype(jnp.bfloat16).astype(jnp.float32)
        terms = (top, middle, rest - middle)
        spread, places = [], []
        for m in range(slots):
            row = slice(m, m + 1)
            hit = high_ids == high_of[row]
            spread.append(
                jnp.concatenate([jnp.where(hit, t[row], 0.0) for t in terms], axis=0).astype(jnp.bfloat16)
            )
            places.append(jnp.where(low_ids == low_of[row], 1.0, 0.0).astype(jnp.bfloat16))
        got = lax.dot_general(
            jnp.concatenate(spread, axis=1),
            jnp.concatenate(places, axis=1),
            (((1,), (1,)), ((), ())),
            preferred_element_type=jnp.float32,
        )
        grad[...] += sum(got[k * high : (k + 1) * high] for k in range(len(terms)))

    @pl.loop(0, clusters, unroll=4)
    def _(c):
        panels(c)


def finish(column_total, fwd_terms, adj_terms, params, weights, counts, high):
    clusters, part, width = fwd_terms[0].shape
    vmem = pl.BlockSpec(memory_space=pltpu.VMEM)
    first_clusters = pl.BlockSpec((clusters, part, width), lambda i: (0, 0, 0))
    field = jax.ShapeDtypeStruct((clusters, part // 2, 2 * width), jnp.float32)
    whole = lambda shape: pl.BlockSpec(shape, lambda i: (0,) * len(shape))
    terms = [*fwd_terms, *adj_terms]
    return pl.pallas_call(
        functools.partial(final_kernel, column_total, len(fwd_terms), len(adj_terms)),
        grid=(1,),
        in_specs=[first_clusters] * len(terms)
        + [whole(params.shape), whole(weights.shape), whole(counts.shape)],
        out_specs=[whole(field.shape), whole(field.shape), whole((high, width))],
        out_shape=[field, field, jax.ShapeDtypeStruct((high, width), jnp.float32)],
        compiler_params=pltpu.CompilerParams(vmem_limit_bytes=VMEM_BYTES),
        cost_estimate=pl.CostEstimate(flops=200_000_000, bytes_accessed=3_000_000, transcendentals=0),
    )(*terms, params, weights, counts)


def shards(
    forward_rhs,
    adjoint_rhs,
    far_clusters,
    far_ranks,
    far_left,
    far_right,
    near_clusters,
    near_blocks,
    panel_params,
    panel_weights,
    panel_counts,
):
    groups = lax.axis_size("clus")
    members = lax.axis_size("sub")
    clusters = forward_rhs.shape[0]
    total = clusters * groups
    column_total = forward_rhs.shape[1] * members
    evens = range(0, members, 2)

    def all_columns(mine):
        pieces = []
        for x in mine:
            pieces += [x, moved(x, 0, 1)]
        return pieces

    w_mine = [adjoint_rhs if m == 0 else moved(adjoint_rhs, 0, m) for m in evens]
    w_pieces = all_columns(w_mine)
    x_next, x_prev = moved(forward_rhs, -1, 0), moved(forward_rhs, 1, 0)
    x_pieces = []
    for x in (forward_rhs, x_next, x_prev):
        x_pieces += all_columns([x if m == 0 else moved(x, 0, m) for m in evens])

    apply = functools.partial(apply_blocks, total=total, members=members)
    adj_parts = apply(
        True, far_ids=far_clusters, ranks=far_ranks, near_ids=near_clusters,
        pieces=w_pieces, first=far_left, second=far_right, near=near_blocks,
    )
    adj_core = [moved(adj_parts[m + 1], 0, 1) for m in evens]
    fwd_parts = apply(
        False, far_ids=far_clusters, ranks=far_ranks, near_ids=near_clusters,
        pieces=x_pieces, first=far_right, second=far_left, near=near_blocks,
    )
    fwd_core = [moved(fwd_parts[m + 1], 0, 1) for m in evens]

    sides, own = [], []
    for k, m in enumerate(evens):
        if m:
            both = adj_parts[m] + adj_core[k]
            sides.append(moved(both[clusters:].astype(jnp.bfloat16), 0, m))
            own.append(moved(both[:clusters].astype(jnp.bfloat16), 0, m))
    side = adj_parts[0][clusters:] + adj_core[0][clusters:]
    for s in sides:
        side = side + s.astype(jnp.float32)
    side = side.astype(jnp.bfloat16)
    ring = [moved(side[:clusters], 1, 0), moved(side[clusters:], -1, 0)]
    adj_terms = [adj_parts[0], adj_core[0], *own, *ring]

    fwd_terms = [fwd_parts[0], fwd_core[0]]
    for k, m in enumerate(evens):
        if m:
            fwd_terms.append(moved((fwd_parts[m] + fwd_core[k]).astype(jnp.bfloat16), 0, m))

    devices = groups * members
    forward_field, adjoint_field, spread = finish(
        column_total, fwd_terms, adj_terms, panel_params, panel_weights, panel_counts[None, :],
        PAR_DEV * devices // near_blocks.shape[-1],
    )
    pieces = lax.all_to_all(spread.reshape(devices, PAR_DEV), AXES, 0, 0, tiled=True)
    return forward_field, adjoint_field, jnp.sum(pieces, axis=0)


def solution(mesh):
    in_specs = (
        P("clus", "sub", None),
        P("clus", "sub", None),
        P(None, ("clus", "sub")),
        P(("clus", "sub")),
        P(("clus", "sub"), None, None, None),
        P(("clus", "sub"), None, None, None),
        P(None, ("clus", "sub")),
        P(("clus", "sub"), None, None, None),
        P(None, "clus"),
        P(None, "clus"),
        P("clus"),
    )
    out_specs = (P("clus", "sub", None), P("clus", "sub", None), P(("clus", "sub")))
    return jax.shard_map(shards, mesh=mesh, in_specs=in_specs, out_specs=out_specs, check_vma=False)
```

time: 301 us -> 82.1 us (0.27)
  other arithmetic: 146 us -> 0.8 us
  blocking collectives: 56.7 us -> 8.83 us
  matrix products: 22.6 us -> 0 us
  Pallas kernels: 0 us -> 15.8 us
  local copies, waits for them, and re-layouts: 21.6 us -> 7.76 us
  between operations: 14.4 us -> 0.75 us
  starting transfers between devices: 9.11 us -> 17.8 us
    scatter-add x5 -> x0, other arithmetic: 127 us -> none  [the longest x1 92.7 us: shards(): jax.ops.segment_sum(weighted.reshape(-1), panel_params.reshape(-1), num_s...]
    unnamed x1 -> x0, blocking collectives: 39.4 us -> none
    dot_general x24 -> x0, matrix products: 22.6 us -> none  [the longest x6 6.73 us: complex_mix(): jnp.einsum(einsum_form, imag_lhs, imag_rhs, preferred_element_type=jnp.fl...]
    ppermute x4 -> x23, waiting for transfers between devices: 10.4 us -> 30 us  [moved(): return lax.ppermute(x, AXES, pairs)]
    reduce_scatter x2 -> x0, waiting for transfers between devices: 18 us -> none  [the longest x1 11.3 us: shards(): lax.psum_scatter(forward_part, 'sub', scatter_dimension=1, tiled=True)]
    all_gather x2 -> x0, blocking collectives: 17.3 us -> none  [the longest x1 10.2 us: shards(): lax.all_gather(forward_rhs, 'sub', axis=1, tiled=True)]
    pallas_call x0 -> x3, Pallas kernels: none -> 15.8 us  [the longest x2 12.8 us: apply_blocks(): pl.pallas_call(functools.partial(block_kernel, transposed, total, members...]
    all_to_all x0 -> x1, blocking collectives: none -> 8.83 us  [shards(): lax.all_to_all(spread.reshape(devices, PAR_DEV), AXES, 0, 0, tiled=True)]
  transfers between devices with their start and end apart: 6 -> 23, of which waited for: 4 -> 13; matrix products, arithmetic and copies ran while one was open for 19% -> 0% of each run, Pallas kernels for 0% -> 8%
where the time goes in v1:
time: 82.1 us; the launch traced here: 81.8 us
  waiting for transfers between devices  30 us (37%)
  starting transfers between devices  17.8 us (22%)
  Pallas kernels  15.8 us (19%)
  blocking collectives  8.83 us (11%)
  local copies, waits for them, and re-layouts  7.76 us (9%)
    ppermute x23, waiting for transfers between devices, moved(): return lax.ppermute(x, AXES, pairs)  30 us
    ppermute x23, starting transfers between devices, moved(): return lax.ppermute(x, AXES, pairs)  17.8 us
    pallas_call x2, Pallas kernels, apply_blocks(): pl.pallas_call(functools.partial(block_kernel, transposed, total, members...  12.8 us
    all_to_all x1, blocking collectives, shards(): lax.all_to_all(spread.reshape(devices, PAR_DEV), AXES, 0, 0, tiled=True)  8.83 us
    unnamed x24, local copies, waits for them, and re-layouts  7.71 us
    pallas_call x1, Pallas kernels, finish(): pl.pallas_call(functools.partial(final_kernel, column_total, len(fwd_term...  3.1 us
  transfers between devices with their start and end apart: 23, of which 13 were waited for; matrix products, arithmetic and copies ran while one was open for 0% of the time, Pallas kernels for 8%

profile of v1, /device:TPU:0, one launch (start us, length us, event | category | flops | bytes accessed | tf_op | source)
XLA Modules:
  0.0 81.8 jit_solution(9465930615340336308)
XLA Ops:
  0.6 3.0 %collective-permute-start.15 = (bf16[32,8,256]{2,1,0:T(8,128)(2,1)}, bf16[32,8,256]{2,1,0:T(8,128)(2,1)S(1)}, u32[]{:S(2)}, u32[]{:S(2)}) collective-permute-start(bf16[32,8,256]{2,1,0:T(8,128)(2,1)} %refs_3_.3), channel_id=1, source_target_pairs={{0,2},{1,3},{2,0},{3,1},{4,6},{5,7},{6,4},{7,5},{8,10},{9,11},{10,... | collective-permute-start | bytes 393224 | tf_op jit(solution)/shard_map/ppermute | solution.py:24
  3.7 0.0 collective-permute-start.14
  3.7 3.7 %collective-permute-done.15.refs_5_ = bf16[32,8,256]{2,1,0:T(8,128)(2,1)S(1)} collective-permute-done((bf16[32,8,256]{2,1,0:T(8,128)(2,1)}, bf16[32,8,256]{2,1,0:T(8,128)(2,1)S(1)}, u32[]{:S(2)}, u32[]{:S(2)}) %collective-permute-start.15) | collective-permute-done | bytes 131104 | tf_op jit(solution)/shard_map/ppermute | solution.py:24
  7.4 0.0 collective-permute-start.16
  7.4 0.0 collective-permute-done.14.refs_4_
  7.4 1.3 %collective-permute-done.16.refs_6_ = bf16[32,8,256]{2,1,0:T(8,128)(2,1)S(1)} collective-permute-done((bf16[32,8,256]{2,1,0:T(8,128)(2,1)S(1)}, bf16[32,8,256]{2,1,0:T(8,128)(2,1)S(1)}, u32[]{:S(2)}, u32[]{:S(2)}) %collective-permute-start.16) | collective-permute-done | bytes 131104 | tf_op jit(solution)/shard_map/ppermute | solution.py:24
  8.7 1.6 %copy-done = bf16[128,2,32,128]{3,2,1,0:T(8,128)(2,1)S(1)} copy-done((bf16[128,2,32,128]{3,2,1,0:T(8,128)(2,1)S(1)}, bf16[128,2,32,128]{3,2,1,0:T(8,128)(2,1)}, u32[]{:S(2)}) %copy-start) | copy-done | bytes 2097176
  10.3 1.6 %copy-done.2 = bf16[128,2,32,128]{3,2,1,0:T(8,128)(2,1)S(1)} copy-done((bf16[128,2,32,128]{3,2,1,0:T(8,128)(2,1)S(1)}, bf16[128,2,32,128]{3,2,1,0:T(8,128)(2,1)}, u32[]{:S(2)}) %copy-start.2) | copy-done | bytes 2097176
  11.9 1.6 %copy-done.3 = bf16[32,2,128,128]{3,2,1,0:T(8,128)(2,1)S(1)} copy-done((bf16[32,2,128,128]{3,2,1,0:T(8,128)(2,1)S(1)}, bf16[32,2,128,128]{3,2,1,0:T(8,128)(2,1)}, u32[]{:S(2)}) %copy-start.3) | copy-done | bytes 2097176
  13.5 0.9 %copy-done.5 = bf16[32,8,256]{2,1,0:T(8,128)(2,1)S(1)} copy-done((bf16[32,8,256]{2,1,0:T(8,128)(2,1)S(1)}, bf16[32,8,256]{2,1,0:T(8,128)(2,1)}, u32[]{:S(2)}) %copy-start.5) | copy-done | bytes 131096
  14.4 0.7 copy-done.9
  15.1 0.7 copy-done.10
  15.8 0.7 copy-done.11
  16.4 6.1 %shard_map.131 = (f32[96,16,128]{2,1,0:T(8,128)S(1)}, f32[96,16,128]{2,1,0:T(8,128)S(1)}, f32[96,16,128]{2,1,0:T(8,128)S(1)}, f32[96,16,128]{2,1,0:T(8,128)S(1)}) custom-call(s32[2,128]{1,0:T(2,128)S(1)} %copy-done.9, s32[128]{0:T(128)S(1)} %copy-done.11, s32[2,32]{1,0:T(2,128)S(1)} %copy-done.10, bf16[32,8,256]{2,1,0:T(8,128)(2,1)S(1)} %copy-done.5, ...), custom_call_target="tpu_custom_call" | custom-call | flops 671088640 | bytes 20000000 | tf_op jit(solution)/shard_map/pallas_call | solution.py:128
  22.5 0.2 collective-permute-start.18
  22.7 4.8 %collective-permute-start.3 = (bf16[32,8,256]{2,1,0:T(8,128)(2,1)S(1)}, bf16[32,8,256]{2,1,0:T(8,128)(2,1)S(1)}, u32[]{:S(2)}, u32[]{:S(2)}) collective-permute-start(bf16[32,8,256]{2,1,0:T(8,128)(2,1)S(1)} %copy-done.4), channel_id=1, source_target_pairs={{0,28},{1,29},{2,30},{3,31},{4,0},{5,1},{6,2},{7,3},{8,4},{9,5},{1... | collective-permute-start | bytes 393224 | tf_op jit(solution)/shard_map/ppermute | solution.py:24
  27.5 1.5 %collective-permute-start.1 = (bf16[32,8,256]{2,1,0:T(8,128)(2,1)S(1)}, bf16[32,8,256]{2,1,0:T(8,128)(2,1)S(1)}, u32[]{:S(2)}, u32[]{:S(2)}) collective-permute-start(bf16[32,8,256]{2,1,0:T(8,128)(2,1)S(1)} %copy-done.4), channel_id=1, source_target_pairs={{0,2},{1,3},{2,0},{3,1},{4,6},{5,7},{6,4},{7,5},{8,10},{9,11},{10,... | collective-permute-start | bytes 393224 | tf_op jit(solution)/shard_map/ppermute | solution.py:24
  29.0 0.0 collective-permute-start
  29.0 0.0 collective-permute-start.7
  29.0 1.7 %collective-permute-done.3.refs_7_ = bf16[32,8,256]{2,1,0:T(8,128)(2,1)S(1)} collective-permute-done((bf16[32,8,256]{2,1,0:T(8,128)(2,1)S(1)}, bf16[32,8,256]{2,1,0:T(8,128)(2,1)S(1)}, u32[]{:S(2)}, u32[]{:S(2)}) %collective-permute-start.3) | collective-permute-done | bytes 131104 | tf_op jit(solution)/shard_map/ppermute | solution.py:24
  30.7 1.5 %collective-permute-start.5 = (bf16[32,8,256]{2,1,0:T(8,128)(2,1)S(1)}, bf16[32,8,256]{2,1,0:T(8,128)(2,1)S(1)}, u32[]{:S(2)}, u32[]{:S(2)}) collective-permute-start(bf16[32,8,256]{2,1,0:T(8,128)(2,1)S(1)} %collective-permute-done.3.refs_7_), channel_id=1, source_target_pairs={{0,2},{1,3},{2,0},{3,1},{4,6},{5,7},{6,4},{7,5},{8,10},{9,11},{10,... | collective-permute-start | bytes 393224 | tf_op jit(solution)/shard_map/ppermute | solution.py:24
  32.3 0.7 collective-permute-done.1.refs_5_
  33.0 0.0 collective-permute-start.4
  33.0 0.0 collective-permute-done.refs_4_
  33.0 0.5 collective-permute-start.2
  33.5 4.1 %collective-permute-done.7.refs_11_ = bf16[32,8,256]{2,1,0:T(8,128)(2,1)S(1)} collective-permute-done((bf16[32,8,256]{2,1,0:T(8,128)(2,1)S(1)}, bf16[32,8,256]{2,1,0:T(8,128)(2,1)S(1)}, u32[]{:S(2)}, u32[]{:S(2)}) %collective-permute-start.7) | collective-permute-done | bytes 131104 | tf_op jit(solution)/shard_map/ppermute | solution.py:24
  37.6 0.5 collective-permute-start.9
  38.1 0.0 collective-permute-done.5.refs_9_
  38.1 0.0 collective-permute-start.17
  38.1 0.0 collective-permute-done.4.refs_8_
  38.1 0.5 collective-permute-start.8
  38.6 0.0 collective-permute-done.2.refs_6_
  38.6 0.1 collective-permute-start.6
  38.7 4.0 %collective-permute-done.9.refs_13_ = bf16[32,8,256]{2,1,0:T(8,128)(2,1)S(1)} collective-permute-done((bf16[32,8,256]{2,1,0:T(8,128)(2,1)S(1)}, bf16[32,8,256]{2,1,0:T(8,128)(2,1)S(1)}, u32[]{:S(2)}, u32[]{:S(2)}) %collective-permute-start.9) | collective-permute-done | bytes 131104 | tf_op jit(solution)/shard_map/ppermute | solution.py:24
  42.7 0.0 collective-permute-start.10
  42.7 0.0 collective-permute-done.8.refs_12_
  42.7 0.0 collective-permute-done.6.refs_10_
  42.8 1.3 %collective-permute-done.10.refs_14_ = bf16[32,8,256]{2,1,0:T(8,128)(2,1)S(1)} collective-permute-done((bf16[32,8,256]{2,1,0:T(8,128)(2,1)S(1)}, bf16[32,8,256]{2,1,0:T(8,128)(2,1)S(1)}, u32[]{:S(2)}, u32[]{:S(2)}) %collective-permute-start.10) | collective-permute-done | bytes 131104 | tf_op jit(solution)/shard_map/ppermute | solution.py:24
  44.1 0.0 copy-done.1
  44.1 6.7 %shard_map.130 = (f32[32,16,128]{2,1,0:T(8,128)S(1)}, f32[32,16,128]{2,1,0:T(8,128)S(1)}, f32[32,16,128]{2,1,0:T(8,128)S(1)}, f32[32,16,128]{2,1,0:T(8,128)S(1)}) custom-call(s32[2,128]{1,0:T(2,128)S(1)} %copy-done.9, s32[128]{0:T(128)S(1)} %copy-done.11, s32[2,32]{1,0:T(2,128)S(1)} %copy-done.10, bf16[32,8,256]{2,1,0:T(8,128)(2,1)S(1)} %copy-done.4, ...), custom_call_target="tpu_custom_call" | custom-call | flops 671088640 | bytes 20000000 | tf_op jit(solution)/shard_map/pallas_call | solution.py:128
  50.8 0.2 collective-permute-start.12
  51.0 0.0 collective-permute-done.18
  51.0 0.1 add_convert_fusion
  51.1 0.0 copy-start.6
  51.1 0.0 copy-start.7
  51.1 0.0 copy-start.8
  51.2 0.6 collective-permute-start.20
  51.7 0.1 collective-permute-start.11
  51.8 0.6 collective-permute-done.12
  52.4 1.0 %collective-permute-start.13 = (bf16[32,16,128]{2,1,0:T(8,128)(2,1)S(1)}, bf16[32,16,128]{2,1,0:T(8,128)(2,1)S(1)}, u32[]{:S(2)}, u32[]{:S(2)}) collective-permute-start(bf16[32,16,128]{2,1,0:T(8,128)(2,1)S(1)} %add_convert_fusion.1), channel_id=1, source_target_pairs={{0,2},{1,3},{2,0},{3,1},{4,6},{5,7},{6,4},{7,5},{8,10},{9,11},{10,... | collective-permute-start | bytes 393224 | tf_op jit(solution)/shard_map/ppermute | solution.py:24
  53.5 1.1 %collective-permute-start.19 = (bf16[32,16,128]{2,1,0:T(8,128)(2,1)S(1)}, bf16[32,16,128]{2,1,0:T(8,128)(2,1)S(1)}, u32[]{:S(2)}, u32[]{:S(2)}) collective-permute-start(bf16[32,16,128]{2,1,0:T(8,128)(2,1)S(1)} %slice.26), channel_id=1, source_target_pairs={{0,2},{1,3},{2,0},{3,1},{4,6},{5,7},{6,4},{7,5},{8,10},{9,11},{10,... | collective-permute-start | bytes 393224 | tf_op jit(solution)/shard_map/ppermute | solution.py:24
  54.6 0.0 collective-permute-done.17.refs_4_
  54.6 5.8 %collective-permute-done.20 = bf16[64,16,128]{2,1,0:T(8,128)(2,1)S(1)} collective-permute-done((bf16[64,16,128]{2,1,0:T(8,128)(2,1)S(1)}, bf16[64,16,128]{2,1,0:T(8,128)(2,1)S(1)}, u32[]{:S(2)}, u32[]{:S(2)}) %collective-permute-start.20) | collective-permute-done | bytes 262176 | tf_op jit(solution)/shard_map/ppermute | solution.py:24
  60.4 0.1 fusion.1
  60.5 1.1 %collective-permute-start.22 = (bf16[32,16,128]{2,1,0:T(8,128)(2,1)S(1)}, bf16[32,16,128]{2,1,0:T(8,128)(2,1)S(1)}, u32[]{:S(2)}, u32[]{:S(2)}) collective-permute-start(bf16[32,16,128]{2,1,0:T(8,128)(2,1)S(1)} %get-tuple-element.25), channel_id=1, source_target_pairs={{0,28},{1,29},{2,30},{3,31},{4,0},{5,1},{6,2},{7,3},{8,4},{9,5},{1... | collective-permute-start | bytes 393224 | tf_op jit(solution)/shard_map/ppermute | solution.py:24
  61.6 0.9 %collective-permute-start.21 = (bf16[32,16,128]{2,1,0:T(8,128)(2,1)S(1)}, bf16[32,16,128]{2,1,0:T(8,128)(2,1)S(1)}, u32[]{:S(2)}, u32[]{:S(2)}) collective-permute-start(bf16[32,16,128]{2,1,0:T(8,128)(2,1)S(1)} %get-tuple-element.26), channel_id=1, source_target_pairs={{0,4},{1,5},{2,6},{3,7},{4,8},{5,9},{6,10},{7,11},{8,12},{9,13},{1... | collective-permute-start | bytes 393224 | tf_op jit(solution)/shard_map/ppermute | solution.py:24
  62.6 0.0 collective-permute-done.11.refs_1_
  62.6 0.6 collective-permute-done.13.refs_2_
  63.2 2.2 %collective-permute-done.19.refs_5_ = bf16[32,16,128]{2,1,0:T(8,128)(2,1)S(1)} collective-permute-done((bf16[32,16,128]{2,1,0:T(8,128)(2,1)S(1)}, bf16[32,16,128]{2,1,0:T(8,128)(2,1)S(1)}, u32[]{:S(2)}, u32[]{:S(2)}) %collective-permute-start.19) | collective-permute-done | bytes 131104 | tf_op jit(solution)/shard_map/ppermute | solution.py:24
  65.4 0.1 collective-permute-done.22.refs_7_
  65.5 3.8 %collective-permute-done.21.refs_6_ = bf16[32,16,128]{2,1,0:T(8,128)(2,1)S(1)} collective-permute-done((bf16[32,16,128]{2,1,0:T(8,128)(2,1)S(1)}, bf16[32,16,128]{2,1,0:T(8,128)(2,1)S(1)}, u32[]{:S(2)}, u32[]{:S(2)}) %collective-permute-start.21) | collective-permute-done | bytes 131104 | tf_op jit(solution)/shard_map/ppermute | solution.py:24
  69.3 3.1 %shard_map.132 = (f32[32,8,256]{2,1,0:T(8,128)}, f32[32,8,256]{2,1,0:T(8,128)}, f32[32,128]{1,0:T(8,128)S(1)}) custom-call(f32[32,16,128]{2,1,0:T(8,128)S(1)} %get-tuple-element.14.refs_0_, f32[32,16,128]{2,1,0:T(8,128)S(1)} %collective-permute-done.11.refs_1_, bf16[32,16,128]{2,1,0:T(8,128)(2,1)S(1)} %collective-permute-done.13.refs_2_, ...), custom_call_target="tpu_custom_call" | custom-call | flops 200000000 | bytes 3000000 | tf_op jit(solution)/shard_map/pallas_call | solution.py:202
  72.4 8.8 %all_to_all.9 = f32[32,1,128]{2,1,0:T(1,128)S(1)} all-to-all(f32[32,1,128]{2,1,0:T(1,128)S(1)} %bitcast.5), channel_id=1, replica_groups=mesh['clus'=8,'sub'=4] {'clus','sub'}, dimensions={0} | all-to-all | bytes 32768 | tf_op jit(solution)/shard_map/all_to_all | solution.py:282
  81.2 0.6 reduce_sum.9
  (17 shorter events, 0.1 us)
Async XLA Ops:
  0.6 6.7 %collective-permute-start.15 = (bf16[32,8,256]{2,1,0:T(8,128)(2,1)}, bf16[32,8,256]{2,1,0:T(8,128)(2,1)S(1)}, u32[]{:S(2)}, u32[]{:S(2)}) collective-permute-start(bf16[32,8,256]{2,1,0:T(8,128)(2,1)} %refs_3_.3), channel_id=1, source_target_pairs={{0,2},{1,3},{2,0},{3,1},{4,6},{5,7},{6,4},{7,5},{8,10},{9,11},{10,... | collective-permute-start | bytes 393224 | tf_op jit(solution)/shard_map/ppermute | solution.py:24
  3.7 3.7 %collective-permute-start.14 = (bf16[32,8,256]{2,1,0:T(8,128)(2,1)}, bf16[32,8,256]{2,1,0:T(8,128)(2,1)S(1)}, u32[]{:S(2)}, u32[]{:S(2)}) collective-permute-start(bf16[32,8,256]{2,1,0:T(8,128)(2,1)} %refs_3_.3), channel_id=1, source_target_pairs={{0,1},{1,0},{2,3},{3,2},{4,5},{5,4},{6,7},{7,6},{8,9},{9,8},{10,11... | collective-permute-start | bytes 393224 | tf_op jit(solution)/shard_map/ppermute | solution.py:24
  7.4 1.3 %collective-permute-start.16 = (bf16[32,8,256]{2,1,0:T(8,128)(2,1)S(1)}, bf16[32,8,256]{2,1,0:T(8,128)(2,1)S(1)}, u32[]{:S(2)}, u32[]{:S(2)}) collective-permute-start(bf16[32,8,256]{2,1,0:T(8,128)(2,1)S(1)} %collective-permute-done.15.refs_5_), channel_id=1, source_target_pairs={{0,1},{1,0},{2,3},{3,2},{4,5},{5,4},{6,7},{7,6},{8,9},{9,8},{10,11... | collective-permute-start | bytes 393224 | tf_op jit(solution)/shard_map/ppermute | solution.py:24
  8.7 1.6 %copy-start = (bf16[128,2,32,128]{3,2,1,0:T(8,128)(2,1)S(1)}, bf16[128,2,32,128]{3,2,1,0:T(8,128)(2,1)}, u32[]{:S(2)}) copy-start(bf16[128,2,32,128]{3,2,1,0:T(8,128)(2,1)} %refs_8_.2) | copy-start | bytes 6291460
  10.3 1.6 %copy-start.2 = (bf16[128,2,32,128]{3,2,1,0:T(8,128)(2,1)S(1)}, bf16[128,2,32,128]{3,2,1,0:T(8,128)(2,1)}, u32[]{:S(2)}) copy-start(bf16[128,2,32,128]{3,2,1,0:T(8,128)(2,1)} %refs_7_.1) | copy-start | bytes 6291460
  11.9 1.6 %copy-start.3 = (bf16[32,2,128,128]{3,2,1,0:T(8,128)(2,1)S(1)}, bf16[32,2,128,128]{3,2,1,0:T(8,128)(2,1)}, u32[]{:S(2)}) copy-start(bf16[32,2,128,128]{3,2,1,0:T(8,128)(2,1)} %refs_9_.2) | copy-start | bytes 6291460
  13.5 0.9 %copy-start.5 = (bf16[32,8,256]{2,1,0:T(8,128)(2,1)S(1)}, bf16[32,8,256]{2,1,0:T(8,128)(2,1)}, u32[]{:S(2)}) copy-start(bf16[32,8,256]{2,1,0:T(8,128)(2,1)} %refs_3_.3) | copy-start | bytes 393220
  14.4 0.7 copy-start.9
  15.1 0.7 copy-start.10
  15.8 0.7 copy-start.11
  16.4 6.3 %copy-start.4 = (bf16[32,8,256]{2,1,0:T(8,128)(2,1)S(1)}, bf16[32,8,256]{2,1,0:T(8,128)(2,1)}, u32[]{:S(2)}) copy-start(bf16[32,8,256]{2,1,0:T(8,128)(2,1)} %refs_3_.2) | copy-start | bytes 393220
  16.4 27.7 %copy-start.1 = (bf16[128,2,32,128]{3,2,1,0:T(8,128)(2,1)S(1)}, bf16[128,2,32,128]{3,2,1,0:T(8,128)(2,1)}, u32[]{:S(2)}) copy-start(bf16[128,2,32,128]{3,2,1,0:T(8,128)(2,1)} %refs_8_.2) | copy-start | bytes 6291460
  22.5 28.5 %collective-permute-start.18 = (f32[96,16,128]{2,1,0:T(8,128)S(1)}, f32[96,16,128]{2,1,0:T(8,128)S(1)}, u32[]{:S(2)}, u32[]{:S(2)}) collective-permute-start(f32[96,16,128]{2,1,0:T(8,128)S(1)} %get-tuple-element.21), channel_id=1, source_target_pairs={{0,1},{1,0},{2,3},{3,2},{4,5},{5,4},{6,7},{7,6},{8,9},{9,8},{10,11... | collective-permute-start | bytes 2359304 | tf_op jit(solution)/shard_map/ppermute | solution.py:24
  22.7 8.0 %collective-permute-start.3 = (bf16[32,8,256]{2,1,0:T(8,128)(2,1)S(1)}, bf16[32,8,256]{2,1,0:T(8,128)(2,1)S(1)}, u32[]{:S(2)}, u32[]{:S(2)}) collective-permute-start(bf16[32,8,256]{2,1,0:T(8,128)(2,1)S(1)} %copy-done.4), channel_id=1, source_target_pairs={{0,28},{1,29},{2,30},{3,31},{4,0},{5,1},{6,2},{7,3},{8,4},{9,5},{1... | collective-permute-start | bytes 393224 | tf_op jit(solution)/shard_map/ppermute | solution.py:24
  27.5 5.5 %collective-permute-start.1 = (bf16[32,8,256]{2,1,0:T(8,128)(2,1)S(1)}, bf16[32,8,256]{2,1,0:T(8,128)(2,1)S(1)}, u32[]{:S(2)}, u32[]{:S(2)}) collective-permute-start(bf16[32,8,256]{2,1,0:T(8,128)(2,1)S(1)} %copy-done.4), channel_id=1, source_target_pairs={{0,2},{1,3},{2,0},{3,1},{4,6},{5,7},{6,4},{7,5},{8,10},{9,11},{10,... | collective-permute-start | bytes 393224 | tf_op jit(solution)/shard_map/ppermute | solution.py:24
  29.0 4.0 %collective-permute-start = (bf16[32,8,256]{2,1,0:T(8,128)(2,1)S(1)}, bf16[32,8,256]{2,1,0:T(8,128)(2,1)S(1)}, u32[]{:S(2)}, u32[]{:S(2)}) collective-permute-start(bf16[32,8,256]{2,1,0:T(8,128)(2,1)S(1)} %copy-done.4), channel_id=1, source_target_pairs={{0,1},{1,0},{2,3},{3,2},{4,5},{5,4},{6,7},{7,6},{8,9},{9,8},{10,11... | collective-permute-start | bytes 393224 | tf_op jit(solution)/shard_map/ppermute | solution.py:24
  29.0 8.6 %collective-permute-start.7 = (bf16[32,8,256]{2,1,0:T(8,128)(2,1)S(1)}, bf16[32,8,256]{2,1,0:T(8,128)(2,1)S(1)}, u32[]{:S(2)}, u32[]{:S(2)}) collective-permute-start(bf16[32,8,256]{2,1,0:T(8,128)(2,1)S(1)} %copy-done.4), channel_id=1, source_target_pairs={{0,4},{1,5},{2,6},{3,7},{4,8},{5,9},{6,10},{7,11},{8,12},{9,13},{1... | collective-permute-start | bytes 393224 | tf_op jit(solution)/shard_map/ppermute | solution.py:24
  30.7 7.4 %collective-permute-start.5 = (bf16[32,8,256]{2,1,0:T(8,128)(2,1)S(1)}, bf16[32,8,256]{2,1,0:T(8,128)(2,1)S(1)}, u32[]{:S(2)}, u32[]{:S(2)}) collective-permute-start(bf16[32,8,256]{2,1,0:T(8,128)(2,1)S(1)} %collective-permute-done.3.refs_7_), channel_id=1, source_target_pairs={{0,2},{1,3},{2,0},{3,1},{4,6},{5,7},{6,4},{7,5},{8,10},{9,11},{10,... | collective-permute-start | bytes 393224 | tf_op jit(solution)/shard_map/ppermute | solution.py:24
  33.0 5.2 %collective-permute-start.4 = (bf16[32,8,256]{2,1,0:T(8,128)(2,1)S(1)}, bf16[32,8,256]{2,1,0:T(8,128)(2,1)S(1)}, u32[]{:S(2)}, u32[]{:S(2)}) collective-permute-start(bf16[32,8,256]{2,1,0:T(8,128)(2,1)S(1)} %collective-permute-done.3.refs_7_), channel_id=1, source_target_pairs={{0,1},{1,0},{2,3},{3,2},{4,5},{5,4},{6,7},{7,6},{8,9},{9,8},{10,11... | collective-permute-start | bytes 393224 | tf_op jit(solution)/shard_map/ppermute | solution.py:24
  33.0 5.7 %collective-permute-start.2 = (bf16[32,8,256]{2,1,0:T(8,128)(2,1)S(1)}, bf16[32,8,256]{2,1,0:T(8,128)(2,1)S(1)}, u32[]{:S(2)}, u32[]{:S(2)}) collective-permute-start(bf16[32,8,256]{2,1,0:T(8,128)(2,1)S(1)} %collective-permute-done.1.refs_5_), channel_id=1, source_target_pairs={{0,1},{1,0},{2,3},{3,2},{4,5},{5,4},{6,7},{7,6},{8,9},{9,8},{10,11... | collective-permute-start | bytes 393224 | tf_op jit(solution)/shard_map/ppermute | solution.py:24
  37.6 5.1 %collective-permute-start.9 = (bf16[32,8,256]{2,1,0:T(8,128)(2,1)S(1)}, bf16[32,8,256]{2,1,0:T(8,128)(2,1)S(1)}, u32[]{:S(2)}, u32[]{:S(2)}) collective-permute-start(bf16[32,8,256]{2,1,0:T(8,128)(2,1)S(1)} %collective-permute-done.7.refs_11_), channel_id=1, source_target_pairs={{0,2},{1,3},{2,0},{3,1},{4,6},{5,7},{6,4},{7,5},{8,10},{9,11},{10,... | collective-permute-start | bytes 393224 | tf_op jit(solution)/shard_map/ppermute | solution.py:24
  38.1 16.5 %collective-permute-start.17 = (f32[96,16,128]{2,1,0:T(8,128)S(1)}, f32[96,16,128]{2,1,0:T(8,128)S(1)}, u32[]{:S(2)}, u32[]{:S(2)}) collective-permute-start(f32[96,16,128]{2,1,0:T(8,128)S(1)} %get-tuple-element.19), channel_id=1, source_target_pairs={{0,1},{1,0},{2,3},{3,2},{4,5},{5,4},{6,7},{7,6},{8,9},{9,8},{10,11... | collective-permute-start | bytes 2359304 | tf_op jit(solution)/shard_map/ppermute | solution.py:24
  38.1 4.6 %collective-permute-start.8 = (bf16[32,8,256]{2,1,0:T(8,128)(2,1)S(1)}, bf16[32,8,256]{2,1,0:T(8,128)(2,1)S(1)}, u32[]{:S(2)}, u32[]{:S(2)}) collective-permute-start(bf16[32,8,256]{2,1,0:T(8,128)(2,1)S(1)} %collective-permute-done.7.refs_11_), channel_id=1, source_target_pairs={{0,1},{1,0},{2,3},{3,2},{4,5},{5,4},{6,7},{7,6},{8,9},{9,8},{10,11... | collective-permute-start | bytes 393224 | tf_op jit(solution)/shard_map/ppermute | solution.py:24
  38.6 4.1 %collective-permute-start.6 = (bf16[32,8,256]{2,1,0:T(8,128)(2,1)S(1)}, bf16[32,8,256]{2,1,0:T(8,128)(2,1)S(1)}, u32[]{:S(2)}, u32[]{:S(2)}) collective-permute-start(bf16[32,8,256]{2,1,0:T(8,128)(2,1)S(1)} %collective-permute-done.5.refs_9_), channel_id=1, source_target_pairs={{0,1},{1,0},{2,3},{3,2},{4,5},{5,4},{6,7},{7,6},{8,9},{9,8},{10,11... | collective-permute-start | bytes 393224 | tf_op jit(solution)/shard_map/ppermute | solution.py:24
  42.7 1.3 %collective-permute-start.10 = (bf16[32,8,256]{2,1,0:T(8,128)(2,1)S(1)}, bf16[32,8,256]{2,1,0:T(8,128)(2,1)S(1)}, u32[]{:S(2)}, u32[]{:S(2)}) collective-permute-start(bf16[32,8,256]{2,1,0:T(8,128)(2,1)S(1)} %collective-permute-done.9.refs_13_), channel_id=1, source_target_pairs={{0,1},{1,0},{2,3},{3,2},{4,5},{5,4},{6,7},{7,6},{8,9},{9,8},{10,11... | collective-permute-start | bytes 393224 | tf_op jit(solution)/shard_map/ppermute | solution.py:24
  50.8 1.6 %collective-permute-start.12 = (f32[32,16,128]{2,1,0:T(8,128)S(1)}, f32[32,16,128]{2,1,0:T(8,128)S(1)}, u32[]{:S(2)}, u32[]{:S(2)}) collective-permute-start(f32[32,16,128]{2,1,0:T(8,128)S(1)} %get-tuple-element.17), channel_id=1, source_target_pairs={{0,1},{1,0},{2,3},{3,2},{4,5},{5,4},{6,7},{7,6},{8,9},{9,8},{10,11... | collective-permute-start | bytes 786440 | tf_op jit(solution)/shard_map/ppermute | solution.py:24
  51.1 18.2 %copy-start.6 = (s32[4,4096]{1,0:T(4,128)S(1)}, s32[4,4096]{1,0:T(4,128)}, u32[]{:S(2)}) copy-start(s32[4,4096]{1,0:T(4,128)} %refs_8_.3) | copy-start | bytes 196612
  51.1 18.2 %copy-start.7 = (f32[4,4096]{1,0:T(4,128)S(1)}, f32[4,4096]{1,0:T(4,128)}, u32[]{:S(2)}) copy-start(f32[4,4096]{1,0:T(4,128)} %refs_9_.3) | copy-start | bytes 196612
  51.1 18.2 %copy-start.8 = (s32[4096]{0:T(1024)S(1)}, s32[4096]{0:T(1024)}, u32[]{:S(2)}) copy-start(s32[4096]{0:T(1024)} %param.21) | copy-start | bytes 49156
  51.2 9.2 %collective-permute-start.20 = (bf16[64,16,128]{2,1,0:T(8,128)(2,1)S(1)}, bf16[64,16,128]{2,1,0:T(8,128)(2,1)S(1)}, u32[]{:S(2)}, u32[]{:S(2)}) collective-permute-start(bf16[64,16,128]{2,1,0:T(8,128)(2,1)S(1)} %slice.28), channel_id=1, source_target_pairs={{0,2},{1,3},{2,0},{3,1},{4,6},{5,7},{6,4},{7,5},{8,10},{9,11},{10,... | collective-permute-start | bytes 786440 | tf_op jit(solution)/shard_map/ppermute | solution.py:24
  51.7 10.8 %collective-permute-start.11 = (f32[32,16,128]{2,1,0:T(8,128)S(1)}, f32[32,16,128]{2,1,0:T(8,128)S(1)}, u32[]{:S(2)}, u32[]{:S(2)}) collective-permute-start(f32[32,16,128]{2,1,0:T(8,128)S(1)} %get-tuple-element.15), channel_id=1, source_target_pairs={{0,1},{1,0},{2,3},{3,2},{4,5},{5,4},{6,7},{7,6},{8,9},{9,8},{10,11... | collective-permute-start | bytes 786440 | tf_op jit(solution)/shard_map/ppermute | solution.py:24
  52.4 10.8 %collective-permute-start.13 = (bf16[32,16,128]{2,1,0:T(8,128)(2,1)S(1)}, bf16[32,16,128]{2,1,0:T(8,128)(2,1)S(1)}, u32[]{:S(2)}, u32[]{:S(2)}) collective-permute-start(bf16[32,16,128]{2,1,0:T(8,128)(2,1)S(1)} %add_convert_fusion.1), channel_id=1, source_target_pairs={{0,2},{1,3},{2,0},{3,1},{4,6},{5,7},{6,4},{7,5},{8,10},{9,11},{10,... | collective-permute-start | bytes 393224 | tf_op jit(solution)/shard_map/ppermute | solution.py:24
  53.5 12.0 %collective-permute-start.19 = (bf16[32,16,128]{2,1,0:T(8,128)(2,1)S(1)}, bf16[32,16,128]{2,1,0:T(8,128)(2,1)S(1)}, u32[]{:S(2)}, u32[]{:S(2)}) collective-permute-start(bf16[32,16,128]{2,1,0:T(8,128)(2,1)S(1)} %slice.26), channel_id=1, source_target_pairs={{0,2},{1,3},{2,0},{3,1},{4,6},{5,7},{6,4},{7,5},{8,10},{9,11},{10,... | collective-permute-start | bytes 393224 | tf_op jit(solution)/shard_map/ppermute | solution.py:24
  60.5 5.0 %collective-permute-start.22 = (bf16[32,16,128]{2,1,0:T(8,128)(2,1)S(1)}, bf16[32,16,128]{2,1,0:T(8,128)(2,1)S(1)}, u32[]{:S(2)}, u32[]{:S(2)}) collective-permute-start(bf16[32,16,128]{2,1,0:T(8,128)(2,1)S(1)} %get-tuple-element.25), channel_id=1, source_target_pairs={{0,28},{1,29},{2,30},{3,31},{4,0},{5,1},{6,2},{7,3},{8,4},{9,5},{1... | collective-permute-start | bytes 393224 | tf_op jit(solution)/shard_map/ppermute | solution.py:24
  61.6 7.7 %collective-permute-start.21 = (bf16[32,16,128]{2,1,0:T(8,128)(2,1)S(1)}, bf16[32,16,128]{2,1,0:T(8,128)(2,1)S(1)}, u32[]{:S(2)}, u32[]{:S(2)}) collective-permute-start(bf16[32,16,128]{2,1,0:T(8,128)(2,1)S(1)} %get-tuple-element.26), channel_id=1, source_target_pairs={{0,4},{1,5},{2,6},{3,7},{4,8},{5,9},{6,10},{7,11},{8,12},{9,13},{1... | collective-permute-start | bytes 393224 | tf_op jit(solution)/shard_map/ppermute | solution.py:24

commit v2 on v1

--- a/solution.py
+++ b/solution.py
@@ -12,6 +12,7 @@
 FAR_UNROLL = 16
 NEAR_UNROLL = 4
 VMEM_BYTES = 40 * 1024 * 1024
+LOAD_BYTES = 40 * 1024 * 1024
 
 
 def moved(x, by, mask):
@@ -31,12 +32,16 @@
 
 
 def block_kernel(transposed, total, members, *refs):
-    far_ids, ranks, near_ids = refs[:3]
+    tables_in = refs[:3]
     halves = 1 if transposed else 3
     pieces = refs[3 : 3 + halves * members]
     first, second, near = refs[3 + halves * members : 6 + halves * members]
     outs = refs[6 + halves * members : 6 + halves * members + members]
-    lhs, coeffs = refs[6 + halves * members + members :]
+    lhs, coeffs, far_ids, ranks, near_ids, sems = refs[6 + halves * members + members :]
+    tables = (far_ids, ranks, near_ids)
+    copies = [pltpu.make_async_copy(a, b, sems.at[i]) for i, (a, b) in enumerate(zip(tables_in, tables))]
+    for copy in copies:
+        copy.start()
     clusters, height, _ = pieces[0].shape
     far, _, rank, width = first.shape
     near_total = near.shape[0]
@@ -56,6 +61,9 @@
                 right += [-im, re]
             both = [jnp.concatenate(left, axis=0), jnp.concatenate(right, axis=0)]
             lhs[g * clusters + c] = jnp.concatenate(both, axis=1).astype(jnp.bfloat16)
+
+    for copy in copies:
+        copy.wait()
 
     def add(place, value):
         for i, out in enumerate(outs):
@@ -122,12 +130,13 @@
     out_clusters = 3 * clusters if transposed else clusters
     rows = members * 2 * height
     rank, width = first.shape[2:]
-    smem = pl.BlockSpec(memory_space=pltpu.SMEM)
+    anywhere = pl.BlockSpec(memory_space=pl.ANY)
     vmem = pl.BlockSpec(memory_space=pltpu.VMEM)
+    tables = (far_ids, ranks, near_ids)
     flops = 2 * rows * (first.shape[0] * 2 * 2 * rank * 2 * width + near.shape[0] * 2 * width * width)
     return pl.pallas_call(
         functools.partial(block_kernel, transposed, total, members),
-        in_specs=[smem] * 3 + [vmem] * (len(pieces) + 3),
+        in_specs=[anywhere] * 3 + [vmem] * (len(pieces) + 3),
         out_specs=[vmem] * members,
         out_shape=[
             jax.ShapeDtypeStruct((out_clusters, 2 * height, width), jnp.float32)
@@ -135,10 +144,40 @@
         scratch_shapes=[
             pltpu.VMEM((halves * clusters, rows, double), jnp.bfloat16),
             pltpu.VMEM((min(FAR_UNROLL, first.shape[0]), rows, 2 * rank), jnp.bfloat16),
+            *[pltpu.SMEM(t.shape, t.dtype) for t in tables],
+            pltpu.SemaphoreType.DMA((len(tables),)),
         ],
         compiler_params=pltpu.CompilerParams(vmem_limit_bytes=VMEM_BYTES),
         cost_estimate=pl.CostEstimate(flops=flops, bytes_accessed=20_000_000, transcendentals=0),
-    )(far_ids, ranks, near_ids, *pieces, first, second, near)
+    )(*tables, *pieces, first, second, near)
+
+
+def load_kernel(parts, *refs):
+    count = (len(refs) - 1) // 2
+    sources, targets, sems = refs[:count], refs[count : 2 * count], refs[2 * count]
+    copies = []
+    for i, (source, target) in enumerate(zip(sources, targets)):
+        length = source.shape[0] // parts
+        for k in range(parts):
+            at = pl.ds(k * length, length)
+            copies.append(pltpu.make_async_copy(source.at[at], target.at[at], sems.at[i, k]))
+    for copy in copies:
+        copy.start()
+    for copy in copies:
+        copy.wait()
+
+
+def loaded(*arrays):
+    parts = 4
+    return pl.pallas_call(
+        functools.partial(load_kernel, parts),
+        in_specs=[pl.BlockSpec(memory_space=pltpu.HBM)] * len(arrays),
+        out_specs=[pl.BlockSpec(memory_space=pltpu.VMEM)] * len(arrays),
+        out_shape=[jax.ShapeDtypeStruct(a.shape, a.dtype) for a in arrays],
+        scratch_shapes=[pltpu.SemaphoreType.DMA((len(arrays), parts))],
+        compiler_params=pltpu.CompilerParams(vmem_limit_bytes=LOAD_BYTES),
+        cost_estimate=pl.CostEstimate(flops=0, bytes_accessed=12_000_000, transcendentals=0),
+    )(*arrays)
 
 
 def final_kernel(column_total, n_fwd, n_adj, *refs):
@@ -231,37 +270,41 @@
     column_total = forward_rhs.shape[1] * members
     evens = range(0, members, 2)
 
-    def all_columns(mine):
+    def across(x):
+        return [x if m == 0 else moved(x, 0, m) for m in evens]
+
+    def both_cores(mine):
         pieces = []
         for x in mine:
             pieces += [x, moved(x, 0, 1)]
         return pieces
 
-    w_mine = [adjoint_rhs if m == 0 else moved(adjoint_rhs, 0, m) for m in evens]
-    w_pieces = all_columns(w_mine)
+    tie = lax.optimization_barrier
+    w_mine = across(adjoint_rhs)
     x_next, x_prev = moved(forward_rhs, -1, 0), moved(forward_rhs, 1, 0)
-    x_pieces = []
-    for x in (forward_rhs, x_next, x_prev):
-        x_pieces += all_columns([x if m == 0 else moved(x, 0, m) for m in evens])
-
-    apply = functools.partial(apply_blocks, total=total, members=members)
-    adj_parts = apply(
-        True, far_ids=far_clusters, ranks=far_ranks, near_ids=near_clusters,
-        pieces=w_pieces, first=far_left, second=far_right, near=near_blocks,
+    factors = loaded(far_left, far_right, near_blocks)
+    w_mine, factors = tie((w_mine, factors))
+    left, right, near = factors
+    w_pieces = both_cores(w_mine)
+    w_pieces, x_next, x_prev = tie((w_pieces, x_next, x_prev))
+    x_mine = [*across(forward_rhs), *across(x_next), *across(x_prev)]
+
+    apply = functools.partial(
+        apply_blocks, total=total, members=members, far_ids=far_clusters, ranks=far_ranks, near_ids=near_clusters
     )
+    adj_parts = apply(True, pieces=w_pieces, first=left, second=right, near=near)
+    adj_parts, x_mine = tie((adj_parts, x_mine))
     adj_core = [moved(adj_parts[m + 1], 0, 1) for m in evens]
-    fwd_parts = apply(
-        False, far_ids=far_clusters, ranks=far_ranks, near_ids=near_clusters,
-        pieces=x_pieces, first=far_right, second=far_left, near=near_blocks,
-    )
+    x_pieces = both_cores(x_mine)
+    away = {
+        m: (adj_parts[m] + adj_core[k]).astype(jnp.bfloat16) for k, m in enumerate(evens) if m
+    }
+    x_pieces, away = tie((x_pieces, away))
+    sides = [moved(away[m][clusters:], 0, m) for m in away]
+    own = [moved(away[m][:clusters], 0, m) for m in away]
+    fwd_parts = apply(False, pieces=x_pieces, first=right, second=left, near=near)
     fwd_core = [moved(fwd_parts[m + 1], 0, 1) for m in evens]
 
-    sides, own = [], []
-    for k, m in enumerate(evens):
-        if m:
-            both = adj_parts[m] + adj_core[k]
-            sides.append(moved(both[clusters:].astype(jnp.bfloat16), 0, m))
-            own.append(moved(both[:clusters].astype(jnp.bfloat16), 0, m))
     side = adj_parts[0][clusters:] + adj_core[0][clusters:]
     for s in sides:
         side = side + s.astype(jnp.float32)

time: 82.1 us -> 64 us (0.78)
  waiting for transfers between devices: 30 us -> 10.9 us
  local copies, waits for them, and re-layouts: 7.76 us -> 5.16 us
  starting transfers between devices: 17.8 us -> 20.4 us
  blocking collectives: 8.83 us -> 10.2 us
    ppermute x23, waiting for transfers between devices: 30 us -> 10.9 us  [moved(): return lax.ppermute(x, AXES, pairs)]
    unnamed x24 -> x22, local copies, waits for them, and re-layouts: 7.71 us -> 5.11 us
    ppermute x23, starting transfers between devices: 17.8 us -> 20.4 us  [moved(): return lax.ppermute(x, AXES, pairs)]
    all_to_all x1, blocking collectives: 8.83 us -> 10.2 us  [shards(): lax.all_to_all(spread.reshape(devices, PAR_DEV), AXES, 0, 0, tiled=True)]
    pallas_call x2, Pallas kernels: 12.8 us -> 11.9 us  [apply_blocks(): pl.pallas_call(functools.partial(block_kernel, transposed, total, members...]
  transfers between devices with their start and end apart: 23 -> 23, of which waited for: 13 -> 8; matrix products, arithmetic and copies ran while one was open for 0% -> 0% of each run, Pallas kernels for 8% -> 20%
where the time goes in v2:
time: 64 us; the launch traced here: 63.7 us
  starting transfers between devices  20.4 us (32%)
  Pallas kernels  15.5 us (24%)
  waiting for transfers between devices  10.9 us (17%)
  blocking collectives  10.2 us (16%)
  local copies, waits for them, and re-layouts  5.16 us (8%)
  other arithmetic  0.8 us (1%)
  between operations  0.8 us (1%)
    ppermute x23, starting transfers between devices, moved(): return lax.ppermute(x, AXES, pairs)  20.4 us
    pallas_call x2, Pallas kernels, apply_blocks(): pl.pallas_call(functools.partial(block_kernel, transposed, total, members...  11.9 us
    ppermute x23, waiting for transfers between devices, moved(): return lax.ppermute(x, AXES, pairs)  10.9 us
    all_to_all x1, blocking collectives, shards(): lax.all_to_all(spread.reshape(devices, PAR_DEV), AXES, 0, 0, tiled=True)  10.2 us
    unnamed x22, local copies, waits for them, and re-layouts  5.11 us
    pallas_call x1, Pallas kernels, finish(): pl.pallas_call(functools.partial(final_kernel, column_total, len(fwd_term...  3.11 us
  transfers between devices with their start and end apart: 23, of which 8 were waited for; matrix products, arithmetic and copies ran while one was open for 0% of the time, Pallas kernels for 20%

profile of v2, /device:TPU:0, one launch (start us, length us, event | category | flops | bytes accessed | tf_op | source)
XLA Modules:
  0.0 63.7 jit_solution(3526189279097127054)
XLA Ops:
  0.6 3.0 %collective-permute-start = (bf16[32,8,256]{2,1,0:T(8,128)(2,1)}, bf16[32,8,256]{2,1,0:T(8,128)(2,1)S(1)}, u32[]{:S(2)}, u32[]{:S(2)}) collective-permute-start(bf16[32,8,256]{2,1,0:T(8,128)(2,1)} %refs_3_), channel_id=1, source_target_pairs={{0,2},{1,3},{2,0},{3,1},{4,6},{5,7},{6,4},{7,5},{8,10},{9,11},{10,... | collective-permute-start | bytes 393224 | tf_op jit(solution)/shard_map/ppermute | solution.py:25
  3.7 4.5 %collective-permute-start.3 = (bf16[32,8,256]{2,1,0:T(8,128)(2,1)}, bf16[32,8,256]{2,1,0:T(8,128)(2,1)S(1)}, u32[]{:S(2)}, u32[]{:S(2)}) collective-permute-start(bf16[32,8,256]{2,1,0:T(8,128)(2,1)} %refs_3_.1), channel_id=1, source_target_pairs={{0,28},{1,29},{2,30},{3,31},{4,0},{5,1},{6,2},{7,3},{8,4},{9,5},{1... | collective-permute-start | bytes 393224 | tf_op jit(solution)/shard_map/ppermute | solution.py:25
  8.2 0.0 collective-permute-start.4
  8.2 1.6 %copy-done = bf16[128,2,32,128]{3,2,1,0:T(8,128)(2,1)S(1)} copy-done((bf16[128,2,32,128]{3,2,1,0:T(8,128)(2,1)S(1)}, bf16[128,2,32,128]{3,2,1,0:T(8,128)(2,1)}, u32[]{:S(2)}) %copy-start) | copy-done | bytes 2097176
  9.8 1.6 %copy-done.1 = bf16[128,2,32,128]{3,2,1,0:T(8,128)(2,1)S(1)} copy-done((bf16[128,2,32,128]{3,2,1,0:T(8,128)(2,1)S(1)}, bf16[128,2,32,128]{3,2,1,0:T(8,128)(2,1)}, u32[]{:S(2)}) %copy-start.1) | copy-done | bytes 2097176
  11.4 1.6 %copy-done.2 = bf16[32,2,128,128]{3,2,1,0:T(8,128)(2,1)S(1)} copy-done((bf16[32,2,128,128]{3,2,1,0:T(8,128)(2,1)S(1)}, bf16[32,2,128,128]{3,2,1,0:T(8,128)(2,1)}, u32[]{:S(2)}) %copy-start.2) | copy-done | bytes 2097176
  13.0 0.0 copy-start.10
  13.0 0.6 shard_map.130
  13.6 0.0 collective-permute-done.refs_5_
  13.6 0.3 copy-done.4
  13.9 0.0 collective-permute-start.1
  13.9 0.5 collective-permute-start.2
  14.4 0.5 collective-permute-start.5
  14.9 0.0 collective-permute-done.3.refs_7_
  14.9 1.2 %collective-permute-done.4.refs_11_ = bf16[32,8,256]{2,1,0:T(8,128)(2,1)S(1)} collective-permute-done((bf16[32,8,256]{2,1,0:T(8,128)(2,1)}, bf16[32,8,256]{2,1,0:T(8,128)(2,1)S(1)}, u32[]{:S(2)}, u32[]{:S(2)}) %collective-permute-start.4) | collective-permute-done | bytes 131104 | tf_op jit(solution)/shard_map/ppermute | solution.py:25
  16.1 0.0 collective-permute-done.1.refs_4_
  16.1 0.0 collective-permute-done.2.refs_6_
  16.1 0.5 collective-permute-start.6
  16.6 1.5 %collective-permute-start.7 = (bf16[32,8,256]{2,1,0:T(8,128)(2,1)S(1)}, bf16[32,8,256]{2,1,0:T(8,128)(2,1)S(1)}, u32[]{:S(2)}, u32[]{:S(2)}) collective-permute-start(bf16[32,8,256]{2,1,0:T(8,128)(2,1)S(1)} %collective-permute-done.4.refs_11_), channel_id=1, source_target_pairs={{0,2},{1,3},{2,0},{3,1},{4,6},{5,7},{6,4},{7,5},{8,10},{9,11},{10,... | collective-permute-start | bytes 393224 | tf_op jit(solution)/shard_map/ppermute | solution.py:25
  18.1 0.0 copy-done.9
  18.1 5.7 %shard_map.131 = (f32[96,16,128]{2,1,0:T(8,128)S(1)}, f32[96,16,128]{2,1,0:T(8,128)S(1)}, f32[96,16,128]{2,1,0:T(8,128)S(1)}, f32[96,16,128]{2,1,0:T(8,128)S(1)}) custom-call(s32[2,128]{1,0:T(2,128)S(1)} %copy-done.8, s32[128]{0:T(128)S(1)} %copy-done.10, s32[2,32]{1,0:T(2,128)S(1)} %copy-done.9, bf16[32,8,256]{2,1,0:T(8,128)(2,1)S(1)} %copy-done.4, ...), custom_call_target="tpu_custom_call" | custom-call | flops 671088640 | bytes 20000000 | tf_op jit(solution)/shard_map/pallas_call | solution.py:137
  23.8 0.0 collective-permute-done.5.refs_5_
  23.8 0.0 collective-permute-done.6.refs_9_
  23.9 1.6 %collective-permute-done.7.refs_13_ = bf16[32,8,256]{2,1,0:T(8,128)(2,1)S(1)} collective-permute-done((bf16[32,8,256]{2,1,0:T(8,128)(2,1)S(1)}, bf16[32,8,256]{2,1,0:T(8,128)(2,1)S(1)}, u32[]{:S(2)}, u32[]{:S(2)}) %collective-permute-start.7) | collective-permute-done | bytes 131104 | tf_op jit(solution)/shard_map/ppermute | solution.py:25
  25.4 0.0 collective-permute-start.14
  25.4 0.5 collective-permute-start.18
  25.9 0.0 collective-permute-start.10
  25.9 0.5 collective-permute-start.11
  26.4 0.0 collective-permute-start.12
  26.4 2.6 %collective-permute-done.10.refs_8_ = bf16[32,8,256]{2,1,0:T(8,128)(2,1)S(1)} collective-permute-done((bf16[32,8,256]{2,1,0:T(8,128)(2,1)S(1)}, bf16[32,8,256]{2,1,0:T(8,128)(2,1)S(1)}, u32[]{:S(2)}, u32[]{:S(2)}) %collective-permute-start.10) | collective-permute-done | bytes 131104 | tf_op jit(solution)/shard_map/ppermute | solution.py:25
  29.0 0.1 collective-permute-start.13
  29.2 0.0 collective-permute-done.11.refs_10_
  29.2 0.3 collective-permute-start.8
  29.5 0.0 collective-permute-done.14
  29.5 0.2 collective-permute-start.9
  29.7 0.1 add_convert_fusion
  29.8 0.0 collective-permute-done.12.refs_12_
  29.8 0.5 collective-permute-done.13.refs_14_
  30.4 0.2 collective-permute-done.8.refs_4_
  30.6 0.3 collective-permute-done.9.refs_6_
  30.9 0.6 collective-permute-start.20
  31.5 6.2 %shard_map.132 = (f32[32,16,128]{2,1,0:T(8,128)S(1)}, f32[32,16,128]{2,1,0:T(8,128)S(1)}, f32[32,16,128]{2,1,0:T(8,128)S(1)}, f32[32,16,128]{2,1,0:T(8,128)S(1)}) custom-call(s32[2,128]{1,0:T(2,128)S(1)} %copy-done.8, s32[128]{0:T(128)S(1)} %copy-done.10, s32[2,32]{1,0:T(2,128)S(1)} %copy-done.9, bf16[32,8,256]{2,1,0:T(8,128)(2,1)S(1)} %copy-done.3, ...), custom_call_target="tpu_custom_call" | custom-call | flops 671088640 | bytes 20000000 | tf_op jit(solution)/shard_map/pallas_call | solution.py:137
  37.7 0.0 copy-start.5
  37.7 0.0 copy-start.6
  37.7 0.0 copy-start.7
  37.7 0.1 collective-permute-start.16
  37.8 0.5 collective-permute-start.15
  38.3 1.5 %collective-permute-start.19 = (bf16[32,16,128]{2,1,0:T(8,128)(2,1)S(1)}, bf16[32,16,128]{2,1,0:T(8,128)(2,1)S(1)}, u32[]{:S(2)}, u32[]{:S(2)}) collective-permute-start(bf16[32,16,128]{2,1,0:T(8,128)(2,1)S(1)} %slice.18), channel_id=1, source_target_pairs={{0,2},{1,3},{2,0},{3,1},{4,6},{5,7},{6,4},{7,5},{8,10},{9,11},{10,... | collective-permute-start | bytes 393224 | tf_op jit(solution)/shard_map/ppermute | solution.py:25
  39.8 0.0 collective-permute-done.18.refs_4_
  39.8 0.0 collective-permute-done.20
  39.8 0.1 fusion.1
  39.9 0.1 collective-permute-start.21
  40.0 4.8 %collective-permute-start.22 = (bf16[32,16,128]{2,1,0:T(8,128)(2,1)S(1)}, bf16[32,16,128]{2,1,0:T(8,128)(2,1)S(1)}, u32[]{:S(2)}, u32[]{:S(2)}) collective-permute-start(bf16[32,16,128]{2,1,0:T(8,128)(2,1)S(1)} %get-tuple-element.99), channel_id=1, source_target_pairs={{0,28},{1,29},{2,30},{3,31},{4,0},{5,1},{6,2},{7,3},{8,4},{9,5},{1... | collective-permute-start | bytes 393224 | tf_op jit(solution)/shard_map/ppermute | solution.py:25
  44.8 0.0 collective-permute-done.16
  44.8 0.6 collective-permute-start.17
  45.4 0.0 collective-permute-done.19.refs_5_
  45.4 0.0 collective-permute-done.15.refs_1_
  45.4 2.8 %collective-permute-done.21.refs_6_ = bf16[32,16,128]{2,1,0:T(8,128)(2,1)S(1)} collective-permute-done((bf16[32,16,128]{2,1,0:T(8,128)(2,1)S(1)}, bf16[32,16,128]{2,1,0:T(8,128)(2,1)S(1)}, u32[]{:S(2)}, u32[]{:S(2)}) %collective-permute-start.21) | collective-permute-done | bytes 131104 | tf_op jit(solution)/shard_map/ppermute | solution.py:25
  48.2 0.0 collective-permute-done.22.refs_7_
  48.2 1.7 %collective-permute-done.17.refs_2_ = bf16[32,16,128]{2,1,0:T(8,128)(2,1)S(1)} collective-permute-done((bf16[32,16,128]{2,1,0:T(8,128)(2,1)S(1)}, bf16[32,16,128]{2,1,0:T(8,128)(2,1)S(1)}, u32[]{:S(2)}, u32[]{:S(2)}) %collective-permute-start.17) | collective-permute-done | bytes 131104 | tf_op jit(solution)/shard_map/ppermute | solution.py:25
  49.9 0.0 copy-done.6
  49.9 3.1 %shard_map.133 = (f32[32,8,256]{2,1,0:T(8,128)}, f32[32,8,256]{2,1,0:T(8,128)}, f32[32,128]{1,0:T(8,128)S(1)}) custom-call(f32[32,16,128]{2,1,0:T(8,128)S(1)} %get-tuple-element.89.refs_0_, f32[32,16,128]{2,1,0:T(8,128)S(1)} %collective-permute-done.15.refs_1_, bf16[32,16,128]{2,1,0:T(8,128)(2,1)S(1)} %collective-permute-done.17.refs_2_, ...), custom_call_target="tpu_custom_call" | custom-call | flops 200000000 | bytes 3000000 | tf_op jit(solution)/shard_map/pallas_call | solution.py:241
  53.0 10.2 %all_to_all.9 = f32[32,1,128]{2,1,0:T(1,128)S(1)} all-to-all(f32[32,1,128]{2,1,0:T(1,128)S(1)} %bitcast.5), channel_id=1, replica_groups=mesh['clus'=8,'sub'=4] {'clus','sub'}, dimensions={0} | all-to-all | bytes 32768 | tf_op jit(solution)/shard_map/all_to_all | solution.py:325
  63.2 0.6 reduce_sum.9
  (16 shorter events, 0.1 us)
Async XLA Ops:
  0.6 12.9 %collective-permute-start = (bf16[32,8,256]{2,1,0:T(8,128)(2,1)}, bf16[32,8,256]{2,1,0:T(8,128)(2,1)S(1)}, u32[]{:S(2)}, u32[]{:S(2)}) collective-permute-start(bf16[32,8,256]{2,1,0:T(8,128)(2,1)} %refs_3_), channel_id=1, source_target_pairs={{0,2},{1,3},{2,0},{3,1},{4,6},{5,7},{6,4},{7,5},{8,10},{9,11},{10,... | collective-permute-start | bytes 393224 | tf_op jit(solution)/shard_map/ppermute | solution.py:25
  3.7 11.2 %collective-permute-start.3 = (bf16[32,8,256]{2,1,0:T(8,128)(2,1)}, bf16[32,8,256]{2,1,0:T(8,128)(2,1)S(1)}, u32[]{:S(2)}, u32[]{:S(2)}) collective-permute-start(bf16[32,8,256]{2,1,0:T(8,128)(2,1)} %refs_3_.1), channel_id=1, source_target_pairs={{0,28},{1,29},{2,30},{3,31},{4,0},{5,1},{6,2},{7,3},{8,4},{9,5},{1... | collective-permute-start | bytes 393224 | tf_op jit(solution)/shard_map/ppermute | solution.py:25
  8.2 7.9 %collective-permute-start.4 = (bf16[32,8,256]{2,1,0:T(8,128)(2,1)}, bf16[32,8,256]{2,1,0:T(8,128)(2,1)S(1)}, u32[]{:S(2)}, u32[]{:S(2)}) collective-permute-start(bf16[32,8,256]{2,1,0:T(8,128)(2,1)} %refs_3_.1), channel_id=1, source_target_pairs={{0,4},{1,5},{2,6},{3,7},{4,8},{5,9},{6,10},{7,11},{8,12},{9,13},{1... | collective-permute-start | bytes 393224 | tf_op jit(solution)/shard_map/ppermute | solution.py:25
  8.2 1.6 %copy-start = (bf16[128,2,32,128]{3,2,1,0:T(8,128)(2,1)S(1)}, bf16[128,2,32,128]{3,2,1,0:T(8,128)(2,1)}, u32[]{:S(2)}) copy-start(bf16[128,2,32,128]{3,2,1,0:T(8,128)(2,1)} %refs_0_.3) | copy-start | bytes 6291460
  9.8 1.6 %copy-start.1 = (bf16[128,2,32,128]{3,2,1,0:T(8,128)(2,1)S(1)}, bf16[128,2,32,128]{3,2,1,0:T(8,128)(2,1)}, u32[]{:S(2)}) copy-start(bf16[128,2,32,128]{3,2,1,0:T(8,128)(2,1)} %refs_1_.3) | copy-start | bytes 6291460
  11.4 1.6 %copy-start.2 = (bf16[32,2,128,128]{3,2,1,0:T(8,128)(2,1)S(1)}, bf16[32,2,128,128]{3,2,1,0:T(8,128)(2,1)}, u32[]{:S(2)}) copy-start(bf16[32,2,128,128]{3,2,1,0:T(8,128)(2,1)} %refs_2_.3) | copy-start | bytes 6291460
  13.0 0.9 %copy-start.4 = (bf16[32,8,256]{2,1,0:T(8,128)(2,1)S(1)}, bf16[32,8,256]{2,1,0:T(8,128)(2,1)}, u32[]{:S(2)}) copy-start(bf16[32,8,256]{2,1,0:T(8,128)(2,1)} %refs_3_) | copy-start | bytes 393220
  13.0 1.4 %copy-start.3 = (bf16[32,8,256]{2,1,0:T(8,128)(2,1)S(1)}, bf16[32,8,256]{2,1,0:T(8,128)(2,1)}, u32[]{:S(2)}) copy-start(bf16[32,8,256]{2,1,0:T(8,128)(2,1)} %refs_3_.1) | copy-start | bytes 393220
  13.0 5.1 %copy-start.8 = (s32[2,128]{1,0:T(2,128)S(1)}, s32[2,128]{1,0:T(2,128)}, u32[]{:S(2)}) copy-start(s32[2,128]{1,0:T(2,128)} %refs_0_.5) | copy-start | bytes 3076
  13.0 5.1 %copy-start.9 = (s32[2,32]{1,0:T(2,128)S(1)}, s32[2,32]{1,0:T(2,128)}, u32[]{:S(2)}) copy-start(s32[2,32]{1,0:T(2,128)} %refs_2_.5) | copy-start | bytes 772
  13.0 5.1 %copy-start.10 = (s32[128]{0:T(128)S(1)}, s32[128]{0:T(128)}, u32[]{:S(2)}) copy-start(s32[128]{0:T(128)} %refs_1_.5) | copy-start | bytes 1540
  13.9 2.2 %collective-permute-start.1 = (bf16[32,8,256]{2,1,0:T(8,128)(2,1)S(1)}, bf16[32,8,256]{2,1,0:T(8,128)(2,1)S(1)}, u32[]{:S(2)}, u32[]{:S(2)}) collective-permute-start(bf16[32,8,256]{2,1,0:T(8,128)(2,1)S(1)} %copy-done.4), channel_id=1, source_target_pairs={{0,1},{1,0},{2,3},{3,2},{4,5},{5,4},{6,7},{7,6},{8,9},{9,8},{10,11... | collective-permute-start | bytes 393224 | tf_op jit(solution)/shard_map/ppermute | solution.py:25
  13.9 2.2 %collective-permute-start.2 = (bf16[32,8,256]{2,1,0:T(8,128)(2,1)S(1)}, bf16[32,8,256]{2,1,0:T(8,128)(2,1)S(1)}, u32[]{:S(2)}, u32[]{:S(2)}) collective-permute-start(bf16[32,8,256]{2,1,0:T(8,128)(2,1)S(1)} %collective-permute-done.refs_5_), channel_id=1, source_target_pairs={{0,1},{1,0},{2,3},{3,2},{4,5},{5,4},{6,7},{7,6},{8,9},{9,8},{10,11... | collective-permute-start | bytes 393224 | tf_op jit(solution)/shard_map/ppermute | solution.py:25
  14.4 9.4 %collective-permute-start.5 = (bf16[32,8,256]{2,1,0:T(8,128)(2,1)S(1)}, bf16[32,8,256]{2,1,0:T(8,128)(2,1)S(1)}, u32[]{:S(2)}, u32[]{:S(2)}) collective-permute-start(bf16[32,8,256]{2,1,0:T(8,128)(2,1)S(1)} %copy-done.3), channel_id=1, source_target_pairs={{0,2},{1,3},{2,0},{3,1},{4,6},{5,7},{6,4},{7,5},{8,10},{9,11},{10,... | collective-permute-start | bytes 393224 | tf_op jit(solution)/shard_map/ppermute | solution.py:25
  16.1 7.8 %collective-permute-start.6 = (bf16[32,8,256]{2,1,0:T(8,128)(2,1)S(1)}, bf16[32,8,256]{2,1,0:T(8,128)(2,1)S(1)}, u32[]{:S(2)}, u32[]{:S(2)}) collective-permute-start(bf16[32,8,256]{2,1,0:T(8,128)(2,1)S(1)} %collective-permute-done.3.refs_7_), channel_id=1, source_target_pairs={{0,2},{1,3},{2,0},{3,1},{4,6},{5,7},{6,4},{7,5},{8,10},{9,11},{10,... | collective-permute-start | bytes 393224 | tf_op jit(solution)/shard_map/ppermute | solution.py:25
  16.6 8.8 %collective-permute-start.7 = (bf16[32,8,256]{2,1,0:T(8,128)(2,1)S(1)}, bf16[32,8,256]{2,1,0:T(8,128)(2,1)S(1)}, u32[]{:S(2)}, u32[]{:S(2)}) collective-permute-start(bf16[32,8,256]{2,1,0:T(8,128)(2,1)S(1)} %collective-permute-done.4.refs_11_), channel_id=1, source_target_pairs={{0,2},{1,3},{2,0},{3,1},{4,6},{5,7},{6,4},{7,5},{8,10},{9,11},{10,... | collective-permute-start | bytes 393224 | tf_op jit(solution)/shard_map/ppermute | solution.py:25
  25.4 4.1 %collective-permute-start.14 = (f32[96,16,128]{2,1,0:T(8,128)S(1)}, f32[96,16,128]{2,1,0:T(8,128)S(1)}, u32[]{:S(2)}, u32[]{:S(2)}) collective-permute-start(f32[96,16,128]{2,1,0:T(8,128)S(1)} %get-tuple-element.76), channel_id=1, source_target_pairs={{0,1},{1,0},{2,3},{3,2},{4,5},{5,4},{6,7},{7,6},{8,9},{9,8},{10,11... | collective-permute-start | bytes 2359304 | tf_op jit(solution)/shard_map/ppermute | solution.py:25
  25.4 14.4 %collective-permute-start.18 = (f32[96,16,128]{2,1,0:T(8,128)S(1)}, f32[96,16,128]{2,1,0:T(8,128)S(1)}, u32[]{:S(2)}, u32[]{:S(2)}) collective-permute-start(f32[96,16,128]{2,1,0:T(8,128)S(1)} %get-tuple-element.94), channel_id=1, source_target_pairs={{0,1},{1,0},{2,3},{3,2},{4,5},{5,4},{6,7},{7,6},{8,9},{9,8},{10,11... | collective-permute-start | bytes 2359304 | tf_op jit(solution)/shard_map/ppermute | solution.py:25
  25.9 3.1 %collective-permute-start.10 = (bf16[32,8,256]{2,1,0:T(8,128)(2,1)S(1)}, bf16[32,8,256]{2,1,0:T(8,128)(2,1)S(1)}, u32[]{:S(2)}, u32[]{:S(2)}) collective-permute-start(bf16[32,8,256]{2,1,0:T(8,128)(2,1)S(1)} %collective-permute-done.3.refs_7_), channel_id=1, source_target_pairs={{0,1},{1,0},{2,3},{3,2},{4,5},{5,4},{6,7},{7,6},{8,9},{9,8},{10,11... | collective-permute-start | bytes 393224 | tf_op jit(solution)/shard_map/ppermute | solution.py:25
  25.9 3.3 %collective-permute-start.11 = (bf16[32,8,256]{2,1,0:T(8,128)(2,1)S(1)}, bf16[32,8,256]{2,1,0:T(8,128)(2,1)S(1)}, u32[]{:S(2)}, u32[]{:S(2)}) collective-permute-start(bf16[32,8,256]{2,1,0:T(8,128)(2,1)S(1)} %collective-permute-done.6.refs_9_), channel_id=1, source_target_pairs={{0,1},{1,0},{2,3},{3,2},{4,5},{5,4},{6,7},{7,6},{8,9},{9,8},{10,11... | collective-permute-start | bytes 393224 | tf_op jit(solution)/shard_map/ppermute | solution.py:25
  26.4 3.4 %collective-permute-start.12 = (bf16[32,8,256]{2,1,0:T(8,128)(2,1)S(1)}, bf16[32,8,256]{2,1,0:T(8,128)(2,1)S(1)}, u32[]{:S(2)}, u32[]{:S(2)}) collective-permute-start(bf16[32,8,256]{2,1,0:T(8,128)(2,1)S(1)} %collective-permute-done.4.refs_11_), channel_id=1, source_target_pairs={{0,1},{1,0},{2,3},{3,2},{4,5},{5,4},{6,7},{7,6},{8,9},{9,8},{10,11... | collective-permute-start | bytes 393224 | tf_op jit(solution)/shard_map/ppermute | solution.py:25
  29.0 1.3 %collective-permute-start.13 = (bf16[32,8,256]{2,1,0:T(8,128)(2,1)S(1)}, bf16[32,8,256]{2,1,0:T(8,128)(2,1)S(1)}, u32[]{:S(2)}, u32[]{:S(2)}) collective-permute-start(bf16[32,8,256]{2,1,0:T(8,128)(2,1)S(1)} %collective-permute-done.7.refs_13_), channel_id=1, source_target_pairs={{0,1},{1,0},{2,3},{3,2},{4,5},{5,4},{6,7},{7,6},{8,9},{9,8},{10,11... | collective-permute-start | bytes 393224 | tf_op jit(solution)/shard_map/ppermute | solution.py:25
  29.2 1.3 %collective-permute-start.8 = (bf16[32,8,256]{2,1,0:T(8,128)(2,1)S(1)}, bf16[32,8,256]{2,1,0:T(8,128)(2,1)S(1)}, u32[]{:S(2)}, u32[]{:S(2)}) collective-permute-start(bf16[32,8,256]{2,1,0:T(8,128)(2,1)S(1)} %copy-done.3), channel_id=1, source_target_pairs={{0,1},{1,0},{2,3},{3,2},{4,5},{5,4},{6,7},{7,6},{8,9},{9,8},{10,11... | collective-permute-start | bytes 393224 | tf_op jit(solution)/shard_map/ppermute | solution.py:25
  29.5 1.3 %collective-permute-start.9 = (bf16[32,8,256]{2,1,0:T(8,128)(2,1)S(1)}, bf16[32,8,256]{2,1,0:T(8,128)(2,1)S(1)}, u32[]{:S(2)}, u32[]{:S(2)}) collective-permute-start(bf16[32,8,256]{2,1,0:T(8,128)(2,1)S(1)} %collective-permute-done.5.refs_5_), channel_id=1, source_target_pairs={{0,1},{1,0},{2,3},{3,2},{4,5},{5,4},{6,7},{7,6},{8,9},{9,8},{10,11... | collective-permute-start | bytes 393224 | tf_op jit(solution)/shard_map/ppermute | solution.py:25
  30.9 8.9 %collective-permute-start.20 = (bf16[64,16,128]{2,1,0:T(8,128)(2,1)S(1)}, bf16[64,16,128]{2,1,0:T(8,128)(2,1)S(1)}, u32[]{:S(2)}, u32[]{:S(2)}) collective-permute-start(bf16[64,16,128]{2,1,0:T(8,128)(2,1)S(1)} %slice.21), channel_id=1, source_target_pairs={{0,2},{1,3},{2,0},{3,1},{4,6},{5,7},{6,4},{7,5},{8,10},{9,11},{10,... | collective-permute-start | bytes 786440 | tf_op jit(solution)/shard_map/ppermute | solution.py:25
  37.7 12.2 %copy-start.5 = (s32[4,4096]{1,0:T(4,128)S(1)}, s32[4,4096]{1,0:T(4,128)}, u32[]{:S(2)}) copy-start(s32[4,4096]{1,0:T(4,128)} %refs_8_.1) | copy-start | bytes 196612
  37.7 12.2 %copy-start.6 = (f32[4,4096]{1,0:T(4,128)S(1)}, f32[4,4096]{1,0:T(4,128)}, u32[]{:S(2)}) copy-start(f32[4,4096]{1,0:T(4,128)} %refs_9_.1) | copy-start | bytes 196612
  37.7 12.2 %copy-start.7 = (s32[4096]{0:T(1024)S(1)}, s32[4096]{0:T(1024)}, u32[]{:S(2)}) copy-start(s32[4096]{0:T(1024)} %param.21) | copy-start | bytes 49156
  37.7 7.1 %collective-permute-start.16 = (f32[32,16,128]{2,1,0:T(8,128)S(1)}, f32[32,16,128]{2,1,0:T(8,128)S(1)}, u32[]{:S(2)}, u32[]{:S(2)}) collective-permute-start(f32[32,16,128]{2,1,0:T(8,128)S(1)} %get-tuple-element.92), channel_id=1, source_target_pairs={{0,1},{1,0},{2,3},{3,2},{4,5},{5,4},{6,7},{7,6},{8,9},{9,8},{10,11... | collective-permute-start | bytes 786440 | tf_op jit(solution)/shard_map/ppermute | solution.py:25
  37.8 7.6 %collective-permute-start.15 = (f32[32,16,128]{2,1,0:T(8,128)S(1)}, f32[32,16,128]{2,1,0:T(8,128)S(1)}, u32[]{:S(2)}, u32[]{:S(2)}) collective-permute-start(f32[32,16,128]{2,1,0:T(8,128)S(1)} %get-tuple-element.90), channel_id=1, source_target_pairs={{0,1},{1,0},{2,3},{3,2},{4,5},{5,4},{6,7},{7,6},{8,9},{9,8},{10,11... | collective-permute-start | bytes 786440 | tf_op jit(solution)/shard_map/ppermute | solution.py:25
  38.3 7.1 %collective-permute-start.19 = (bf16[32,16,128]{2,1,0:T(8,128)(2,1)S(1)}, bf16[32,16,128]{2,1,0:T(8,128)(2,1)S(1)}, u32[]{:S(2)}, u32[]{:S(2)}) collective-permute-start(bf16[32,16,128]{2,1,0:T(8,128)(2,1)S(1)} %slice.18), channel_id=1, source_target_pairs={{0,2},{1,3},{2,0},{3,1},{4,6},{5,7},{6,4},{7,5},{8,10},{9,11},{10,... | collective-permute-start | bytes 393224 | tf_op jit(solution)/shard_map/ppermute | solution.py:25
  39.9 8.2 %collective-permute-start.21 = (bf16[32,16,128]{2,1,0:T(8,128)(2,1)S(1)}, bf16[32,16,128]{2,1,0:T(8,128)(2,1)S(1)}, u32[]{:S(2)}, u32[]{:S(2)}) collective-permute-start(bf16[32,16,128]{2,1,0:T(8,128)(2,1)S(1)} %get-tuple-element.100), channel_id=1, source_target_pairs={{0,4},{1,5},{2,6},{3,7},{4,8},{5,9},{6,10},{7,11},{8,12},{9,13},{1... | collective-permute-start | bytes 393224 | tf_op jit(solution)/shard_map/ppermute | solution.py:25
  40.0 8.2 %collective-permute-start.22 = (bf16[32,16,128]{2,1,0:T(8,128)(2,1)S(1)}, bf16[32,16,128]{2,1,0:T(8,128)(2,1)S(1)}, u32[]{:S(2)}, u32[]{:S(2)}) collective-permute-start(bf16[32,16,128]{2,1,0:T(8,128)(2,1)S(1)} %get-tuple-element.99), channel_id=1, source_target_pairs={{0,28},{1,29},{2,30},{3,31},{4,0},{5,1},{6,2},{7,3},{8,4},{9,5},{1... | collective-permute-start | bytes 393224 | tf_op jit(solution)/shard_map/ppermute | solution.py:25
  44.8 5.0 %collective-permute-start.17 = (bf16[32,16,128]{2,1,0:T(8,128)(2,1)S(1)}, bf16[32,16,128]{2,1,0:T(8,128)(2,1)S(1)}, u32[]{:S(2)}, u32[]{:S(2)}) collective-permute-start(bf16[32,16,128]{2,1,0:T(8,128)(2,1)S(1)} %add_convert_fusion.1), channel_id=1, source_target_pairs={{0,2},{1,3},{2,0},{3,1},{4,6},{5,7},{6,4},{7,5},{8,10},{9,11},{10,... | collective-permute-start | bytes 393224 | tf_op jit(solution)/shard_map/ppermute | solution.py:25

commit v3 on v2

--- a/solution.py
+++ b/solution.py
@@ -9,10 +9,10 @@
 
 PAR_DEV = 128
 AXES = ("clus", "sub")
-FAR_UNROLL = 16
-NEAR_UNROLL = 4
+FAR_UNROLL = 128
+NEAR_UNROLL = 32
 VMEM_BYTES = 40 * 1024 * 1024
-LOAD_BYTES = 40 * 1024 * 1024
+LOAD_BYTES = 46 * 1024 * 1024
 
 
 def moved(x, by, mask):
@@ -33,34 +33,33 @@
 
 def block_kernel(transposed, total, members, *refs):
     tables_in = refs[:3]
-    halves = 1 if transposed else 3
-    pieces = refs[3 : 3 + halves * members]
-    first, second, near = refs[3 + halves * members : 6 + halves * members]
-    outs = refs[6 + halves * members : 6 + halves * members + members]
-    lhs, coeffs, far_ids, ranks, near_ids, sems = refs[6 + halves * members + members :]
+    pieces = refs[3 : 3 + members]
+    first, second, near = refs[3 + members : 6 + members]
+    outs = refs[6 + members : 6 + 2 * members]
+    lhs, coeffs, far_ids, ranks, near_ids, sems = refs[6 + 2 * members :]
     tables = (far_ids, ranks, near_ids)
     copies = [pltpu.make_async_copy(a, b, sems.at[i]) for i, (a, b) in enumerate(zip(tables_in, tables))]
     for copy in copies:
         copy.start()
-    clusters, height, _ = pieces[0].shape
+    field_clusters, height, _ = pieces[0].shape
+    clusters = field_clusters if transposed else field_clusters // 3
     far, _, rank, width = first.shape
     near_total = near.shape[0]
     rows = lhs.shape[1]
     part = 2 * height
     for out in outs:
         out[...] = jnp.zeros_like(out)
-    for g in range(halves):
-
-        @pl.loop(0, clusters, unroll=2)
-        def _(c):
-            left, right = [], []
-            for piece in pieces[g * members : (g + 1) * members]:
-                x = piece[c].astype(jnp.float32)
-                re, im = x[:, :width], x[:, width:]
-                left += [re, im]
-                right += [-im, re]
-            both = [jnp.concatenate(left, axis=0), jnp.concatenate(right, axis=0)]
-            lhs[g * clusters + c] = jnp.concatenate(both, axis=1).astype(jnp.bfloat16)
+
+    @pl.loop(0, field_clusters, unroll=4)
+    def _(c):
+        left, right = [], []
+        for piece in pieces:
+            x = piece[c].astype(jnp.float32)
+            re, im = x[:, :width], x[:, width:]
+            left += [re, im]
+            right += [-im, re]
+        both = [jnp.concatenate(left, axis=0), jnp.concatenate(right, axis=0)]
+        lhs[c] = jnp.concatenate(both, axis=1).astype(jnp.bfloat16)
 
     for copy in copies:
         copy.wait()
@@ -125,9 +124,8 @@
 
 
 def apply_blocks(transposed, total, members, far_ids, ranks, near_ids, pieces, first, second, near):
-    clusters, height, double = pieces[0].shape
-    halves = len(pieces) // members
-    out_clusters = 3 * clusters if transposed else clusters
+    field_clusters, height, double = pieces[0].shape
+    out_clusters = 3 * field_clusters if transposed else field_clusters // 3
     rows = members * 2 * height
     rank, width = first.shape[2:]
     anywhere = pl.BlockSpec(memory_space=pl.ANY)
@@ -142,7 +140,7 @@
             jax.ShapeDtypeStruct((out_clusters, 2 * height, width), jnp.float32)
         ] * members,
         scratch_shapes=[
-            pltpu.VMEM((halves * clusters, rows, double), jnp.bfloat16),
+            pltpu.VMEM((field_clusters, rows, double), jnp.bfloat16),
             pltpu.VMEM((min(FAR_UNROLL, first.shape[0]), rows, 2 * rank), jnp.bfloat16),
             *[pltpu.SMEM(t.shape, t.dtype) for t in tables],
             pltpu.SemaphoreType.DMA((len(tables),)),
@@ -180,20 +178,50 @@
     )(*arrays)
 
 
+def table_kernel(params, weights, counts, spread, places):
+    slots, panels = params.shape
+    high, width = spread.shape[0], places.shape[0]
+    shift = width.bit_length() - 1
+    high_ids = lax.broadcasted_iota(jnp.int32, (high, width), 0)
+    low_ids = lax.broadcasted_iota(jnp.int32, (width, width), 0)
+    slot_ids = lax.broadcasted_iota(jnp.int32, (slots, width), 0)
+    for c in range(panels // width):
+        at = slice(c * width, (c + 1) * width)
+        value = jnp.where(slot_ids < counts[:, at], weights[:, at], 0.0)
+        ids = params[:, at]
+        high_of, low_of = ids >> shift, ids & (width - 1)
+        for m in range(slots):
+            row = slice(m, m + 1)
+            to = slice((c * slots + m) * width, (c * slots + m + 1) * width)
+            spread[:, to] = jnp.where(high_ids == high_of[row], value[row], 0.0)
+            places[:, to] = jnp.where(low_ids == low_of[row], 1.0, 0.0).astype(jnp.bfloat16)
+
+
+def gradient_tables(params, weights, counts, high, width):
+    vmem = pl.BlockSpec(memory_space=pltpu.VMEM)
+    entries = params.size
+    return pl.pallas_call(
+        table_kernel,
+        in_specs=[vmem] * 3,
+        out_specs=[vmem] * 2,
+        out_shape=[
+            jax.ShapeDtypeStruct((high, entries), jnp.float32),
+            jax.ShapeDtypeStruct((width, entries), jnp.bfloat16),
+        ],
+        compiler_params=pltpu.CompilerParams(vmem_limit_bytes=VMEM_BYTES),
+        cost_estimate=pl.CostEstimate(flops=0, bytes_accessed=8_000_000, transcendentals=0),
+    )(params, weights, counts)
+
+
 def final_kernel(column_total, n_fwd, n_adj, *refs):
     fwd_terms = refs[:n_fwd]
     adj_terms = refs[n_fwd : n_fwd + n_adj]
-    params, weights, counts = refs[n_fwd + n_adj : n_fwd + n_adj + 3]
-    fwd_out, adj_out, grad = refs[n_fwd + n_adj + 3 :]
+    spread, places, fwd_out, adj_out, grad, scaled = refs[n_fwd + n_adj :]
     clusters, height, _ = fwd_out.shape
-    slots = params.shape[0]
     high, width = grad.shape
-    high_ids = lax.broadcasted_iota(jnp.int32, (high, width), 0)
-    low_ids = lax.broadcasted_iota(jnp.int32, (width, width), 0)
-    shift = width.bit_length() - 1
-    grad[...] = jnp.zeros_like(grad)
-
-    def panels(c):
+    entries = spread.shape[1] // clusters
+    slots = entries // width
+    for c in range(clusters):
         fwd = sum(t[c].astype(jnp.float32) for t in fwd_terms)
         adj = sum(t[c].astype(jnp.float32) for t in adj_terms)
         for out, value in ((fwd_out, fwd), (adj_out, adj)):
@@ -201,39 +229,20 @@
             out[c, :, width:] = value[height:]
         product = fwd * adj
         sens = jnp.sum(product[:height] - product[height:], axis=0, keepdims=True) / column_total
-        at = pl.ds(pl.multiple_of(c * width, width), width)
-        slot_ids = lax.broadcasted_iota(jnp.int32, (slots, width), 0)
-        value = jnp.where(slot_ids < counts[:, at], weights[:, at] * sens, 0.0)
-        ids = params[:, at]
-        high_of, low_of = ids >> shift, ids & (width - 1)
-        top = value.astype(jnp.bfloat16).astype(jnp.float32)
-        rest = value - top
-        middle = rest.astype(jnp.bfloat16).astype(jnp.float32)
-        terms = (top, middle, rest - middle)
-        spread, places = [], []
-        for m in range(slots):
-            row = slice(m, m + 1)
-            hit = high_ids == high_of[row]
-            spread.append(
-                jnp.concatenate([jnp.where(hit, t[row], 0.0) for t in terms], axis=0).astype(jnp.bfloat16)
-            )
-            places.append(jnp.where(low_ids == low_of[row], 1.0, 0.0).astype(jnp.bfloat16))
-        got = lax.dot_general(
-            jnp.concatenate(spread, axis=1),
-            jnp.concatenate(places, axis=1),
-            (((1,), (1,)), ((), ())),
-            preferred_element_type=jnp.float32,
-        )
-        grad[...] += sum(got[k * high : (k + 1) * high] for k in range(len(terms)))
-
-    @pl.loop(0, clusters, unroll=4)
-    def _(c):
-        panels(c)
-
-
-def finish(column_total, fwd_terms, adj_terms, params, weights, counts, high):
+        at = slice(c * entries, (c + 1) * entries)
+        value = spread[:, at] * jnp.concatenate([sens] * slots, axis=1)
+        top = value.astype(jnp.bfloat16)
+        scaled[:high, at] = top
+        scaled[high:, at] = (value - top.astype(jnp.float32)).astype(jnp.bfloat16)
+    got = lax.dot_general(
+        scaled[...], places[...], (((1,), (1,)), ((), ())), preferred_element_type=jnp.float32
+    )
+    grad[...] = got[:high] + got[high:]
+
+
+def finish(column_total, fwd_terms, adj_terms, spread, places):
     clusters, part, width = fwd_terms[0].shape
-    vmem = pl.BlockSpec(memory_space=pltpu.VMEM)
+    high = spread.shape[0]
     first_clusters = pl.BlockSpec((clusters, part, width), lambda i: (0, 0, 0))
     field = jax.ShapeDtypeStruct((clusters, part // 2, 2 * width), jnp.float32)
     whole = lambda shape: pl.BlockSpec(shape, lambda i: (0,) * len(shape))
@@ -242,12 +251,13 @@
         functools.partial(final_kernel, column_total, len(fwd_terms), len(adj_terms)),
         grid=(1,),
         in_specs=[first_clusters] * len(terms)
-        + [whole(params.shape), whole(weights.shape), whole(counts.shape)],
+        + [pl.BlockSpec(memory_space=pltpu.VMEM)] * 2,
         out_specs=[whole(field.shape), whole(field.shape), whole((high, width))],
         out_shape=[field, field, jax.ShapeDtypeStruct((high, width), jnp.float32)],
+        scratch_shapes=[pltpu.VMEM((2 * high, spread.shape[1]), jnp.bfloat16)],
         compiler_params=pltpu.CompilerParams(vmem_limit_bytes=VMEM_BYTES),
         cost_estimate=pl.CostEstimate(flops=200_000_000, bytes_accessed=3_000_000, transcendentals=0),
-    )(*terms, params, weights, counts)
+    )(*terms, spread, places)
 
 
 def shards(
@@ -281,13 +291,16 @@
 
     tie = lax.optimization_barrier
     w_mine = across(adjoint_rhs)
-    x_next, x_prev = moved(forward_rhs, -1, 0), moved(forward_rhs, 1, 0)
-    factors = loaded(far_left, far_right, near_blocks)
-    w_mine, factors = tie((w_mine, factors))
-    left, right, near = factors
+    x_prev = moved(forward_rhs, 1, 0)
+    x_next = moved(forward_rhs, -1, 0)
+    left, right, near, w_mine[0] = loaded(far_left, far_right, near_blocks, adjoint_rhs)
+    x_own = across(forward_rhs)
+    w_mine, x_own, left, right, near = tie((w_mine, x_own, left, right, near))
     w_pieces = both_cores(w_mine)
-    w_pieces, x_next, x_prev = tie((w_pieces, x_next, x_prev))
-    x_mine = [*across(forward_rhs), *across(x_next), *across(x_prev)]
+    x_near = jnp.concatenate([x_next, x_prev], axis=0)
+    w_pieces, x_near = tie((w_pieces, x_near))
+    x_near = across(x_near)
+    x_mine = [jnp.concatenate(pair, axis=0) for pair in zip(x_own, x_near)]
 
     apply = functools.partial(
         apply_blocks, total=total, members=members, far_ids=far_clusters, ranks=far_ranks, near_ids=near_clusters
@@ -303,12 +316,18 @@
     sides = [moved(away[m][clusters:], 0, m) for m in away]
     own = [moved(away[m][:clusters], 0, m) for m in away]
     fwd_parts = apply(False, pieces=x_pieces, first=right, second=left, near=near)
+    fwd_parts, sides = tie((fwd_parts, sides))
     fwd_core = [moved(fwd_parts[m + 1], 0, 1) for m in evens]
 
     side = adj_parts[0][clusters:] + adj_core[0][clusters:]
     for s in sides:
         side = side + s.astype(jnp.float32)
     side = side.astype(jnp.bfloat16)
+    panel_params, side = tie((panel_params, side))
+    spread, places = gradient_tables(
+        panel_params, panel_weights, panel_counts[None, :],
+        PAR_DEV * groups * members // near_blocks.shape[-1], near_blocks.shape[-1],
+    )
     ring = [moved(side[:clusters], 1, 0), moved(side[clusters:], -1, 0)]
     adj_terms = [adj_parts[0], adj_core[0], *own, *ring]
 
@@ -318,11 +337,8 @@
             fwd_terms.append(moved((fwd_parts[m] + fwd_core[k]).astype(jnp.bfloat16), 0, m))
 
     devices = groups * members
-    forward_field, adjoint_field, spread = finish(
-        column_total, fwd_terms, adj_terms, panel_params, panel_weights, panel_counts[None, :],
-        PAR_DEV * devices // near_blocks.shape[-1],
-    )
-    pieces = lax.all_to_all(spread.reshape(devices, PAR_DEV), AXES, 0, 0, tiled=True)
+    forward_field, adjoint_field, grad = finish(column_total, fwd_terms, adj_terms, spread, places)
+    pieces = lax.all_to_all(grad.reshape(devices, PAR_DEV), AXES, 0, 0, tiled=True)
     return forward_field, adjoint_field, jnp.sum(pieces, axis=0)
 
 

time: 64 us -> 61.4 us (0.959)
  waiting for transfers between devices: 10.9 us -> 15.2 us
  local copies, waits for them, and re-layouts: 5.16 us -> 0.99 us
  Pallas kernels: 15.5 us -> 12.9 us
    pallas_call x2, Pallas kernels: 11.9 us -> 6.51 us  [apply_blocks(): pl.pallas_call(functools.partial(block_kernel, transposed, total, members...]
    ppermute x23 -> x18, waiting for transfers between devices: 10.9 us -> 15.2 us  [moved(): return lax.ppermute(x, AXES, pairs)]
    unnamed x22 -> x16, local copies, waits for them, and re-layouts: 5.11 us -> 0.94 us
    pallas_call x1, Pallas kernels: 0.56 us -> 2.96 us  [loaded(): pl.pallas_call(functools.partial(load_kernel, parts), in_specs=[pl.BlockS...]
    pallas_call x0 -> x1, Pallas kernels: none -> 1.27 us  [gradient_tables(): pl.pallas_call(table_kernel, in_specs=[vmem] * 3, out_specs=[vmem] * 2, o...]
    pallas_call x1, Pallas kernels: 3.11 us -> 2.11 us  [finish(): pl.pallas_call(functools.partial(final_kernel, column_total, len(fwd_term...]
    ppermute x23 -> x18, starting transfers between devices: 20.4 us -> 19.8 us  [moved(): return lax.ppermute(x, AXES, pairs)]
  transfers between devices with their start and end apart: 23 -> 18, of which waited for: 8 -> 9; matrix products, arithmetic and copies ran while one was open for 0% -> 1% of each run, Pallas kernels for 20% -> 18%
where the time goes in v3:
time: 61.4 us; the launch traced here: 61.2 us
  starting transfers between devices  19.8 us (32%)
  waiting for transfers between devices  15.2 us (25%)
  Pallas kernels  12.9 us (21%)
  blocking collectives  10.6 us (17%)
  local copies, waits for them, and re-layouts  0.99 us (2%)
  other arithmetic  0.9 us (1%)
  between operations  0.83 us (1%)
    ppermute x18, starting transfers between devices, moved(): return lax.ppermute(x, AXES, pairs)  19.8 us
    ppermute x18, waiting for transfers between devices, moved(): return lax.ppermute(x, AXES, pairs)  15.2 us
    all_to_all x1, blocking collectives, shards(): lax.all_to_all(grad.reshape(devices, PAR_DEV), AXES, 0, 0, tiled=True)  10.6 us
    pallas_call x2, Pallas kernels, apply_blocks(): pl.pallas_call(functools.partial(block_kernel, transposed, total, members...  6.51 us
    pallas_call x1, Pallas kernels, loaded(): pl.pallas_call(functools.partial(load_kernel, parts), in_specs=[pl.BlockS...  2.96 us
    pallas_call x1, Pallas kernels, finish(): pl.pallas_call(functools.partial(final_kernel, column_total, len(fwd_term...  2.11 us
    pallas_call x1, Pallas kernels, gradient_tables(): pl.pallas_call(table_kernel, in_specs=[vmem] * 3, out_specs=[vmem] * 2, o...  1.27 us
  transfers between devices with their start and end apart: 18, of which 9 were waited for; matrix products, arithmetic and copies ran while one was open for 1% of the time, Pallas kernels for 18%

profile of v3, /device:TPU:0, one launch (start us, length us, event | category | flops | bytes accessed | tf_op | source)
XLA Modules:
  0.0 61.2 jit_solution(17755291587683626049)
XLA Ops:
  0.6 3.0 %collective-permute-start = (bf16[32,8,256]{2,1,0:T(8,128)(2,1)}, bf16[32,8,256]{2,1,0:T(8,128)(2,1)S(1)}, u32[]{:S(2)}, u32[]{:S(2)}) collective-permute-start(bf16[32,8,256]{2,1,0:T(8,128)(2,1)} %refs_3_.1), channel_id=1, source_target_pairs={{0,2},{1,3},{2,0},{3,1},{4,6},{5,7},{6,4},{7,5},{8,10},{9,11},{10,... | collective-permute-start | bytes 393224 | tf_op jit(solution)/shard_map/ppermute | solution.py:25
  3.7 0.1 collective-permute-start.1
  3.7 5.0 %collective-permute-start.4 = (bf16[32,8,256]{2,1,0:T(8,128)(2,1)}, bf16[32,8,256]{2,1,0:T(8,128)(2,1)S(1)}, u32[]{:S(2)}, u32[]{:S(2)}) collective-permute-start(bf16[32,8,256]{2,1,0:T(8,128)(2,1)} %param.11), channel_id=1, source_target_pairs={{0,28},{1,29},{2,30},{3,31},{4,0},{5,1},{6,2},{7,3},{8,4},{9,5},{1... | collective-permute-start | bytes 393224 | tf_op jit(solution)/shard_map/ppermute | solution.py:25
  8.7 0.0 collective-permute-start.5
  8.7 0.0 copy-start
  8.7 0.9 %copy-done = bf16[32,8,256]{2,1,0:T(8,128)(2,1)S(1)} copy-done((bf16[32,8,256]{2,1,0:T(8,128)(2,1)S(1)}, bf16[32,8,256]{2,1,0:T(8,128)(2,1)}, u32[]{:S(2)}) %copy-start) | copy-done | bytes 131096
  9.6 0.0 copy-start.4
  9.6 0.0 copy-start.5
  9.6 0.0 copy-start.6
  9.6 3.0 %shard_map.130 = (bf16[128,2,32,128]{3,2,1,0:T(8,128)(2,1)S(1)}, bf16[128,2,32,128]{3,2,1,0:T(8,128)(2,1)S(1)}, bf16[32,2,128,128]{3,2,1,0:T(8,128)(2,1)S(1)}, bf16[32,8,256]{2,1,0:T(8,128)(2,1)S(1)}) custom-call(bf16[128,2,32,128]{3,2,1,0:T(8,128)(2,1)} %refs_0_.3, bf16[128,2,32,128]{3,2,1,0:T(8,128)(2,1)} %refs_1_.3, bf16[32,2,128,128]{3,2,1,0:T(8,128)(2,1)} %refs_2_.3, ...), custom_call_target="tpu_custom_call" | custom-call | bytes 12000000 | tf_op jit(solution)/shard_map/pallas_call | solution.py:170
  12.6 0.0 collective-permute-done.refs_5_
  12.6 0.0 collective-permute-done.1
  12.6 0.1 collective-permute-start.2
  12.7 0.5 collective-permute-start.3
  13.2 0.0 collective-permute-done.4
  13.2 3.4 %collective-permute-done.5 = bf16[32,8,256]{2,1,0:T(8,128)(2,1)S(1)} collective-permute-done((bf16[32,8,256]{2,1,0:T(8,128)(2,1)}, bf16[32,8,256]{2,1,0:T(8,128)(2,1)S(1)}, u32[]{:S(2)}, u32[]{:S(2)}) %collective-permute-start.5) | collective-permute-done | bytes 131104 | tf_op jit(solution)/shard_map/ppermute | solution.py:25
  16.6 0.0 copy-start.7
  16.6 0.0 collective-permute-done.2.refs_4_
  16.6 0.0 collective-permute-done.3.refs_6_
  16.6 1.6 %collective-permute-start.6 = (bf16[64,8,256]{2,1,0:T(8,128)(2,1)S(1)}, bf16[64,8,256]{2,1,0:T(8,128)(2,1)S(1)}, u32[]{:S(2)}, u32[]{:S(2)}) collective-permute-start(bf16[64,8,256]{2,1,0:T(8,128)(2,1)S(1)} %pad_maximum_fusion.2), channel_id=1, source_target_pairs={{0,2},{1,3},{2,0},{3,1},{4,6},{5,7},{6,4},{7,5},{8,10},{9,11},{10,... | collective-permute-start | bytes 786440 | tf_op jit(solution)/shard_map/ppermute | solution.py:25
  18.2 0.0 copy-done.4
  18.2 0.0 copy-done.5
  18.2 0.0 copy-done.6
  18.2 3.3 %shard_map.131 = (f32[96,16,128]{2,1,0:T(8,128)S(1)}, f32[96,16,128]{2,1,0:T(8,128)S(1)}, f32[96,16,128]{2,1,0:T(8,128)S(1)}, f32[96,16,128]{2,1,0:T(8,128)S(1)}) custom-call(s32[2,128]{1,0:T(2,128)S(1)} %copy-done.4, s32[128]{0:T(128)S(1)} %copy-done.6, s32[2,32]{1,0:T(2,128)S(1)} %copy-done.5, bf16[32,8,256]{2,1,0:T(8,128)(2,1)S(1)} %get-tuple-element.56.refs_3_, ...), custom_call_target="tpu_custom_call" | custom-call | flops 671088640 | bytes 20000000 | tf_op jit(solution)/shard_map/pallas_call | solution.py:135
  21.6 0.0 copy-done.7
  21.6 1.5 %collective-permute-done.6 = bf16[64,8,256]{2,1,0:T(8,128)(2,1)S(1)} collective-permute-done((bf16[64,8,256]{2,1,0:T(8,128)(2,1)S(1)}, bf16[64,8,256]{2,1,0:T(8,128)(2,1)S(1)}, u32[]{:S(2)}, u32[]{:S(2)}) %collective-permute-start.6) | collective-permute-done | bytes 262176 | tf_op jit(solution)/shard_map/ppermute | solution.py:25
  23.1 0.1 collective-permute-start.9
  23.2 0.5 collective-permute-start.14
  23.7 0.1 collective-permute-start.7
  23.8 0.4 collective-permute-start.8
  24.2 1.3 %collective-permute-done.9 = f32[96,16,128]{2,1,0:T(8,128)S(1)} collective-permute-done((f32[96,16,128]{2,1,0:T(8,128)S(1)}, f32[96,16,128]{2,1,0:T(8,128)S(1)}, u32[]{:S(2)}, u32[]{:S(2)}) %collective-permute-start.9) | collective-permute-done | bytes 786464 | tf_op jit(solution)/shard_map/ppermute | solution.py:25
  25.5 0.1 add_convert_fusion
  25.6 1.6 %collective-permute-done.7.refs_4_ = bf16[96,8,256]{2,1,0:T(8,128)(2,1)S(1)} collective-permute-done((bf16[96,8,256]{2,1,0:T(8,128)(2,1)S(1)}, bf16[96,8,256]{2,1,0:T(8,128)(2,1)S(1)}, u32[]{:S(2)}, u32[]{:S(2)}) %collective-permute-start.7) | collective-permute-done | bytes 393248 | tf_op jit(solution)/shard_map/ppermute | solution.py:25
  27.2 0.6 collective-permute-done.8.refs_6_
  27.7 1.6 %collective-permute-start.10 = (bf16[64,16,128]{2,1,0:T(8,128)(2,1)S(1)}, bf16[64,16,128]{2,1,0:T(8,128)(2,1)S(1)}, u32[]{:S(2)}, u32[]{:S(2)}) collective-permute-start(bf16[64,16,128]{2,1,0:T(8,128)(2,1)S(1)} %slice.18), channel_id=1, source_target_pairs={{0,2},{1,3},{2,0},{3,1},{4,6},{5,7},{6,4},{7,5},{8,10},{9,11},{10,... | collective-permute-start | bytes 786440 | tf_op jit(solution)/shard_map/ppermute | solution.py:25
  29.3 0.6 collective-permute-start.15
  29.9 3.2 %shard_map.132 = (f32[32,16,128]{2,1,0:T(8,128)S(1)}, f32[32,16,128]{2,1,0:T(8,128)S(1)}, f32[32,16,128]{2,1,0:T(8,128)S(1)}, f32[32,16,128]{2,1,0:T(8,128)S(1)}) custom-call(s32[2,128]{1,0:T(2,128)S(1)} %copy-done.4, s32[128]{0:T(128)S(1)} %copy-done.6, s32[2,32]{1,0:T(2,128)S(1)} %copy-done.5, bf16[96,8,256]{2,1,0:T(8,128)(2,1)S(1)} %pad_maximum_fusion.refs_3_, ...), custom_call_target="tpu_custom_call" | custom-call | flops 671088640 | bytes 20000000 | tf_op jit(solution)/shard_map/pallas_call | solution.py:135
  33.1 0.0 copy-start.1
  33.1 0.0 copy-start.2
  33.1 0.0 copy-start.3
  33.2 3.8 %collective-permute-done.10 = bf16[64,16,128]{2,1,0:T(8,128)(2,1)S(1)} collective-permute-done((bf16[64,16,128]{2,1,0:T(8,128)(2,1)S(1)}, bf16[64,16,128]{2,1,0:T(8,128)(2,1)S(1)}, u32[]{:S(2)}, u32[]{:S(2)}) %collective-permute-start.10) | collective-permute-done | bytes 262176 | tf_op jit(solution)/shard_map/ppermute | solution.py:25
  37.0 0.0 collective-permute-start.12
  37.0 0.0 collective-permute-done.14.refs_4_
  37.0 0.1 fusion.1
  37.1 0.1 collective-permute-start.16
  37.2 4.7 %collective-permute-start.17 = (bf16[32,16,128]{2,1,0:T(8,128)(2,1)S(1)}, bf16[32,16,128]{2,1,0:T(8,128)(2,1)S(1)}, u32[]{:S(2)}, u32[]{:S(2)}) collective-permute-start(bf16[32,16,128]{2,1,0:T(8,128)(2,1)S(1)} %get-tuple-element.97), channel_id=1, source_target_pairs={{0,28},{1,29},{2,30},{3,31},{4,0},{5,1},{6,2},{7,3},{8,4},{9,5},{1... | collective-permute-start | bytes 393224 | tf_op jit(solution)/shard_map/ppermute | solution.py:25
  41.9 0.0 collective-permute-start.11
  41.9 0.0 collective-permute-done.12
  41.9 1.6 %collective-permute-start.13 = (bf16[32,16,128]{2,1,0:T(8,128)(2,1)S(1)}, bf16[32,16,128]{2,1,0:T(8,128)(2,1)S(1)}, u32[]{:S(2)}, u32[]{:S(2)}) collective-permute-start(bf16[32,16,128]{2,1,0:T(8,128)(2,1)S(1)} %add_convert_fusion.1), channel_id=1, source_target_pairs={{0,2},{1,3},{2,0},{3,1},{4,6},{5,7},{6,4},{7,5},{8,10},{9,11},{10,... | collective-permute-start | bytes 393224 | tf_op jit(solution)/shard_map/ppermute | solution.py:25
  43.5 0.0 copy-done.1
  43.5 0.0 copy-done.2
  43.5 0.0 copy-done.3
  43.5 1.3 %shard_map.133 = (f32[32,16384]{1,0:T(8,128)S(1)}, bf16[128,16384]{1,0:T(8,128)(2,1)S(1)}) custom-call(s32[4,4096]{1,0:T(4,128)S(1)} %copy-done.1, f32[4,4096]{1,0:T(4,128)S(1)} %copy-done.2, s32[1,4096]{1,0:T(1,128)S(1)} %bitcast.4), custom_call_target="tpu_custom_call" | custom-call | bytes 8000000 | tf_op jit(solution)/shard_map/pallas_call | solution.py:203
  44.8 0.0 collective-permute-done.15.refs_5_
  44.8 1.1 %collective-permute-done.16.refs_6_ = bf16[32,16,128]{2,1,0:T(8,128)(2,1)S(1)} collective-permute-done((bf16[32,16,128]{2,1,0:T(8,128)(2,1)S(1)}, bf16[32,16,128]{2,1,0:T(8,128)(2,1)S(1)}, u32[]{:S(2)}, u32[]{:S(2)}) %collective-permute-start.16) | collective-permute-done | bytes 131104 | tf_op jit(solution)/shard_map/ppermute | solution.py:25
  45.9 0.1 collective-permute-done.17.refs_7_
  45.9 0.0 collective-permute-done.11.refs_1_
  45.9 2.0 %collective-permute-done.13.refs_2_ = bf16[32,16,128]{2,1,0:T(8,128)(2,1)S(1)} collective-permute-done((bf16[32,16,128]{2,1,0:T(8,128)(2,1)S(1)}, bf16[32,16,128]{2,1,0:T(8,128)(2,1)S(1)}, u32[]{:S(2)}, u32[]{:S(2)}) %collective-permute-start.13) | collective-permute-done | bytes 131104 | tf_op jit(solution)/shard_map/ppermute | solution.py:25
  47.9 2.1 %shard_map.134 = (f32[32,8,256]{2,1,0:T(8,128)}, f32[32,8,256]{2,1,0:T(8,128)}, f32[32,128]{1,0:T(8,128)S(1)}) custom-call(f32[32,16,128]{2,1,0:T(8,128)S(1)} %get-tuple-element.83.refs_0_, f32[32,16,128]{2,1,0:T(8,128)S(1)} %collective-permute-done.11.refs_1_, bf16[32,16,128]{2,1,0:T(8,128)(2,1)S(1)} %collective-permute-done.13.refs_2_, ...), custom_call_target="tpu_custom_call" | custom-call | flops 200000000 | bytes 3000000 | tf_op jit(solution)/shard_map/pallas_call | solution.py:250
  50.0 10.6 %all_to_all.9 = f32[32,1,128]{2,1,0:T(1,128)S(1)} all-to-all(f32[32,1,128]{2,1,0:T(1,128)S(1)} %bitcast.5), channel_id=1, replica_groups=mesh['clus'=8,'sub'=4] {'clus','sub'}, dimensions={0} | all-to-all | bytes 32768 | tf_op jit(solution)/shard_map/all_to_all | solution.py:341
  60.6 0.6 reduce_sum.9
  (7 shorter events, 0.2 us)
Async XLA Ops:
  0.6 11.9 %collective-permute-start = (bf16[32,8,256]{2,1,0:T(8,128)(2,1)}, bf16[32,8,256]{2,1,0:T(8,128)(2,1)S(1)}, u32[]{:S(2)}, u32[]{:S(2)}) collective-permute-start(bf16[32,8,256]{2,1,0:T(8,128)(2,1)} %refs_3_.1), channel_id=1, source_target_pairs={{0,2},{1,3},{2,0},{3,1},{4,6},{5,7},{6,4},{7,5},{8,10},{9,11},{10,... | collective-permute-start | bytes 393224 | tf_op jit(solution)/shard_map/ppermute | solution.py:25
  3.7 8.9 %collective-permute-start.1 = (bf16[32,8,256]{2,1,0:T(8,128)(2,1)}, bf16[32,8,256]{2,1,0:T(8,128)(2,1)S(1)}, u32[]{:S(2)}, u32[]{:S(2)}) collective-permute-start(bf16[32,8,256]{2,1,0:T(8,128)(2,1)} %param.11), channel_id=1, source_target_pairs={{0,2},{1,3},{2,0},{3,1},{4,6},{5,7},{6,4},{7,5},{8,10},{9,11},{10,... | collective-permute-start | bytes 393224 | tf_op jit(solution)/shard_map/ppermute | solution.py:25
  3.7 9.4 %collective-permute-start.4 = (bf16[32,8,256]{2,1,0:T(8,128)(2,1)}, bf16[32,8,256]{2,1,0:T(8,128)(2,1)S(1)}, u32[]{:S(2)}, u32[]{:S(2)}) collective-permute-start(bf16[32,8,256]{2,1,0:T(8,128)(2,1)} %param.11), channel_id=1, source_target_pairs={{0,28},{1,29},{2,30},{3,31},{4,0},{5,1},{6,2},{7,3},{8,4},{9,5},{1... | collective-permute-start | bytes 393224 | tf_op jit(solution)/shard_map/ppermute | solution.py:25
  8.7 7.9 %collective-permute-start.5 = (bf16[32,8,256]{2,1,0:T(8,128)(2,1)}, bf16[32,8,256]{2,1,0:T(8,128)(2,1)S(1)}, u32[]{:S(2)}, u32[]{:S(2)}) collective-permute-start(bf16[32,8,256]{2,1,0:T(8,128)(2,1)} %param.11), channel_id=1, source_target_pairs={{0,4},{1,5},{2,6},{3,7},{4,8},{5,9},{6,10},{7,11},{8,12},{9,13},{1... | collective-permute-start | bytes 393224 | tf_op jit(solution)/shard_map/ppermute | solution.py:25
  8.7 0.9 %copy-start = (bf16[32,8,256]{2,1,0:T(8,128)(2,1)S(1)}, bf16[32,8,256]{2,1,0:T(8,128)(2,1)}, u32[]{:S(2)}) copy-start(bf16[32,8,256]{2,1,0:T(8,128)(2,1)} %refs_3_.1) | copy-start | bytes 393220
  9.6 8.6 %copy-start.4 = (s32[2,128]{1,0:T(2,128)S(1)}, s32[2,128]{1,0:T(2,128)}, u32[]{:S(2)}) copy-start(s32[2,128]{1,0:T(2,128)} %refs_0_.5) | copy-start | bytes 3076
  9.6 8.6 %copy-start.5 = (s32[2,32]{1,0:T(2,128)S(1)}, s32[2,32]{1,0:T(2,128)}, u32[]{:S(2)}) copy-start(s32[2,32]{1,0:T(2,128)} %refs_2_.5) | copy-start | bytes 772
  9.6 8.6 %copy-start.6 = (s32[128]{0:T(128)S(1)}, s32[128]{0:T(128)}, u32[]{:S(2)}) copy-start(s32[128]{0:T(128)} %refs_1_.5) | copy-start | bytes 1540
  12.6 4.0 %collective-permute-start.2 = (bf16[32,8,256]{2,1,0:T(8,128)(2,1)S(1)}, bf16[32,8,256]{2,1,0:T(8,128)(2,1)S(1)}, u32[]{:S(2)}, u32[]{:S(2)}) collective-permute-start(bf16[32,8,256]{2,1,0:T(8,128)(2,1)S(1)} %get-tuple-element.56.refs_3_), channel_id=1, source_target_pairs={{0,1},{1,0},{2,3},{3,2},{4,5},{5,4},{6,7},{7,6},{8,9},{9,8},{10,11... | collective-permute-start | bytes 393224 | tf_op jit(solution)/shard_map/ppermute | solution.py:25
  12.7 4.0 %collective-permute-start.3 = (bf16[32,8,256]{2,1,0:T(8,128)(2,1)S(1)}, bf16[32,8,256]{2,1,0:T(8,128)(2,1)S(1)}, u32[]{:S(2)}, u32[]{:S(2)}) collective-permute-start(bf16[32,8,256]{2,1,0:T(8,128)(2,1)S(1)} %collective-permute-done.refs_5_), channel_id=1, source_target_pairs={{0,1},{1,0},{2,3},{3,2},{4,5},{5,4},{6,7},{7,6},{8,9},{9,8},{10,11... | collective-permute-start | bytes 393224 | tf_op jit(solution)/shard_map/ppermute | solution.py:25
  16.6 5.0 %copy-start.7 = (bf16[32,8,256]{2,1,0:T(8,128)(2,1)S(1)}, bf16[32,8,256]{2,1,0:T(8,128)(2,1)}, u32[]{:S(2)}) copy-start(bf16[32,8,256]{2,1,0:T(8,128)(2,1)} %param.11) | copy-start | bytes 393220
  16.6 6.4 %collective-permute-start.6 = (bf16[64,8,256]{2,1,0:T(8,128)(2,1)S(1)}, bf16[64,8,256]{2,1,0:T(8,128)(2,1)S(1)}, u32[]{:S(2)}, u32[]{:S(2)}) collective-permute-start(bf16[64,8,256]{2,1,0:T(8,128)(2,1)S(1)} %pad_maximum_fusion.2), channel_id=1, source_target_pairs={{0,2},{1,3},{2,0},{3,1},{4,6},{5,7},{6,4},{7,5},{8,10},{9,11},{10,... | collective-permute-start | bytes 786440 | tf_op jit(solution)/shard_map/ppermute | solution.py:25
  23.1 2.4 %collective-permute-start.9 = (f32[96,16,128]{2,1,0:T(8,128)S(1)}, f32[96,16,128]{2,1,0:T(8,128)S(1)}, u32[]{:S(2)}, u32[]{:S(2)}) collective-permute-start(f32[96,16,128]{2,1,0:T(8,128)S(1)} %get-tuple-element.73), channel_id=1, source_target_pairs={{0,1},{1,0},{2,3},{3,2},{4,5},{5,4},{6,7},{7,6},{8,9},{9,8},{10,11... | collective-permute-start | bytes 2359304 | tf_op jit(solution)/shard_map/ppermute | solution.py:25
  23.2 13.8 %collective-permute-start.14 = (f32[96,16,128]{2,1,0:T(8,128)S(1)}, f32[96,16,128]{2,1,0:T(8,128)S(1)}, u32[]{:S(2)}, u32[]{:S(2)}) collective-permute-start(f32[96,16,128]{2,1,0:T(8,128)S(1)} %get-tuple-element.88), channel_id=1, source_target_pairs={{0,1},{1,0},{2,3},{3,2},{4,5},{5,4},{6,7},{7,6},{8,9},{9,8},{10,11... | collective-permute-start | bytes 2359304 | tf_op jit(solution)/shard_map/ppermute | solution.py:25
  23.7 3.5 %collective-permute-start.7 = (bf16[96,8,256]{2,1,0:T(8,128)(2,1)S(1)}, bf16[96,8,256]{2,1,0:T(8,128)(2,1)S(1)}, u32[]{:S(2)}, u32[]{:S(2)}) collective-permute-start(bf16[96,8,256]{2,1,0:T(8,128)(2,1)S(1)} %pad_maximum_fusion.refs_3_), channel_id=1, source_target_pairs={{0,1},{1,0},{2,3},{3,2},{4,5},{5,4},{6,7},{7,6},{8,9},{9,8},{10,11... | collective-permute-start | bytes 1179656 | tf_op jit(solution)/shard_map/ppermute | solution.py:25
  23.8 3.9 %collective-permute-start.8 = (bf16[96,8,256]{2,1,0:T(8,128)(2,1)S(1)}, bf16[96,8,256]{2,1,0:T(8,128)(2,1)S(1)}, u32[]{:S(2)}, u32[]{:S(2)}) collective-permute-start(bf16[96,8,256]{2,1,0:T(8,128)(2,1)S(1)} %pad_maximum_fusion.1.refs_5_), channel_id=1, source_target_pairs={{0,1},{1,0},{2,3},{3,2},{4,5},{5,4},{6,7},{7,6},{8,9},{9,8},{10,11... | collective-permute-start | bytes 1179656 | tf_op jit(solution)/shard_map/ppermute | solution.py:25
  27.7 9.2 %collective-permute-start.10 = (bf16[64,16,128]{2,1,0:T(8,128)(2,1)S(1)}, bf16[64,16,128]{2,1,0:T(8,128)(2,1)S(1)}, u32[]{:S(2)}, u32[]{:S(2)}) collective-permute-start(bf16[64,16,128]{2,1,0:T(8,128)(2,1)S(1)} %slice.18), channel_id=1, source_target_pairs={{0,2},{1,3},{2,0},{3,1},{4,6},{5,7},{6,4},{7,5},{8,10},{9,11},{10,... | collective-permute-start | bytes 786440 | tf_op jit(solution)/shard_map/ppermute | solution.py:25
  29.3 15.5 %collective-permute-start.15 = (bf16[32,16,128]{2,1,0:T(8,128)(2,1)S(1)}, bf16[32,16,128]{2,1,0:T(8,128)(2,1)S(1)}, u32[]{:S(2)}, u32[]{:S(2)}) collective-permute-start(bf16[32,16,128]{2,1,0:T(8,128)(2,1)S(1)} %slice.19), channel_id=1, source_target_pairs={{0,2},{1,3},{2,0},{3,1},{4,6},{5,7},{6,4},{7,5},{8,10},{9,11},{10,... | collective-permute-start | bytes 393224 | tf_op jit(solution)/shard_map/ppermute | solution.py:25
  33.1 10.4 %copy-start.1 = (s32[4,4096]{1,0:T(4,128)S(1)}, s32[4,4096]{1,0:T(4,128)}, u32[]{:S(2)}) copy-start(s32[4,4096]{1,0:T(4,128)} %params) | copy-start | bytes 196612
  33.1 10.4 %copy-start.2 = (f32[4,4096]{1,0:T(4,128)S(1)}, f32[4,4096]{1,0:T(4,128)}, u32[]{:S(2)}) copy-start(f32[4,4096]{1,0:T(4,128)} %weights.1) | copy-start | bytes 196612
  33.1 10.4 %copy-start.3 = (s32[4096]{0:T(1024)S(1)}, s32[4096]{0:T(1024)}, u32[]{:S(2)}) copy-start(s32[4096]{0:T(1024)} %param.21) | copy-start | bytes 49156
  37.0 4.9 %collective-permute-start.12 = (f32[32,16,128]{2,1,0:T(8,128)S(1)}, f32[32,16,128]{2,1,0:T(8,128)S(1)}, u32[]{:S(2)}, u32[]{:S(2)}) collective-permute-start(f32[32,16,128]{2,1,0:T(8,128)S(1)} %get-tuple-element.86), channel_id=1, source_target_pairs={{0,1},{1,0},{2,3},{3,2},{4,5},{5,4},{6,7},{7,6},{8,9},{9,8},{10,11... | collective-permute-start | bytes 786440 | tf_op jit(solution)/shard_map/ppermute | solution.py:25
  37.1 8.8 %collective-permute-start.16 = (bf16[32,16,128]{2,1,0:T(8,128)(2,1)S(1)}, bf16[32,16,128]{2,1,0:T(8,128)(2,1)S(1)}, u32[]{:S(2)}, u32[]{:S(2)}) collective-permute-start(bf16[32,16,128]{2,1,0:T(8,128)(2,1)S(1)} %get-tuple-element.98), channel_id=1, source_target_pairs={{0,4},{1,5},{2,6},{3,7},{4,8},{5,9},{6,10},{7,11},{8,12},{9,13},{1... | collective-permute-start | bytes 393224 | tf_op jit(solution)/shard_map/ppermute | solution.py:25
  37.2 8.8 %collective-permute-start.17 = (bf16[32,16,128]{2,1,0:T(8,128)(2,1)S(1)}, bf16[32,16,128]{2,1,0:T(8,128)(2,1)S(1)}, u32[]{:S(2)}, u32[]{:S(2)}) collective-permute-start(bf16[32,16,128]{2,1,0:T(8,128)(2,1)S(1)} %get-tuple-element.97), channel_id=1, source_target_pairs={{0,28},{1,29},{2,30},{3,31},{4,0},{5,1},{6,2},{7,3},{8,4},{9,5},{1... | collective-permute-start | bytes 393224 | tf_op jit(solution)/shard_map/ppermute | solution.py:25
  41.9 4.1 %collective-permute-start.11 = (f32[32,16,128]{2,1,0:T(8,128)S(1)}, f32[32,16,128]{2,1,0:T(8,128)S(1)}, u32[]{:S(2)}, u32[]{:S(2)}) collective-permute-start(f32[32,16,128]{2,1,0:T(8,128)S(1)} %get-tuple-element.84), channel_id=1, source_target_pairs={{0,1},{1,0},{2,3},{3,2},{4,5},{5,4},{6,7},{7,6},{8,9},{9,8},{10,11... | collective-permute-start | bytes 786440 | tf_op jit(solution)/shard_map/ppermute | solution.py:25
  41.9 6.0 %collective-permute-start.13 = (bf16[32,16,128]{2,1,0:T(8,128)(2,1)S(1)}, bf16[32,16,128]{2,1,0:T(8,128)(2,1)S(1)}, u32[]{:S(2)}, u32[]{:S(2)}) collective-permute-start(bf16[32,16,128]{2,1,0:T(8,128)(2,1)S(1)} %add_convert_fusion.1), channel_id=1, source_target_pairs={{0,2},{1,3},{2,0},{3,1},{4,6},{5,7},{6,4},{7,5},{8,10},{9,11},{10,... | collective-permute-start | bytes 393224 | tf_op jit(solution)/shard_map/ppermute | solution.py:25

commit v4 on v3

v4 whole, which is shorter than its diff:
```python
import functools

import jax
import jax.numpy as jnp
from jax import lax
from jax.experimental import pallas as pl
from jax.experimental.pallas import tpu as pltpu
from jax.sharding import PartitionSpec as P

PAR_DEV = 128
AXES = ("clus", "sub")
LOADS = 4
VMEM_BYTES = 40 * 1024 * 1024
LOAD_BYTES = 46 * 1024 * 1024


def moved(x, by, mask):
    groups, members = lax.axis_size("clus"), lax.axis_size("sub")
    pairs = [
        (g * members + s, ((g + by) % groups) * members + (s ^ mask))
        for g in range(groups)
        for s in range(members)
    ]
    return lax.ppermute(x, AXES, pairs)


def round_ring(x):
    groups, members = lax.axis_size("clus"), lax.axis_size("sub")
    pairs = [
        (g * members + s, ((g + 1 - 2 * (s % 2)) % groups) * members + s)
        for g in range(groups)
        for s in range(members)
    ]
    return lax.ppermute(x, AXES, pairs)


def wide_place(cluster, row, clusters, total, previous_first):
    first = row - lax.rem(row, clusters)
    place = lax.rem(cluster - first + total, total)
    near = lax.rem(place, clusters)
    following = jnp.where(previous_first, 2 * clusters, clusters)
    preceding = 3 * clusters - following
    side = jnp.where(place < 2 * clusters, following, preceding)
    return jnp.where(place < clusters, place, side + near)


def block_kernel(transposed, total, members, *refs):
    tables_in = refs[:3]
    count = members if transposed else members + 2
    fields = refs[3 : 3 + count]
    first, second, near, out = refs[3 + count : -6]
    lhs, coeffs, far_ids, ranks, near_ids, sems = refs[-6:]
    tables = (far_ids, ranks, near_ids)
    copies = [pltpu.make_async_copy(a, b, sems.at[i]) for i, (a, b) in enumerate(zip(tables_in, tables))]
    for copy in copies:
        copy.start()

    height = fields[0].shape[1]
    clusters = fields[0].shape[0]
    far, _, rank, width = first.shape
    near_total = near.shape[0]
    rows = lhs.shape[1]
    core = lax.rem(lax.axis_index("sub"), 2)
    previous_first = core == (1 if transposed else 0)
    out[...] = jnp.zeros_like(out)

    def build(place, pieces):
        left, right = [], []
        for piece in pieces:
            x = piece.astype(jnp.float32)
            re, im = x[:, :width], x[:, width:]
            left += [re, im]
            right += [-im, re]
        both = [jnp.concatenate(left, axis=0), jnp.concatenate(right, axis=0)]
        lhs[place] = jnp.concatenate(both, axis=1).astype(jnp.bfloat16)

    @pl.loop(0, clusters, unroll=4)
    def _(c):
        build(c, [field[c] for field in fields[:members]])

    if not transposed:

        @pl.loop(0, clusters, unroll=4)
        def _(c):
            here, there = fields[members:]
            build(clusters + c, [here[m * clusters + c] for m in range(members)])
            build(2 * clusters + c, [there[(m ^ 1) * clusters + c] for m in range(members)])

    for copy in copies:
        copy.wait()

    def places(ids, b):
        row = ids[0, b]
        column = wide_place(ids[1, b], row, clusters, total, previous_first)
        row = lax.rem(row, clusters)
        return (row, column) if transposed else (column, row)

    rank_ids = lax.broadcasted_iota(jnp.int32, (rows, 2 * rank), 1)
    rank_ids = jnp.where(rank_ids >= rank, rank_ids - rank, rank_ids)

    for b in range(far):
        re, im = first[b, 0], first[b, 1]
        factor = jnp.concatenate(
            [jnp.concatenate([re, im], axis=1), jnp.concatenate([-im, re], axis=1)], axis=0
        )
        coeff = lax.dot_general(
            lhs[places(far_ids, b)[0]],
            factor,
            (((1,), (1,)), ((), ())),
            preferred_element_type=jnp.float32,
        )
        coeffs[b] = jnp.where(rank_ids < ranks[b], coeff, 0.0).astype(jnp.bfloat16)
    for b in range(far):
        out[places(far_ids, b)[1]] += jnp.dot(
            coeffs[b], second[b].reshape(2 * rank, width), preferred_element_type=jnp.float32
        )
    for b in range(near_total):
        source, place = places(near_ids, b)
        if transposed:
            value = jnp.dot(
                lhs[source], near[b].reshape(2 * width, width), preferred_element_type=jnp.float32
            )
        else:
            value = lax.dot_general(
                lhs[source],
                jnp.concatenate([near[b, 0], near[b, 1]], axis=1),
                (((1,), (1,)), ((), ())),
                preferred_element_type=jnp.float32,
            )
        out[place] += value


def apply_blocks(transposed, total, members, far_ids, ranks, near_ids, fields, first, second, near):
    clusters, height, double = fields[0].shape
    rows = members * 2 * height
    rank, width = first.shape[2:]
    anywhere = pl.BlockSpec(memory_space=pl.ANY)
    vmem = pl.BlockSpec(memory_space=pltpu.VMEM)
    tables = (far_ids, ranks, near_ids)
    flops = 2 * rows * (first.shape[0] * 2 * 2 * rank * 2 * width + near.shape[0] * 2 * width * width)
    return pl.pallas_call(
        functools.partial(block_kernel, transposed, total, members),
        in_specs=[anywhere] * 3 + [vmem] * (len(fields) + 3),
        out_specs=vmem,
        out_shape=jax.ShapeDtypeStruct((clusters * (3 if transposed else 1), rows, width), jnp.float32),
        scratch_shapes=[
            pltpu.VMEM((clusters * (1 if transposed else 3), rows, double), jnp.bfloat16),
            pltpu.VMEM((first.shape[0], rows, 2 * rank), jnp.bfloat16),
            *[pltpu.SMEM(t.shape, t.dtype) for t in tables],
            pltpu.SemaphoreType.DMA((len(tables),)),
        ],
        compiler_params=pltpu.CompilerParams(vmem_limit_bytes=VMEM_BYTES),
        cost_estimate=pl.CostEstimate(flops=flops, bytes_accessed=20_000_000, transcendentals=0),
    )(*tables, *fields, first, second, near)


def load_kernel(parts, *refs):
    count = (len(refs) - 1) // 2
    sources, targets, sems = refs[:count], refs[count : 2 * count], refs[2 * count]
    copies = []
    for i, (source, target) in enumerate(zip(sources, targets)):
        length = source.shape[0] // parts
        for k in range(parts):
            at = pl.ds(k * length, length)
            copies.append(pltpu.make_async_copy(source.at[at], target.at[at], sems.at[i, k]))
    for copy in copies:
        copy.start()
    for copy in copies:
        copy.wait()


def loaded(*arrays):
    return pl.pallas_call(
        functools.partial(load_kernel, LOADS),
        in_specs=[pl.BlockSpec(memory_space=pltpu.HBM)] * len(arrays),
        out_specs=[pl.BlockSpec(memory_space=pltpu.VMEM)] * len(arrays),
        out_shape=[jax.ShapeDtypeStruct(a.shape, a.dtype) for a in arrays],
        scratch_shapes=[pltpu.SemaphoreType.DMA((len(arrays), LOADS))],
        compiler_params=pltpu.CompilerParams(vmem_limit_bytes=LOAD_BYTES),
        cost_estimate=pl.CostEstimate(flops=0, bytes_accessed=12_000_000, transcendentals=0),
    )(*arrays)


def table_kernel(params, weights, counts, spread, places):
    slots, panels = params.shape
    high, width = spread.shape[0], places.shape[0]
    shift = width.bit_length() - 1
    high_ids = lax.broadcasted_iota(jnp.int32, (high, width), 0)
    low_ids = lax.broadcasted_iota(jnp.int32, (width, width), 0)
    slot_ids = lax.broadcasted_iota(jnp.int32, (slots, width), 0)
    for c in range(panels // width):
        at = slice(c * width, (c + 1) * width)
        value = jnp.where(slot_ids < counts[:, at], weights[:, at], 0.0)
        ids = params[:, at]
        high_of, low_of = ids >> shift, ids & (width - 1)
        for m in range(slots):
            row = slice(m, m + 1)
            to = slice((c * slots + m) * width, (c * slots + m + 1) * width)
            spread[:, to] = jnp.where(high_ids == high_of[row], value[row], 0.0)
            places[:, to] = jnp.where(low_ids == low_of[row], 1.0, 0.0).astype(jnp.bfloat16)


def gradient_tables(params, weights, counts, high, width):
    vmem = pl.BlockSpec(memory_space=pltpu.VMEM)
    entries = params.size
    return pl.pallas_call(
        table_kernel,
        in_specs=[vmem] * 3,
        out_specs=[vmem] * 2,
        out_shape=[
            jax.ShapeDtypeStruct((high, entries), jnp.float32),
            jax.ShapeDtypeStruct((width, entries), jnp.bfloat16),
        ],
        compiler_params=pltpu.CompilerParams(vmem_limit_bytes=VMEM_BYTES),
        cost_estimate=pl.CostEstimate(flops=0, bytes_accessed=8_000_000, transcendentals=0),
    )(params, weights, counts)


def final_kernel(column_total, n_fwd, n_adj, *refs):
    fwd_terms = refs[:n_fwd]
    adj_terms = refs[n_fwd : n_fwd + n_adj]
    spread, places, fwd_out, adj_out, grad, scaled = refs[n_fwd + n_adj :]
    clusters, height, _ = fwd_out.shape
    high, width = grad.shape
    entries = spread.shape[1] // clusters
    slots = entries // width
    for c in range(clusters):
        fwd = sum(t[c, : 2 * height].astype(jnp.float32) for t in fwd_terms)
        adj = sum(t[c, : 2 * height].astype(jnp.float32) for t in adj_terms)
        for out, value in ((fwd_out, fwd), (adj_out, adj)):
            out[c, :, :width] = value[:height]
            out[c, :, width:] = value[height:]
        product = fwd * adj
        sens = jnp.sum(product[:height] - product[height:], axis=0, keepdims=True) / column_total
        at = slice(c * entries, (c + 1) * entries)
        value = spread[:, at] * jnp.concatenate([sens] * slots, axis=1)
        top = value.astype(jnp.bfloat16)
        scaled[:high, at] = top
        scaled[high:, at] = (value - top.astype(jnp.float32)).astype(jnp.bfloat16)
    got = lax.dot_general(
        scaled[...], places[...], (((1,), (1,)), ((), ())), preferred_element_type=jnp.float32
    )
    grad[...] = got[:high] + got[high:]


def finish(column_total, shape, fwd_terms, adj_terms, spread, places):
    high, width = spread.shape[0], places.shape[0]
    vmem = pl.BlockSpec(memory_space=pltpu.VMEM)
    terms = [*fwd_terms, *adj_terms]
    field = jax.ShapeDtypeStruct(shape, jnp.float32)
    return pl.pallas_call(
        functools.partial(final_kernel, column_total, len(fwd_terms), len(adj_terms)),
        in_specs=[vmem] * (len(terms) + 2),
        out_specs=[vmem] * 3,
        out_shape=[field, field, jax.ShapeDtypeStruct((high, width), jnp.float32)],
        scratch_shapes=[pltpu.VMEM((2 * high, spread.shape[1]), jnp.bfloat16)],
        compiler_params=pltpu.CompilerParams(vmem_limit_bytes=VMEM_BYTES),
        cost_estimate=pl.CostEstimate(flops=200_000_000, bytes_accessed=3_000_000, transcendentals=0),
    )(*terms, spread, places)


def shards(
    forward_rhs,
    adjoint_rhs,
    far_clusters,
    far_ranks,
    far_left,
    far_right,
    near_clusters,
    near_blocks,
    panel_params,
    panel_weights,
    panel_counts,
):
    groups = lax.axis_size("clus")
    members = lax.axis_size("sub")
    clusters = forward_rhs.shape[0]
    total = clusters * groups
    column_total = forward_rhs.shape[1] * members
    evens = range(0, members, 2)

    height = forward_rhs.shape[1]
    part, rows = 2 * height, 2 * height * members
    tie = lax.optimization_barrier

    w_mine = [adjoint_rhs if m == 0 else moved(adjoint_rhs, 0, m) for m in evens]
    x_chip = [forward_rhs, moved(forward_rhs, 0, 1)]
    x_ring = jnp.concatenate([round_ring(x) for x in x_chip], axis=0)
    x_own = [forward_rhs if m == 0 else moved(forward_rhs, 0, m) for m in evens]
    left, right, near = loaded(far_left, far_right, near_blocks)
    w_mine, x_own, left, right, near = tie((w_mine, x_own, left, right, near))
    w_pieces = [x for m in range(0, members, 2) for x in (w_mine[m // 2], moved(w_mine[m // 2], 0, 1))]
    x_pieces = [*x_chip]
    for x in x_own[1:]:
        x_pieces += [x, moved(x, 0, 1)]
    w_pieces, x_ring = tie((w_pieces, x_ring))
    x_side = [x_ring if m == 0 else moved(x_ring, 0, m) for m in evens]

    apply = functools.partial(
        apply_blocks, total=total, members=members, far_ids=far_clusters, ranks=far_ranks, near_ids=near_clusters
    )
    adj = apply(True, fields=w_pieces, first=left, second=right, near=near)
    x_side, _ = tie((x_side, adj))
    x_here = jnp.concatenate(x_side, axis=0)
    x_there = moved(x_here, 0, 1)

    def rows_of(field, m):
        return field[:, m * part : (m + 2) * part]

    def chip_sums(m):
        given = moved(rows_of(adj[2 * clusters :], m).astype(jnp.bfloat16), 0, 1).astype(jnp.float32)
        given = jnp.concatenate([given[:, part:], given[:, :part]], axis=1)
        return rows_of(adj[clusters : 2 * clusters], m) + given

    sides = [moved(chip_sums(m).astype(jnp.bfloat16), 0, m) for m in evens if m]
    odd_rows = [adj[:clusters, m * part : (m + 1) * part] for m in range(1, members, 2)]
    x_there, odd_rows = tie((x_there, odd_rows))
    adj_core = moved(jnp.concatenate(odd_rows, axis=1), 0, 1)
    fwd = apply(False, fields=[*x_pieces, x_here, x_there], first=right, second=left, near=near)
    fwd, sides, adj_core = tie((fwd, sides, adj_core))

    def own_sum(field, core_part, m):
        k = m // 2
        return field[:clusters, m * part : (m + 1) * part] + core_part[:, k * part : (k + 1) * part]

    fwd_core = moved(
        jnp.concatenate([fwd[:, m * part : (m + 1) * part] for m in range(1, members, 2)], axis=1), 0, 1
    )
    side = chip_sums(0)
    for s in sides:
        side = side + s.astype(jnp.float32)
    side = side.astype(jnp.bfloat16)
    panel_params, side = tie((panel_params, side))
    spread, places = gradient_tables(
        panel_params, panel_weights, panel_counts[None, :],
        PAR_DEV * groups * members // near_blocks.shape[-1], near_blocks.shape[-1],
    )
    ring = round_ring(side)
    own = [moved(own_sum(adj, adj_core, m).astype(jnp.bfloat16), 0, m) for m in evens if m]
    over = [moved(own_sum(fwd, fwd_core, m).astype(jnp.bfloat16), 0, m) for m in evens if m]
    ring, over = tie((ring, over))
    ring_core = moved(ring[:, part:], 0, 1)
    forward_field, adjoint_field, grad = finish(
        column_total, forward_rhs.shape, [fwd, fwd_core, *over], [adj, adj_core, *own, ring, ring_core], spread, places
    )
    devices = groups * members
    pieces = lax.all_to_all(grad.reshape(devices, PAR_DEV), AXES, 0, 0, tiled=True)
    return forward_field, adjoint_field, jnp.sum(pieces, axis=0)


def solution(mesh):
    in_specs = (
        P("clus", "sub", None),
        P("clus", "sub", None),
        P(None, ("clus", "sub")),
        P(("clus", "sub")),
        P(("clus", "sub"), None, None, None),
        P(("clus", "sub"), None, None, None),
        P(None, ("clus", "sub")),
        P(("clus", "sub"), None, None, None),
        P(None, "clus"),
        P(None, "clus"),
        P("clus"),
    )
    out_specs = (P("clus", "sub", None), P("clus", "sub", None), P(("clus", "sub")))
    return jax.shard_map(shards, mesh=mesh, in_specs=in_specs, out_specs=out_specs, check_vma=False)
```

time: 61.4 us -> 59 us (0.961)
  starting transfers between devices: 19.8 us -> 14.9 us
  waiting for transfers between devices: 15.2 us -> 16.9 us
  blocking collectives: 10.6 us -> 11.5 us
  local copies, waits for them, and re-layouts: 0.99 us -> 0.27 us
    ppermute x18 -> x16, starting transfers between devices: 19.8 us -> 11.2 us  [moved(): return lax.ppermute(x, AXES, pairs)]
    ppermute x0 -> x3, waiting for transfers between devices: none -> 6.94 us  [round_ring(): return lax.ppermute(x, AXES, pairs)]
    ppermute x18 -> x16, waiting for transfers between devices: 15.2 us -> 9.95 us  [moved(): return lax.ppermute(x, AXES, pairs)]
    ppermute x0 -> x3, starting transfers between devices: none -> 3.75 us  [round_ring(): return lax.ppermute(x, AXES, pairs)]
    all_to_all x1, blocking collectives: 10.6 us -> 11.5 us  [shards(): lax.all_to_all(grad.reshape(devices, PAR_DEV), AXES, 0, 0, tiled=True)]
    unnamed x16 -> x17, local copies, waits for them, and re-layouts: 0.94 us -> 0.06 us
  transfers between devices with their start and end apart: 18 -> 19, of which waited for: 9 -> 10; matrix products, arithmetic and copies ran while one was open for 1% -> 2% of each run, Pallas kernels for 18% -> 19%
where the time goes in v4:
time: 59 us; the launch traced here: 58.9 us
  waiting for transfers between devices  16.9 us (29%)
  starting transfers between devices  14.9 us (25%)
  Pallas kernels  13 us (22%)
  blocking collectives  11.5 us (19%)
  other arithmetic  1.3 us (2%)
  between operations  0.91 us (2%)
    all_to_all x1, blocking collectives, shards(): lax.all_to_all(grad.reshape(devices, PAR_DEV), AXES, 0, 0, tiled=True)  11.5 us
    ppermute x16, starting transfers between devices, moved(): return lax.ppermute(x, AXES, pairs)  11.2 us
    ppermute x16, waiting for transfers between devices, moved(): return lax.ppermute(x, AXES, pairs)  9.95 us
    ppermute x3, waiting for transfers between devices, round_ring(): return lax.ppermute(x, AXES, pairs)  6.94 us
    pallas_call x2, Pallas kernels, apply_blocks(): pl.pallas_call(functools.partial(block_kernel, transposed, total, members...  6.79 us
    ppermute x3, starting transfers between devices, round_ring(): return lax.ppermute(x, AXES, pairs)  3.75 us
    pallas_call x1, Pallas kernels, loaded(): pl.pallas_call(functools.partial(load_kernel, LOADS), in_specs=[pl.BlockS...  2.87 us
    pallas_call x1, Pallas kernels, finish(): pl.pallas_call(functools.partial(final_kernel, column_total, len(fwd_term...  2.11 us
  transfers between devices with their start and end apart: 19, of which 10 were waited for; matrix products, arithmetic and copies ran while one was open for 2% of the time, Pallas kernels for 19%

profile of v4, /device:TPU:0, one launch (start us, length us, event | category | flops | bytes accessed | tf_op | source)
XLA Modules:
  0.0 58.9 jit_solution(6307890946725748340)
XLA Ops:
  0.6 0.0 copy-start
  0.6 0.0 copy-start.6
  0.7 0.0 copy-start.7
  0.7 0.0 copy-start.5
  0.7 0.5 collective-permute-start
  1.2 2.6 %collective-permute-start.1 = (bf16[32,8,256]{2,1,0:T(8,128)(2,1)}, bf16[32,8,256]{2,1,0:T(8,128)(2,1)S(1)}, u32[]{:S(2)}, u32[]{:S(2)}) collective-permute-start(bf16[32,8,256]{2,1,0:T(8,128)(2,1)} %refs_3_.1), channel_id=1, source_target_pairs={{0,2},{1,3},{2,0},{3,1},{4,6},{5,7},{6,4},{7,5},{8,10},{9,11},{10,... | collective-permute-start | bytes 393224 | tf_op jit(solution)/shard_map/ppermute | solution.py:24
  3.8 0.1 collective-permute-start.2
  3.9 1.9 %collective-permute-start.6 = (bf16[32,8,256]{2,1,0:T(8,128)(2,1)}, bf16[32,8,256]{2,1,0:T(8,128)(2,1)S(1)}, u32[]{:S(2)}, u32[]{:S(2)}) collective-permute-start(bf16[32,8,256]{2,1,0:T(8,128)(2,1)} %refs_3_.2), channel_id=1, source_target_pairs={{0,4},{1,29},{2,6},{3,31},{4,8},{5,1},{6,10},{7,3},{8,12},{9,5},{1... | collective-permute-start | bytes 393224 | tf_op jit(solution)/shard_map/ppermute | solution.py:34
  5.8 0.0 collective-permute-done.refs_4_
  5.8 1.5 %collective-permute-start.7 = (bf16[32,8,256]{2,1,0:T(8,128)(2,1)S(1)}, bf16[32,8,256]{2,1,0:T(8,128)(2,1)S(1)}, u32[]{:S(2)}, u32[]{:S(2)}) collective-permute-start(bf16[32,8,256]{2,1,0:T(8,128)(2,1)S(1)} %collective-permute-done.refs_4_), channel_id=1, source_target_pairs={{0,4},{1,29},{2,6},{3,31},{4,8},{5,1},{6,10},{7,3},{8,12},{9,5},{1... | collective-permute-start | bytes 393224 | tf_op jit(solution)/shard_map/ppermute | solution.py:34
  7.3 2.9 %shard_map.130 = (bf16[128,2,32,128]{3,2,1,0:T(8,128)(2,1)S(1)}, bf16[128,2,32,128]{3,2,1,0:T(8,128)(2,1)S(1)}, bf16[32,2,128,128]{3,2,1,0:T(8,128)(2,1)S(1)}) custom-call(bf16[128,2,32,128]{3,2,1,0:T(8,128)(2,1)} %refs_0_.3, bf16[128,2,32,128]{3,2,1,0:T(8,128)(2,1)} %refs_1_.3, bf16[32,2,128,128]{3,2,1,0:T(8,128)(2,1)} %refs_2_.3), custom_call_target="tpu_custom_call" | custom-call | bytes 12000000 | tf_op jit(solution)/shard_map/pallas_call | solution.py:173
  10.2 0.0 collective-permute-done.1.refs_5_
  10.2 0.7 %collective-permute-done.2.refs_5_ = bf16[32,8,256]{2,1,0:T(8,128)(2,1)S(1)} collective-permute-done((bf16[32,8,256]{2,1,0:T(8,128)(2,1)}, bf16[32,8,256]{2,1,0:T(8,128)(2,1)S(1)}, u32[]{:S(2)}, u32[]{:S(2)}) %collective-permute-start.2) | collective-permute-done | bytes 131104 | tf_op jit(solution)/shard_map/ppermute | solution.py:24
  10.9 0.0 copy-done
  10.9 0.8 %collective-permute-start.4 = (bf16[32,8,256]{2,1,0:T(8,128)(2,1)S(1)}, bf16[32,8,256]{2,1,0:T(8,128)(2,1)S(1)}, u32[]{:S(2)}, u32[]{:S(2)}) collective-permute-start(bf16[32,8,256]{2,1,0:T(8,128)(2,1)S(1)} %copy-done), channel_id=1, source_target_pairs={{0,1},{1,0},{2,3},{3,2},{4,5},{5,4},{6,7},{7,6},{8,9},{9,8},{10,11... | collective-permute-start | bytes 393224 | tf_op jit(solution)/shard_map/ppermute | solution.py:24
  11.7 0.1 collective-permute-start.5
  11.7 0.4 collective-permute-done.6
  12.1 1.4 %collective-permute-done.7 = bf16[32,8,256]{2,1,0:T(8,128)(2,1)S(1)} collective-permute-done((bf16[32,8,256]{2,1,0:T(8,128)(2,1)S(1)}, bf16[32,8,256]{2,1,0:T(8,128)(2,1)S(1)}, u32[]{:S(2)}, u32[]{:S(2)}) %collective-permute-start.7) | collective-permute-done | bytes 131104 | tf_op jit(solution)/shard_map/ppermute | solution.py:34
  13.5 0.0 collective-permute-done.4.refs_4_
  13.6 0.0 collective-permute-done.5.refs_6_
  13.6 1.7 %collective-permute-start.8 = (bf16[64,8,256]{2,1,0:T(8,128)(2,1)S(1)}, bf16[64,8,256]{2,1,0:T(8,128)(2,1)S(1)}, u32[]{:S(2)}, u32[]{:S(2)}) collective-permute-start(bf16[64,8,256]{2,1,0:T(8,128)(2,1)S(1)} %pad_maximum_fusion.2), channel_id=1, source_target_pairs={{0,2},{1,3},{2,0},{3,1},{4,6},{5,7},{6,4},{7,5},{8,10},{9,11},{10,... | collective-permute-start | bytes 786440 | tf_op jit(solution)/shard_map/ppermute | solution.py:24
  15.3 0.0 copy-done.6
  15.3 0.0 copy-done.7
  15.3 0.0 copy-done.5
  15.3 3.4 %shard_map.131.refs_3_ = f32[96,64,128]{2,1,0:T(8,128)S(1)} custom-call(s32[2,128]{1,0:T(2,128)S(1)} %copy-done.5, s32[128]{0:T(128)S(1)} %copy-done.7, s32[2,32]{1,0:T(2,128)S(1)} %copy-done.6, bf16[32,8,256]{2,1,0:T(8,128)(2,1)S(1)} %copy-done, bf16[32,8,256]{2,1,0:T(8,128)(2,1)S(1)} %collective-permute-done.4.refs_4_, ...), custom_call_target="tpu_custom_call" | custom-call | flops 671088640 | bytes 20000000 | tf_op jit(solution)/shard_map/pallas_call | solution.py:141
  18.7 3.9 %collective-permute-done.8 = bf16[64,8,256]{2,1,0:T(8,128)(2,1)S(1)} collective-permute-done((bf16[64,8,256]{2,1,0:T(8,128)(2,1)S(1)}, bf16[64,8,256]{2,1,0:T(8,128)(2,1)S(1)}, u32[]{:S(2)}, u32[]{:S(2)}) %collective-permute-start.8) | collective-permute-done | bytes 262176 | tf_op jit(solution)/shard_map/ppermute | solution.py:24
  22.7 0.2 collective-permute-start.9
  22.9 0.3 convert.4
  23.3 0.0 copy-start.1
  23.3 0.5 collective-permute-start.10
  23.8 0.9 %collective-permute-done.9.refs_8_ = bf16[128,8,256]{2,1,0:T(8,128)(2,1)S(1)} collective-permute-done((bf16[128,8,256]{2,1,0:T(8,128)(2,1)S(1)}, bf16[128,8,256]{2,1,0:T(8,128)(2,1)S(1)}, u32[]{:S(2)}, u32[]{:S(2)}) %collective-permute-start.9) | collective-permute-done | bytes 524320 | tf_op jit(solution)/shard_map/ppermute | solution.py:24
  24.7 0.1 pad_maximum_fusion
  24.8 0.2 collective-permute-start.12
  25.0 0.1 collective-permute-done.10
  25.1 0.1 fusion.2
  25.2 1.7 %collective-permute-start.11 = (bf16[32,32,128]{2,1,0:T(8,128)(2,1)S(1)}, bf16[32,32,128]{2,1,0:T(8,128)(2,1)S(1)}, u32[]{:S(2)}, u32[]{:S(2)}) collective-permute-start(bf16[32,32,128]{2,1,0:T(8,128)(2,1)S(1)} %fusion.2), channel_id=1, source_target_pairs={{0,2},{1,3},{2,0},{3,1},{4,6},{5,7},{6,4},{7,5},{8,10},{9,11},{10,... | collective-permute-start | bytes 786440 | tf_op jit(solution)/shard_map/ppermute | solution.py:24
  26.9 0.0 collective-permute-start.3
  26.9 0.5 collective-permute-start.14
  27.4 0.8 %collective-permute-done.3.refs_6_ = bf16[32,8,256]{2,1,0:T(8,128)(2,1)S(1)} collective-permute-done((bf16[32,8,256]{2,1,0:T(8,128)(2,1)S(1)}, bf16[32,8,256]{2,1,0:T(8,128)(2,1)S(1)}, u32[]{:S(2)}, u32[]{:S(2)}) %collective-permute-start.3) | collective-permute-done | bytes 131104 | tf_op jit(solution)/shard_map/ppermute | solution.py:24
  28.3 0.0 copy-done.1
  28.3 3.4 %shard_map.132.refs_0_ = f32[32,64,128]{2,1,0:T(8,128)S(1)} custom-call(s32[2,128]{1,0:T(2,128)S(1)} %copy-done.5, s32[128]{0:T(128)S(1)} %copy-done.7, s32[2,32]{1,0:T(2,128)S(1)} %copy-done.6, bf16[32,8,256]{2,1,0:T(8,128)(2,1)S(1)} %copy-done.1, bf16[32,8,256]{2,1,0:T(8,128)(2,1)S(1)} %collective-permute-done.refs_4_, ...), custom_call_target="tpu_custom_call" | custom-call | flops 671088640 | bytes 20000000 | tf_op jit(solution)/shard_map/pallas_call | solution.py:141
  31.7 2.0 %collective-permute-done.11 = bf16[32,32,128]{2,1,0:T(8,128)(2,1)S(1)} collective-permute-done((bf16[32,32,128]{2,1,0:T(8,128)(2,1)S(1)}, bf16[32,32,128]{2,1,0:T(8,128)(2,1)S(1)}, u32[]{:S(2)}, u32[]{:S(2)}) %collective-permute-start.11) | collective-permute-done | bytes 262176 | tf_op jit(solution)/shard_map/ppermute | solution.py:24
  33.7 0.0 collective-permute-done.12.refs_4_
  33.8 0.1 pad_maximum_fusion.1
  33.8 0.0 copy-start.2
  33.9 0.0 copy-start.3
  33.9 0.0 copy-start.4
  33.9 0.1 collective-permute-start.13
  34.0 0.0 collective-permute-done.14
  34.0 0.1 fusion.1
  34.1 0.3 collective-permute-start.15
  34.4 1.4 %collective-permute-done.13.refs_1_ = f32[32,32,128]{2,1,0:T(8,128)S(1)} collective-permute-done((f32[32,32,128]{2,1,0:T(8,128)S(1)}, f32[32,32,128]{2,1,0:T(8,128)S(1)}, u32[]{:S(2)}, u32[]{:S(2)}) %collective-permute-start.13) | collective-permute-done | bytes 524320 | tf_op jit(solution)/shard_map/ppermute | solution.py:24
  35.9 1.7 %collective-permute-start.16 = (bf16[32,16,128]{2,1,0:T(8,128)(2,1)S(1)}, bf16[32,16,128]{2,1,0:T(8,128)(2,1)S(1)}, u32[]{:S(2)}, u32[]{:S(2)}) collective-permute-start(bf16[32,16,128]{2,1,0:T(8,128)(2,1)S(1)} %fusion.4), channel_id=1, source_target_pairs={{0,2},{1,3},{2,0},{3,1},{4,6},{5,7},{6,4},{7,5},{8,10},{9,11},{10,... | collective-permute-start | bytes 393224 | tf_op jit(solution)/shard_map/ppermute | solution.py:24
  37.7 0.4 collective-permute-start.17
  38.1 5.2 %collective-permute-done.15.refs_6_ = bf16[32,32,128]{2,1,0:T(8,128)(2,1)S(1)} collective-permute-done((bf16[32,32,128]{2,1,0:T(8,128)(2,1)S(1)}, bf16[32,32,128]{2,1,0:T(8,128)(2,1)S(1)}, u32[]{:S(2)}, u32[]{:S(2)}) %collective-permute-start.15) | collective-permute-done | bytes 262176 | tf_op jit(solution)/shard_map/ppermute | solution.py:34
  43.2 0.0 collective-permute-done.16.refs_2_
  43.3 0.1 collective-permute-start.18
  43.3 0.0 copy-done.2
  43.4 1.3 %shard_map.133 = (f32[32,16384]{1,0:T(8,128)S(1)}, bf16[128,16384]{1,0:T(8,128)(2,1)S(1)}) custom-call(s32[4,4096]{1,0:T(4,128)S(1)} %copy-done.2, f32[4,4096]{1,0:T(4,128)S(1)} %copy-done.3, s32[1,4096]{1,0:T(1,128)S(1)} %bitcast.4), custom_call_target="tpu_custom_call" | custom-call | bytes 8000000 | tf_op jit(solution)/shard_map/pallas_call | solution.py:206
  44.7 0.0 collective-permute-done.17.refs_5_
  44.7 0.0 collective-permute-done.18.refs_7_
  44.7 2.1 %shard_map.134 = (f32[32,8,256]{2,1,0:T(8,128)}, f32[32,8,256]{2,1,0:T(8,128)}, f32[32,128]{1,0:T(8,128)S(1)}) custom-call(f32[32,64,128]{2,1,0:T(8,128)S(1)} %shard_map.132.refs_0_, f32[32,32,128]{2,1,0:T(8,128)S(1)} %collective-permute-done.13.refs_1_, bf16[32,16,128]{2,1,0:T(8,128)(2,1)S(1)} %collective-permute-done.16.refs_2_, ...), custom_call_target="tpu_custom_call" | custom-call | flops 200000000 | bytes 3000000 | tf_op jit(solution)/shard_map/pallas_call | solution.py:251
  46.8 11.5 %all_to_all.9 = f32[32,1,128]{2,1,0:T(1,128)S(1)} all-to-all(f32[32,1,128]{2,1,0:T(1,128)S(1)} %bitcast.5), channel_id=1, replica_groups=mesh['clus'=8,'sub'=4] {'clus','sub'}, dimensions={0} | all-to-all | bytes 32768 | tf_op jit(solution)/shard_map/all_to_all | solution.py:347
  58.3 0.6 reduce_sum.9
  (13 shorter events, 0.3 us)
Async XLA Ops:
  0.6 10.3 %copy-start = (bf16[32,8,256]{2,1,0:T(8,128)(2,1)S(1)}, bf16[32,8,256]{2,1,0:T(8,128)(2,1)}, u32[]{:S(2)}) copy-start(bf16[32,8,256]{2,1,0:T(8,128)(2,1)} %refs_3_.1) | copy-start | bytes 393220
  0.6 14.7 %copy-start.6 = (s32[2,32]{1,0:T(2,128)S(1)}, s32[2,32]{1,0:T(2,128)}, u32[]{:S(2)}) copy-start(s32[2,32]{1,0:T(2,128)} %refs_2_.5) | copy-start | bytes 772
  0.7 14.7 %copy-start.7 = (s32[128]{0:T(128)S(1)}, s32[128]{0:T(128)}, u32[]{:S(2)}) copy-start(s32[128]{0:T(128)} %refs_1_.5) | copy-start | bytes 1540
  0.7 14.7 %copy-start.5 = (s32[2,128]{1,0:T(2,128)S(1)}, s32[2,128]{1,0:T(2,128)}, u32[]{:S(2)}) copy-start(s32[2,128]{1,0:T(2,128)} %refs_0_.5) | copy-start | bytes 3076
  0.7 5.1 %collective-permute-start = (bf16[32,8,256]{2,1,0:T(8,128)(2,1)}, bf16[32,8,256]{2,1,0:T(8,128)(2,1)S(1)}, u32[]{:S(2)}, u32[]{:S(2)}) collective-permute-start(bf16[32,8,256]{2,1,0:T(8,128)(2,1)} %refs_3_.2), channel_id=1, source_target_pairs={{0,1},{1,0},{2,3},{3,2},{4,5},{5,4},{6,7},{7,6},{8,9},{9,8},{10,11... | collective-permute-start | bytes 393224 | tf_op jit(solution)/shard_map/ppermute | solution.py:24
  1.2 9.0 %collective-permute-start.1 = (bf16[32,8,256]{2,1,0:T(8,128)(2,1)}, bf16[32,8,256]{2,1,0:T(8,128)(2,1)S(1)}, u32[]{:S(2)}, u32[]{:S(2)}) collective-permute-start(bf16[32,8,256]{2,1,0:T(8,128)(2,1)} %refs_3_.1), channel_id=1, source_target_pairs={{0,2},{1,3},{2,0},{3,1},{4,6},{5,7},{6,4},{7,5},{8,10},{9,11},{10,... | collective-permute-start | bytes 393224 | tf_op jit(solution)/shard_map/ppermute | solution.py:24
  3.8 7.1 %collective-permute-start.2 = (bf16[32,8,256]{2,1,0:T(8,128)(2,1)}, bf16[32,8,256]{2,1,0:T(8,128)(2,1)S(1)}, u32[]{:S(2)}, u32[]{:S(2)}) collective-permute-start(bf16[32,8,256]{2,1,0:T(8,128)(2,1)} %refs_3_.2), channel_id=1, source_target_pairs={{0,2},{1,3},{2,0},{3,1},{4,6},{5,7},{6,4},{7,5},{8,10},{9,11},{10,... | collective-permute-start | bytes 393224 | tf_op jit(solution)/shard_map/ppermute | solution.py:24
  3.9 8.2 %collective-permute-start.6 = (bf16[32,8,256]{2,1,0:T(8,128)(2,1)}, bf16[32,8,256]{2,1,0:T(8,128)(2,1)S(1)}, u32[]{:S(2)}, u32[]{:S(2)}) collective-permute-start(bf16[32,8,256]{2,1,0:T(8,128)(2,1)} %refs_3_.2), channel_id=1, source_target_pairs={{0,4},{1,29},{2,6},{3,31},{4,8},{5,1},{6,10},{7,3},{8,12},{9,5},{1... | collective-permute-start | bytes 393224 | tf_op jit(solution)/shard_map/ppermute | solution.py:34
  5.8 7.7 %collective-permute-start.7 = (bf16[32,8,256]{2,1,0:T(8,128)(2,1)S(1)}, bf16[32,8,256]{2,1,0:T(8,128)(2,1)S(1)}, u32[]{:S(2)}, u32[]{:S(2)}) collective-permute-start(bf16[32,8,256]{2,1,0:T(8,128)(2,1)S(1)} %collective-permute-done.refs_4_), channel_id=1, source_target_pairs={{0,4},{1,29},{2,6},{3,31},{4,8},{5,1},{6,10},{7,3},{8,12},{9,5},{1... | collective-permute-start | bytes 393224 | tf_op jit(solution)/shard_map/ppermute | solution.py:34
  10.9 2.7 %collective-permute-start.4 = (bf16[32,8,256]{2,1,0:T(8,128)(2,1)S(1)}, bf16[32,8,256]{2,1,0:T(8,128)(2,1)S(1)}, u32[]{:S(2)}, u32[]{:S(2)}) collective-permute-start(bf16[32,8,256]{2,1,0:T(8,128)(2,1)S(1)} %copy-done), channel_id=1, source_target_pairs={{0,1},{1,0},{2,3},{3,2},{4,5},{5,4},{6,7},{7,6},{8,9},{9,8},{10,11... | collective-permute-start | bytes 393224 | tf_op jit(solution)/shard_map/ppermute | solution.py:24
  11.7 1.9 %collective-permute-start.5 = (bf16[32,8,256]{2,1,0:T(8,128)(2,1)S(1)}, bf16[32,8,256]{2,1,0:T(8,128)(2,1)S(1)}, u32[]{:S(2)}, u32[]{:S(2)}) collective-permute-start(bf16[32,8,256]{2,1,0:T(8,128)(2,1)S(1)} %collective-permute-done.1.refs_5_), channel_id=1, source_target_pairs={{0,1},{1,0},{2,3},{3,2},{4,5},{5,4},{6,7},{7,6},{8,9},{9,8},{10,11... | collective-permute-start | bytes 393224 | tf_op jit(solution)/shard_map/ppermute | solution.py:24
  13.6 9.1 %collective-permute-start.8 = (bf16[64,8,256]{2,1,0:T(8,128)(2,1)S(1)}, bf16[64,8,256]{2,1,0:T(8,128)(2,1)S(1)}, u32[]{:S(2)}, u32[]{:S(2)}) collective-permute-start(bf16[64,8,256]{2,1,0:T(8,128)(2,1)S(1)} %pad_maximum_fusion.2), channel_id=1, source_target_pairs={{0,2},{1,3},{2,0},{3,1},{4,6},{5,7},{6,4},{7,5},{8,10},{9,11},{10,... | collective-permute-start | bytes 786440 | tf_op jit(solution)/shard_map/ppermute | solution.py:24
  22.7 2.0 %collective-permute-start.9 = (bf16[128,8,256]{2,1,0:T(8,128)(2,1)S(1)}, bf16[128,8,256]{2,1,0:T(8,128)(2,1)S(1)}, u32[]{:S(2)}, u32[]{:S(2)}) collective-permute-start(bf16[128,8,256]{2,1,0:T(8,128)(2,1)S(1)} %constant_dynamic-update-slice_fusion.refs_7_), channel_id=1, source_target_pairs={{0,1},{1,0},{2,3},{3,2},{4,5},{5,4},{6,7},{7,6},{8,9},{9,8},{10,11... | collective-permute-start | bytes 1572872 | tf_op jit(solution)/shard_map/ppermute | solution.py:24
  23.3 5.0 %copy-start.1 = (bf16[32,8,256]{2,1,0:T(8,128)(2,1)S(1)}, bf16[32,8,256]{2,1,0:T(8,128)(2,1)}, u32[]{:S(2)}) copy-start(bf16[32,8,256]{2,1,0:T(8,128)(2,1)} %refs_3_.2) | copy-start | bytes 393220
  23.3 1.8 %collective-permute-start.10 = (bf16[32,32,128]{2,1,0:T(8,128)(2,1)S(1)}, bf16[32,32,128]{2,1,0:T(8,128)(2,1)S(1)}, u32[]{:S(2)}, u32[]{:S(2)}) collective-permute-start(bf16[32,32,128]{2,1,0:T(8,128)(2,1)S(1)} %get-tuple-element.68), channel_id=1, source_target_pairs={{0,1},{1,0},{2,3},{3,2},{4,5},{5,4},{6,7},{7,6},{8,9},{9,8},{10,11... | collective-permute-start | bytes 786440 | tf_op jit(solution)/shard_map/ppermute | solution.py:24
  24.8 9.0 %collective-permute-start.12 = (f32[32,32,128]{2,1,0:T(8,128)S(1)}, f32[32,32,128]{2,1,0:T(8,128)S(1)}, u32[]{:S(2)}, u32[]{:S(2)}) collective-permute-start(f32[32,32,128]{2,1,0:T(8,128)S(1)} %pad_maximum_fusion), channel_id=1, source_target_pairs={{0,1},{1,0},{2,3},{3,2},{4,5},{5,4},{6,7},{7,6},{8,9},{9,8},{10,11... | collective-permute-start | bytes 1572872 | tf_op jit(solution)/shard_map/ppermute | solution.py:24
  25.2 8.5 %collective-permute-start.11 = (bf16[32,32,128]{2,1,0:T(8,128)(2,1)S(1)}, bf16[32,32,128]{2,1,0:T(8,128)(2,1)S(1)}, u32[]{:S(2)}, u32[]{:S(2)}) collective-permute-start(bf16[32,32,128]{2,1,0:T(8,128)(2,1)S(1)} %fusion.2), channel_id=1, source_target_pairs={{0,2},{1,3},{2,0},{3,1},{4,6},{5,7},{6,4},{7,5},{8,10},{9,11},{10,... | collective-permute-start | bytes 786440 | tf_op jit(solution)/shard_map/ppermute | solution.py:24
  26.9 1.3 %collective-permute-start.3 = (bf16[32,8,256]{2,1,0:T(8,128)(2,1)S(1)}, bf16[32,8,256]{2,1,0:T(8,128)(2,1)S(1)}, u32[]{:S(2)}, u32[]{:S(2)}) collective-permute-start(bf16[32,8,256]{2,1,0:T(8,128)(2,1)S(1)} %collective-permute-done.2.refs_5_), channel_id=1, source_target_pairs={{0,1},{1,0},{2,3},{3,2},{4,5},{5,4},{6,7},{7,6},{8,9},{9,8},{10,11... | collective-permute-start | bytes 393224 | tf_op jit(solution)/shard_map/ppermute | solution.py:24
  26.9 7.0 %collective-permute-start.14 = (bf16[32,32,128]{2,1,0:T(8,128)(2,1)S(1)}, bf16[32,32,128]{2,1,0:T(8,128)(2,1)S(1)}, u32[]{:S(2)}, u32[]{:S(2)}) collective-permute-start(bf16[32,32,128]{2,1,0:T(8,128)(2,1)S(1)} %get-tuple-element.67), channel_id=1, source_target_pairs={{0,1},{1,0},{2,3},{3,2},{4,5},{5,4},{6,7},{7,6},{8,9},{9,8},{10,11... | collective-permute-start | bytes 786440 | tf_op jit(solution)/shard_map/ppermute | solution.py:24
  33.8 9.5 %copy-start.2 = (s32[4,4096]{1,0:T(4,128)S(1)}, s32[4,4096]{1,0:T(4,128)}, u32[]{:S(2)}) copy-start(s32[4,4096]{1,0:T(4,128)} %params) | copy-start | bytes 196612
  33.9 9.5 %copy-start.3 = (f32[4,4096]{1,0:T(4,128)S(1)}, f32[4,4096]{1,0:T(4,128)}, u32[]{:S(2)}) copy-start(f32[4,4096]{1,0:T(4,128)} %weights.1) | copy-start | bytes 196612
  33.9 9.5 %copy-start.4 = (s32[4096]{0:T(1024)S(1)}, s32[4096]{0:T(1024)}, u32[]{:S(2)}) copy-start(s32[4096]{0:T(1024)} %param.21) | copy-start | bytes 49156
  33.9 2.0 %collective-permute-start.13 = (f32[32,32,128]{2,1,0:T(8,128)S(1)}, f32[32,32,128]{2,1,0:T(8,128)S(1)}, u32[]{:S(2)}, u32[]{:S(2)}) collective-permute-start(f32[32,32,128]{2,1,0:T(8,128)S(1)} %pad_maximum_fusion.1), channel_id=1, source_target_pairs={{0,1},{1,0},{2,3},{3,2},{4,5},{5,4},{6,7},{7,6},{8,9},{9,8},{10,11... | collective-permute-start | bytes 1572872 | tf_op jit(solution)/shard_map/ppermute | solution.py:24
  34.1 9.1 %collective-permute-start.15 = (bf16[32,32,128]{2,1,0:T(8,128)(2,1)S(1)}, bf16[32,32,128]{2,1,0:T(8,128)(2,1)S(1)}, u32[]{:S(2)}, u32[]{:S(2)}) collective-permute-start(bf16[32,32,128]{2,1,0:T(8,128)(2,1)S(1)} %fusion.1), channel_id=1, source_target_pairs={{0,4},{1,29},{2,6},{3,31},{4,8},{5,1},{6,10},{7,3},{8,12},{9,5},{1... | collective-permute-start | bytes 786440 | tf_op jit(solution)/shard_map/ppermute | solution.py:34
  35.9 7.4 %collective-permute-start.16 = (bf16[32,16,128]{2,1,0:T(8,128)(2,1)S(1)}, bf16[32,16,128]{2,1,0:T(8,128)(2,1)S(1)}, u32[]{:S(2)}, u32[]{:S(2)}) collective-permute-start(bf16[32,16,128]{2,1,0:T(8,128)(2,1)S(1)} %fusion.4), channel_id=1, source_target_pairs={{0,2},{1,3},{2,0},{3,1},{4,6},{5,7},{6,4},{7,5},{8,10},{9,11},{10,... | collective-permute-start | bytes 393224 | tf_op jit(solution)/shard_map/ppermute | solution.py:24
  37.7 7.0 %collective-permute-start.17 = (bf16[32,16,128]{2,1,0:T(8,128)(2,1)S(1)}, bf16[32,16,128]{2,1,0:T(8,128)(2,1)S(1)}, u32[]{:S(2)}, u32[]{:S(2)}) collective-permute-start(bf16[32,16,128]{2,1,0:T(8,128)(2,1)S(1)} %fusion.3), channel_id=1, source_target_pairs={{0,2},{1,3},{2,0},{3,1},{4,6},{5,7},{6,4},{7,5},{8,10},{9,11},{10,... | collective-permute-start | bytes 393224 | tf_op jit(solution)/shard_map/ppermute | solution.py:24
  43.3 1.4 %collective-permute-start.18 = (bf16[32,16,128]{2,1,0:T(8,128)(2,1)S(1)}, bf16[32,16,128]{2,1,0:T(8,128)(2,1)S(1)}, u32[]{:S(2)}, u32[]{:S(2)}) collective-permute-start(bf16[32,16,128]{2,1,0:T(8,128)(2,1)S(1)} %slice.77), channel_id=1, source_target_pairs={{0,1},{1,0},{2,3},{3,2},{4,5},{5,4},{6,7},{7,6},{8,9},{9,8},{10,11... | collective-permute-start | bytes 393224 | tf_op jit(solution)/shard_map/ppermute | solution.py:24

commit v5 on v4

--- a/solution.py
+++ b/solution.py
@@ -48,7 +48,7 @@
     tables_in = refs[:3]
     count = members if transposed else members + 2
     fields = refs[3 : 3 + count]
-    first, second, near, out = refs[3 + count : -6]
+    first, second, near, out, *give = refs[3 + count : -6]
     lhs, coeffs, far_ids, ranks, near_ids, sems = refs[-6:]
     tables = (far_ids, ranks, near_ids)
     copies = [pltpu.make_async_copy(a, b, sems.at[i]) for i, (a, b) in enumerate(zip(tables_in, tables))]
@@ -128,6 +128,10 @@
                 preferred_element_type=jnp.float32,
             )
         out[place] += value
+    part = 2 * height
+    for k, half in enumerate(give):
+        rows_here = out[2 * clusters :, 2 * k * part : (2 * k + 2) * part]
+        half[...] = jnp.concatenate([rows_here[:, part:], rows_here[:, :part]], axis=1).astype(half.dtype)
 
 
 def apply_blocks(transposed, total, members, far_ids, ranks, near_ids, fields, first, second, near):
@@ -137,12 +141,17 @@
     anywhere = pl.BlockSpec(memory_space=pl.ANY)
     vmem = pl.BlockSpec(memory_space=pltpu.VMEM)
     tables = (far_ids, ranks, near_ids)
+    give = jax.ShapeDtypeStruct((clusters, 4 * height, width), jnp.bfloat16)
+    gives = [give] * (members // 2) if transposed else []
     flops = 2 * rows * (first.shape[0] * 2 * 2 * rank * 2 * width + near.shape[0] * 2 * width * width)
     return pl.pallas_call(
         functools.partial(block_kernel, transposed, total, members),
         in_specs=[anywhere] * 3 + [vmem] * (len(fields) + 3),
-        out_specs=vmem,
-        out_shape=jax.ShapeDtypeStruct((clusters * (3 if transposed else 1), rows, width), jnp.float32),
+        out_specs=[vmem] * (1 + len(gives)),
+        out_shape=[
+            jax.ShapeDtypeStruct((clusters * (3 if transposed else 1), rows, width), jnp.float32),
+            *gives,
+        ],
         scratch_shapes=[
             pltpu.VMEM((clusters * (1 if transposed else 3), rows, double), jnp.bfloat16),
             pltpu.VMEM((first.shape[0], rows, 2 * rank), jnp.bfloat16),
@@ -288,18 +297,18 @@
     x_ring = jnp.concatenate([round_ring(x) for x in x_chip], axis=0)
     x_own = [forward_rhs if m == 0 else moved(forward_rhs, 0, m) for m in evens]
     left, right, near = loaded(far_left, far_right, near_blocks)
-    w_mine, x_own, left, right, near = tie((w_mine, x_own, left, right, near))
+    x_ring, x_own, left, right, near = tie((x_ring, x_own, left, right, near))
     w_pieces = [x for m in range(0, members, 2) for x in (w_mine[m // 2], moved(w_mine[m // 2], 0, 1))]
     x_pieces = [*x_chip]
     for x in x_own[1:]:
         x_pieces += [x, moved(x, 0, 1)]
-    w_pieces, x_ring = tie((w_pieces, x_ring))
     x_side = [x_ring if m == 0 else moved(x_ring, 0, m) for m in evens]
 
+    w_pieces, x_pieces = tie((w_pieces, x_pieces))
     apply = functools.partial(
         apply_blocks, total=total, members=members, far_ids=far_clusters, ranks=far_ranks, near_ids=near_clusters
     )
-    adj = apply(True, fields=w_pieces, first=left, second=right, near=near)
+    adj, *give = apply(True, fields=w_pieces, first=left, second=right, near=near)
     x_side, _ = tie((x_side, adj))
     x_here = jnp.concatenate(x_side, axis=0)
     x_there = moved(x_here, 0, 1)
@@ -307,17 +316,17 @@
     def rows_of(field, m):
         return field[:, m * part : (m + 2) * part]
 
+    given = [moved(x, 0, 1) for x in give]
+
     def chip_sums(m):
-        given = moved(rows_of(adj[2 * clusters :], m).astype(jnp.bfloat16), 0, 1).astype(jnp.float32)
-        given = jnp.concatenate([given[:, part:], given[:, :part]], axis=1)
-        return rows_of(adj[clusters : 2 * clusters], m) + given
+        return rows_of(adj[clusters : 2 * clusters], m) + given[m // 2].astype(jnp.float32)
 
     sides = [moved(chip_sums(m).astype(jnp.bfloat16), 0, m) for m in evens if m]
     odd_rows = [adj[:clusters, m * part : (m + 1) * part] for m in range(1, members, 2)]
     x_there, odd_rows = tie((x_there, odd_rows))
     adj_core = moved(jnp.concatenate(odd_rows, axis=1), 0, 1)
-    fwd = apply(False, fields=[*x_pieces, x_here, x_there], first=right, second=left, near=near)
-    fwd, sides, adj_core = tie((fwd, sides, adj_core))
+    fwd, = apply(False, fields=[*x_pieces, x_here, x_there], first=right, second=left, near=near)
+    fwd, sides, adj_core, given[0] = tie((fwd, sides, adj_core, given[0]))
 
     def own_sum(field, core_part, m):
         k = m // 2
@@ -336,8 +345,8 @@
         PAR_DEV * groups * members // near_blocks.shape[-1], near_blocks.shape[-1],
     )
     ring = round_ring(side)
-    own = [moved(own_sum(adj, adj_core, m).astype(jnp.bfloat16), 0, m) for m in evens if m]
-    over = [moved(own_sum(fwd, fwd_core, m).astype(jnp.bfloat16), 0, m) for m in evens if m]
+    own = [moved(own_sum(adj, adj_core, m).astype(jnp.bfloat16), 0, m) for m in evens[1:]]
+    over = [moved(own_sum(fwd, fwd_core, m).astype(jnp.bfloat16), 0, m) for m in evens[1:]]
     ring, over = tie((ring, over))
     ring_core = moved(ring[:, part:], 0, 1)
     forward_field, adjoint_field, grad = finish(

time: 59 us -> 57.1 us (0.968)
  waiting for transfers between devices: 16.9 us -> 12.8 us
  starting transfers between devices: 14.9 us -> 17.4 us
    ppermute x16, waiting for transfers between devices: 9.95 us -> 6.51 us  [moved(): return lax.ppermute(x, AXES, pairs)]
    ppermute x3, starting transfers between devices: 3.75 us -> 5.94 us  [round_ring(): return lax.ppermute(x, AXES, pairs)]
    ppermute x3, waiting for transfers between devices: 6.94 us -> 6.31 us  [round_ring(): return lax.ppermute(x, AXES, pairs)]
  transfers between devices with their start and end apart: 19 -> 19, of which waited for: 10 -> 8; matrix products, arithmetic and copies ran while one was open for 2% -> 1% of each run, Pallas kernels for 19% -> 19%
where the time goes in v5:
time: 57.1 us; the launch traced here: 57 us
  starting transfers between devices  17.4 us (30%)
  Pallas kernels  13 us (23%)
  waiting for transfers between devices  12.8 us (22%)
  blocking collectives  11.8 us (21%)
  other arithmetic  0.96 us (2%)
  between operations  0.85 us (1%)
    all_to_all x1, blocking collectives, shards(): lax.all_to_all(grad.reshape(devices, PAR_DEV), AXES, 0, 0, tiled=True)  11.8 us
    ppermute x16, starting transfers between devices, moved(): return lax.ppermute(x, AXES, pairs)  11.4 us
    pallas_call x2, Pallas kernels, apply_blocks(): pl.pallas_call(functools.partial(block_kernel, transposed, total, members...  6.79 us
    ppermute x16, waiting for transfers between devices, moved(): return lax.ppermute(x, AXES, pairs)  6.51 us
    ppermute x3, waiting for transfers between devices, round_ring(): return lax.ppermute(x, AXES, pairs)  6.31 us
    ppermute x3, starting transfers between devices, round_ring(): return lax.ppermute(x, AXES, pairs)  5.94 us
    pallas_call x1, Pallas kernels, loaded(): pl.pallas_call(functools.partial(load_kernel, LOADS), in_specs=[pl.BlockS...  2.87 us
    pallas_call x1, Pallas kernels, finish(): pl.pallas_call(functools.partial(final_kernel, column_total, len(fwd_term...  2.11 us
  transfers between devices with their start and end apart: 19, of which 8 were waited for; matrix products, arithmetic and copies ran while one was open for 1% of the time, Pallas kernels for 19%

profile of v5, /device:TPU:0, one launch (start us, length us, event | category | flops | bytes accessed | tf_op | source)
XLA Modules:
  0.0 57.0 jit_solution(4756349093077388324)
XLA Ops:
  0.6 0.0 copy-start.1
  0.6 0.0 copy-start.6
  0.7 0.0 copy-start.7
  0.7 0.0 copy-start.5
  0.7 0.5 collective-permute-start.3
  1.2 2.6 %collective-permute-start.4 = (bf16[32,8,256]{2,1,0:T(8,128)(2,1)}, bf16[32,8,256]{2,1,0:T(8,128)(2,1)S(1)}, u32[]{:S(2)}, u32[]{:S(2)}) collective-permute-start(bf16[32,8,256]{2,1,0:T(8,128)(2,1)} %refs_3_.1), channel_id=1, source_target_pairs={{0,4},{1,29},{2,6},{3,31},{4,8},{5,1},{6,10},{7,3},{8,12},{9,5},{1... | collective-permute-start | bytes 393224 | tf_op jit(solution)/shard_map/ppermute | solution.py:34
  3.7 0.0 collective-permute-done.3.refs_4_
  3.7 1.5 %collective-permute-start.5 = (bf16[32,8,256]{2,1,0:T(8,128)(2,1)S(1)}, bf16[32,8,256]{2,1,0:T(8,128)(2,1)S(1)}, u32[]{:S(2)}, u32[]{:S(2)}) collective-permute-start(bf16[32,8,256]{2,1,0:T(8,128)(2,1)S(1)} %collective-permute-done.3.refs_4_), channel_id=1, source_target_pairs={{0,4},{1,29},{2,6},{3,31},{4,8},{5,1},{6,10},{7,3},{8,12},{9,5},{1... | collective-permute-start | bytes 393224 | tf_op jit(solution)/shard_map/ppermute | solution.py:34
  5.3 1.5 %collective-permute-start.6 = (bf16[32,8,256]{2,1,0:T(8,128)(2,1)}, bf16[32,8,256]{2,1,0:T(8,128)(2,1)S(1)}, u32[]{:S(2)}, u32[]{:S(2)}) collective-permute-start(bf16[32,8,256]{2,1,0:T(8,128)(2,1)} %refs_3_.1), channel_id=1, source_target_pairs={{0,2},{1,3},{2,0},{3,1},{4,6},{5,7},{6,4},{7,5},{8,10},{9,11},{10,... | collective-permute-start | bytes 393224 | tf_op jit(solution)/shard_map/ppermute | solution.py:24
  6.8 0.5 collective-permute-start.1
  7.3 2.9 %shard_map.130 = (bf16[128,2,32,128]{3,2,1,0:T(8,128)(2,1)S(1)}, bf16[128,2,32,128]{3,2,1,0:T(8,128)(2,1)S(1)}, bf16[32,2,128,128]{3,2,1,0:T(8,128)(2,1)S(1)}) custom-call(bf16[128,2,32,128]{3,2,1,0:T(8,128)(2,1)} %refs_0_.3, bf16[128,2,32,128]{3,2,1,0:T(8,128)(2,1)} %refs_1_.3, bf16[32,2,128,128]{3,2,1,0:T(8,128)(2,1)} %refs_2_.3), custom_call_target="tpu_custom_call" | custom-call | bytes 12000000 | tf_op jit(solution)/shard_map/pallas_call | solution.py:182
  10.2 0.0 collective-permute-done.4
  10.2 1.3 %collective-permute-done.5 = bf16[32,8,256]{2,1,0:T(8,128)(2,1)S(1)} collective-permute-done((bf16[32,8,256]{2,1,0:T(8,128)(2,1)S(1)}, bf16[32,8,256]{2,1,0:T(8,128)(2,1)S(1)}, u32[]{:S(2)}, u32[]{:S(2)}) %collective-permute-start.5) | collective-permute-done | bytes 131104 | tf_op jit(solution)/shard_map/ppermute | solution.py:34
  11.5 0.0 collective-permute-done.6.refs_5_
  11.5 1.7 %collective-permute-start.8 = (bf16[64,8,256]{2,1,0:T(8,128)(2,1)S(1)}, bf16[64,8,256]{2,1,0:T(8,128)(2,1)S(1)}, u32[]{:S(2)}, u32[]{:S(2)}) collective-permute-start(bf16[64,8,256]{2,1,0:T(8,128)(2,1)S(1)} %pad_maximum_fusion.2), channel_id=1, source_target_pairs={{0,2},{1,3},{2,0},{3,1},{4,6},{5,7},{6,4},{7,5},{8,10},{9,11},{10,... | collective-permute-start | bytes 786440 | tf_op jit(solution)/shard_map/ppermute | solution.py:24
  13.3 0.0 copy-done.1
  13.3 1.1 %collective-permute-start = (bf16[32,8,256]{2,1,0:T(8,128)(2,1)S(1)}, bf16[32,8,256]{2,1,0:T(8,128)(2,1)S(1)}, u32[]{:S(2)}, u32[]{:S(2)}) collective-permute-start(bf16[32,8,256]{2,1,0:T(8,128)(2,1)S(1)} %copy-done.1), channel_id=1, source_target_pairs={{0,1},{1,0},{2,3},{3,2},{4,5},{5,4},{6,7},{7,6},{8,9},{9,8},{10,11... | collective-permute-start | bytes 393224 | tf_op jit(solution)/shard_map/ppermute | solution.py:24
  14.3 0.0 collective-permute-done.1.refs_5_
  14.4 0.3 collective-permute-start.2
  14.6 0.2 collective-permute-start.7
  14.9 0.5 collective-permute-done.refs_4_
  15.3 0.4 collective-permute-done.2.refs_6_
  15.7 0.3 collective-permute-done.7.refs_6_
  16.0 0.0 copy-done.6
  16.0 0.0 copy-done.7
  16.0 0.0 copy-done.5
  16.0 3.4 %shard_map.131 = (f32[96,64,128]{2,1,0:T(8,128)S(1)}, bf16[32,32,128]{2,1,0:T(8,128)(2,1)S(1)}, bf16[32,32,128]{2,1,0:T(8,128)(2,1)S(1)}) custom-call(s32[2,128]{1,0:T(2,128)S(1)} %copy-done.5, s32[128]{0:T(128)S(1)} %copy-done.7, s32[2,32]{1,0:T(2,128)S(1)} %copy-done.6, bf16[32,8,256]{2,1,0:T(8,128)(2,1)S(1)} %copy-done.1, ...), custom_call_target="tpu_custom_call" | custom-call | flops 671088640 | bytes 20000000 | tf_op jit(solution)/shard_map/pallas_call | solution.py:147
  19.4 0.7 %collective-permute-done.8 = bf16[64,8,256]{2,1,0:T(8,128)(2,1)S(1)} collective-permute-done((bf16[64,8,256]{2,1,0:T(8,128)(2,1)S(1)}, bf16[64,8,256]{2,1,0:T(8,128)(2,1)S(1)}, u32[]{:S(2)}, u32[]{:S(2)}) %collective-permute-start.8) | collective-permute-done | bytes 262176 | tf_op jit(solution)/shard_map/ppermute | solution.py:24
  20.1 0.5 collective-permute-start.9
  20.7 0.1 collective-permute-start.10
  20.8 1.4 %collective-permute-done.9.refs_8_ = bf16[128,8,256]{2,1,0:T(8,128)(2,1)S(1)} collective-permute-done((bf16[128,8,256]{2,1,0:T(8,128)(2,1)S(1)}, bf16[128,8,256]{2,1,0:T(8,128)(2,1)S(1)}, u32[]{:S(2)}, u32[]{:S(2)}) %collective-permute-start.9) | collective-permute-done | bytes 524320 | tf_op jit(solution)/shard_map/ppermute | solution.py:24
  22.2 0.1 pad_maximum_fusion
  22.3 0.4 collective-permute-start.12
  22.7 0.1 collective-permute-start.13
  22.9 0.0 collective-permute-done.10
  22.9 0.1 add_convert_fusion.1
  22.9 2.0 %collective-permute-start.11 = (bf16[32,32,128]{2,1,0:T(8,128)(2,1)S(1)}, bf16[32,32,128]{2,1,0:T(8,128)(2,1)S(1)}, u32[]{:S(2)}, u32[]{:S(2)}) collective-permute-start(bf16[32,32,128]{2,1,0:T(8,128)(2,1)S(1)} %add_convert_fusion.1), channel_id=1, source_target_pairs={{0,2},{1,3},{2,0},{3,1},{4,6},{5,7},{6,4},{7,5},{8,10},{9,11},{10,... | collective-permute-start | bytes 786440 | tf_op jit(solution)/shard_map/ppermute | solution.py:24
  24.9 0.0 copy-done
  24.9 3.4 %shard_map.132.refs_0_ = f32[32,64,128]{2,1,0:T(8,128)S(1)} custom-call(s32[2,128]{1,0:T(2,128)S(1)} %copy-done.5, s32[128]{0:T(128)S(1)} %copy-done.7, s32[2,32]{1,0:T(2,128)S(1)} %copy-done.6, bf16[32,8,256]{2,1,0:T(8,128)(2,1)S(1)} %copy-done, bf16[32,8,256]{2,1,0:T(8,128)(2,1)S(1)} %collective-permute-done.3.refs_4_, ...), custom_call_target="tpu_custom_call" | custom-call | flops 671088640 | bytes 20000000 | tf_op jit(solution)/shard_map/pallas_call | solution.py:147
  28.3 0.0 collective-permute-done.13
  28.3 3.3 %collective-permute-done.11 = bf16[32,32,128]{2,1,0:T(8,128)(2,1)S(1)} collective-permute-done((bf16[32,32,128]{2,1,0:T(8,128)(2,1)S(1)}, bf16[32,32,128]{2,1,0:T(8,128)(2,1)S(1)}, u32[]{:S(2)}, u32[]{:S(2)}) %collective-permute-start.11) | collective-permute-done | bytes 262176 | tf_op jit(solution)/shard_map/ppermute | solution.py:24
  31.6 0.0 collective-permute-done.12.refs_4_
  31.6 0.0 copy-start.2
  31.7 0.0 copy-start.3
  31.7 0.0 copy-start.4
  31.7 0.1 pad_maximum_fusion.1
  31.7 0.1 collective-permute-start.14
  31.8 0.1 add_convert_fusion
  32.0 1.8 %collective-permute-start.15 = (bf16[32,32,128]{2,1,0:T(8,128)(2,1)S(1)}, bf16[32,32,128]{2,1,0:T(8,128)(2,1)S(1)}, u32[]{:S(2)}, u32[]{:S(2)}) collective-permute-start(bf16[32,32,128]{2,1,0:T(8,128)(2,1)S(1)} %add_convert_fusion), channel_id=1, source_target_pairs={{0,4},{1,29},{2,6},{3,31},{4,8},{5,1},{6,10},{7,3},{8,12},{9,5},{1... | collective-permute-start | bytes 786440 | tf_op jit(solution)/shard_map/ppermute | solution.py:34
  33.8 0.0 collective-permute-done.14.refs_1_
  33.8 1.7 %collective-permute-start.16 = (bf16[32,16,128]{2,1,0:T(8,128)(2,1)S(1)}, bf16[32,16,128]{2,1,0:T(8,128)(2,1)S(1)}, u32[]{:S(2)}, u32[]{:S(2)}) collective-permute-start(bf16[32,16,128]{2,1,0:T(8,128)(2,1)S(1)} %fusion), channel_id=1, source_target_pairs={{0,2},{1,3},{2,0},{3,1},{4,6},{5,7},{6,4},{7,5},{8,10},{9,11},{10,... | collective-permute-start | bytes 393224 | tf_op jit(solution)/shard_map/ppermute | solution.py:24
  35.5 0.5 collective-permute-start.17
  36.0 5.1 %collective-permute-done.15.refs_6_ = bf16[32,32,128]{2,1,0:T(8,128)(2,1)S(1)} collective-permute-done((bf16[32,32,128]{2,1,0:T(8,128)(2,1)S(1)}, bf16[32,32,128]{2,1,0:T(8,128)(2,1)S(1)}, u32[]{:S(2)}, u32[]{:S(2)}) %collective-permute-start.15) | collective-permute-done | bytes 262176 | tf_op jit(solution)/shard_map/ppermute | solution.py:34
  41.1 0.0 collective-permute-done.16.refs_2_
  41.1 0.1 collective-permute-start.18
  41.2 0.0 copy-done.2
  41.2 0.0 copy-done.3
  41.2 0.0 copy-done.4
  41.2 1.3 %shard_map.133 = (f32[32,16384]{1,0:T(8,128)S(1)}, bf16[128,16384]{1,0:T(8,128)(2,1)S(1)}) custom-call(s32[4,4096]{1,0:T(4,128)S(1)} %copy-done.2, f32[4,4096]{1,0:T(4,128)S(1)} %copy-done.3, s32[1,4096]{1,0:T(1,128)S(1)} %bitcast.4), custom_call_target="tpu_custom_call" | custom-call | bytes 8000000 | tf_op jit(solution)/shard_map/pallas_call | solution.py:215
  42.5 0.0 collective-permute-done.17.refs_5_
  42.5 0.0 collective-permute-done.18.refs_7_
  42.5 2.1 %shard_map.134 = (f32[32,8,256]{2,1,0:T(8,128)}, f32[32,8,256]{2,1,0:T(8,128)}, f32[32,128]{1,0:T(8,128)S(1)}) custom-call(f32[32,64,128]{2,1,0:T(8,128)S(1)} %shard_map.132.refs_0_, f32[32,32,128]{2,1,0:T(8,128)S(1)} %collective-permute-done.14.refs_1_, bf16[32,16,128]{2,1,0:T(8,128)(2,1)S(1)} %collective-permute-done.16.refs_2_, ...), custom_call_target="tpu_custom_call" | custom-call | flops 200000000 | bytes 3000000 | tf_op jit(solution)/shard_map/pallas_call | solution.py:260
  44.6 11.8 %all_to_all.9 = f32[32,1,128]{2,1,0:T(1,128)S(1)} all-to-all(f32[32,1,128]{2,1,0:T(1,128)S(1)} %bitcast.5), channel_id=1, replica_groups=mesh['clus'=8,'sub'=4] {'clus','sub'}, dimensions={0} | all-to-all | bytes 32768 | tf_op jit(solution)/shard_map/all_to_all | solution.py:356
  56.4 0.6 reduce_sum.9
  (9 shorter events, 0.2 us)
Async XLA Ops:
  0.6 12.6 %copy-start.1 = (bf16[32,8,256]{2,1,0:T(8,128)(2,1)S(1)}, bf16[32,8,256]{2,1,0:T(8,128)(2,1)}, u32[]{:S(2)}) copy-start(bf16[32,8,256]{2,1,0:T(8,128)(2,1)} %refs_3_) | copy-start | bytes 393220
  0.6 15.3 %copy-start.6 = (s32[2,32]{1,0:T(2,128)S(1)}, s32[2,32]{1,0:T(2,128)}, u32[]{:S(2)}) copy-start(s32[2,32]{1,0:T(2,128)} %refs_2_.5) | copy-start | bytes 772
  0.7 15.3 %copy-start.7 = (s32[128]{0:T(128)S(1)}, s32[128]{0:T(128)}, u32[]{:S(2)}) copy-start(s32[128]{0:T(128)} %refs_1_.5) | copy-start | bytes 1540
  0.7 15.3 %copy-start.5 = (s32[2,128]{1,0:T(2,128)S(1)}, s32[2,128]{1,0:T(2,128)}, u32[]{:S(2)}) copy-start(s32[2,128]{1,0:T(2,128)} %refs_0_.5) | copy-start | bytes 3076
  0.7 3.1 %collective-permute-start.3 = (bf16[32,8,256]{2,1,0:T(8,128)(2,1)}, bf16[32,8,256]{2,1,0:T(8,128)(2,1)S(1)}, u32[]{:S(2)}, u32[]{:S(2)}) collective-permute-start(bf16[32,8,256]{2,1,0:T(8,128)(2,1)} %refs_3_.1), channel_id=1, source_target_pairs={{0,1},{1,0},{2,3},{3,2},{4,5},{5,4},{6,7},{7,6},{8,9},{9,8},{10,11... | collective-permute-start | bytes 393224 | tf_op jit(solution)/shard_map/ppermute | solution.py:24
  1.2 9.0 %collective-permute-start.4 = (bf16[32,8,256]{2,1,0:T(8,128)(2,1)}, bf16[32,8,256]{2,1,0:T(8,128)(2,1)S(1)}, u32[]{:S(2)}, u32[]{:S(2)}) collective-permute-start(bf16[32,8,256]{2,1,0:T(8,128)(2,1)} %refs_3_.1), channel_id=1, source_target_pairs={{0,4},{1,29},{2,6},{3,31},{4,8},{5,1},{6,10},{7,3},{8,12},{9,5},{1... | collective-permute-start | bytes 393224 | tf_op jit(solution)/shard_map/ppermute | solution.py:34
  3.7 7.7 %collective-permute-start.5 = (bf16[32,8,256]{2,1,0:T(8,128)(2,1)S(1)}, bf16[32,8,256]{2,1,0:T(8,128)(2,1)S(1)}, u32[]{:S(2)}, u32[]{:S(2)}) collective-permute-start(bf16[32,8,256]{2,1,0:T(8,128)(2,1)S(1)} %collective-permute-done.3.refs_4_), channel_id=1, source_target_pairs={{0,4},{1,29},{2,6},{3,31},{4,8},{5,1},{6,10},{7,3},{8,12},{9,5},{1... | collective-permute-start | bytes 393224 | tf_op jit(solution)/shard_map/ppermute | solution.py:34
  5.3 6.2 %collective-permute-start.6 = (bf16[32,8,256]{2,1,0:T(8,128)(2,1)}, bf16[32,8,256]{2,1,0:T(8,128)(2,1)S(1)}, u32[]{:S(2)}, u32[]{:S(2)}) collective-permute-start(bf16[32,8,256]{2,1,0:T(8,128)(2,1)} %refs_3_.1), channel_id=1, source_target_pairs={{0,2},{1,3},{2,0},{3,1},{4,6},{5,7},{6,4},{7,5},{8,10},{9,11},{10,... | collective-permute-start | bytes 393224 | tf_op jit(solution)/shard_map/ppermute | solution.py:24
  6.8 7.5 %collective-permute-start.1 = (bf16[32,8,256]{2,1,0:T(8,128)(2,1)}, bf16[32,8,256]{2,1,0:T(8,128)(2,1)S(1)}, u32[]{:S(2)}, u32[]{:S(2)}) collective-permute-start(bf16[32,8,256]{2,1,0:T(8,128)(2,1)} %refs_3_), channel_id=1, source_target_pairs={{0,2},{1,3},{2,0},{3,1},{4,6},{5,7},{6,4},{7,5},{8,10},{9,11},{10,... | collective-permute-start | bytes 393224 | tf_op jit(solution)/shard_map/ppermute | solution.py:24
  11.5 8.6 %collective-permute-start.8 = (bf16[64,8,256]{2,1,0:T(8,128)(2,1)S(1)}, bf16[64,8,256]{2,1,0:T(8,128)(2,1)S(1)}, u32[]{:S(2)}, u32[]{:S(2)}) collective-permute-start(bf16[64,8,256]{2,1,0:T(8,128)(2,1)S(1)} %pad_maximum_fusion.2), channel_id=1, source_target_pairs={{0,2},{1,3},{2,0},{3,1},{4,6},{5,7},{6,4},{7,5},{8,10},{9,11},{10,... | collective-permute-start | bytes 786440 | tf_op jit(solution)/shard_map/ppermute | solution.py:24
  13.3 2.1 %collective-permute-start = (bf16[32,8,256]{2,1,0:T(8,128)(2,1)S(1)}, bf16[32,8,256]{2,1,0:T(8,128)(2,1)S(1)}, u32[]{:S(2)}, u32[]{:S(2)}) collective-permute-start(bf16[32,8,256]{2,1,0:T(8,128)(2,1)S(1)} %copy-done.1), channel_id=1, source_target_pairs={{0,1},{1,0},{2,3},{3,2},{4,5},{5,4},{6,7},{7,6},{8,9},{9,8},{10,11... | collective-permute-start | bytes 393224 | tf_op jit(solution)/shard_map/ppermute | solution.py:24
  14.4 1.3 %collective-permute-start.2 = (bf16[32,8,256]{2,1,0:T(8,128)(2,1)S(1)}, bf16[32,8,256]{2,1,0:T(8,128)(2,1)S(1)}, u32[]{:S(2)}, u32[]{:S(2)}) collective-permute-start(bf16[32,8,256]{2,1,0:T(8,128)(2,1)S(1)} %collective-permute-done.1.refs_5_), channel_id=1, source_target_pairs={{0,1},{1,0},{2,3},{3,2},{4,5},{5,4},{6,7},{7,6},{8,9},{9,8},{10,11... | collective-permute-start | bytes 393224 | tf_op jit(solution)/shard_map/ppermute | solution.py:24
  14.6 1.3 %collective-permute-start.7 = (bf16[32,8,256]{2,1,0:T(8,128)(2,1)S(1)}, bf16[32,8,256]{2,1,0:T(8,128)(2,1)S(1)}, u32[]{:S(2)}, u32[]{:S(2)}) collective-permute-start(bf16[32,8,256]{2,1,0:T(8,128)(2,1)S(1)} %collective-permute-done.6.refs_5_), channel_id=1, source_target_pairs={{0,1},{1,0},{2,3},{3,2},{4,5},{5,4},{6,7},{7,6},{8,9},{9,8},{10,11... | collective-permute-start | bytes 393224 | tf_op jit(solution)/shard_map/ppermute | solution.py:24
  20.1 4.8 %copy-start = (bf16[32,8,256]{2,1,0:T(8,128)(2,1)S(1)}, bf16[32,8,256]{2,1,0:T(8,128)(2,1)}, u32[]{:S(2)}) copy-start(bf16[32,8,256]{2,1,0:T(8,128)(2,1)} %refs_3_.1) | copy-start | bytes 393220
  20.1 2.1 %collective-permute-start.9 = (bf16[128,8,256]{2,1,0:T(8,128)(2,1)S(1)}, bf16[128,8,256]{2,1,0:T(8,128)(2,1)S(1)}, u32[]{:S(2)}, u32[]{:S(2)}) collective-permute-start(bf16[128,8,256]{2,1,0:T(8,128)(2,1)S(1)} %constant_dynamic-update-slice_fusion.refs_7_), channel_id=1, source_target_pairs={{0,1},{1,0},{2,3},{3,2},{4,5},{5,4},{6,7},{7,6},{8,9},{9,8},{10,11... | collective-permute-start | bytes 1572872 | tf_op jit(solution)/shard_map/ppermute | solution.py:24
  20.7 2.2 %collective-permute-start.10 = (bf16[32,32,128]{2,1,0:T(8,128)(2,1)S(1)}, bf16[32,32,128]{2,1,0:T(8,128)(2,1)S(1)}, u32[]{:S(2)}, u32[]{:S(2)}) collective-permute-start(bf16[32,32,128]{2,1,0:T(8,128)(2,1)S(1)} %get-tuple-element.60), channel_id=1, source_target_pairs={{0,1},{1,0},{2,3},{3,2},{4,5},{5,4},{6,7},{7,6},{8,9},{9,8},{10,11... | collective-permute-start | bytes 786440 | tf_op jit(solution)/shard_map/ppermute | solution.py:24
  22.3 9.3 %collective-permute-start.12 = (f32[32,32,128]{2,1,0:T(8,128)S(1)}, f32[32,32,128]{2,1,0:T(8,128)S(1)}, u32[]{:S(2)}, u32[]{:S(2)}) collective-permute-start(f32[32,32,128]{2,1,0:T(8,128)S(1)} %pad_maximum_fusion), channel_id=1, source_target_pairs={{0,1},{1,0},{2,3},{3,2},{4,5},{5,4},{6,7},{7,6},{8,9},{9,8},{10,11... | collective-permute-start | bytes 1572872 | tf_op jit(solution)/shard_map/ppermute | solution.py:24
  22.7 5.6 %collective-permute-start.13 = (bf16[32,32,128]{2,1,0:T(8,128)(2,1)S(1)}, bf16[32,32,128]{2,1,0:T(8,128)(2,1)S(1)}, u32[]{:S(2)}, u32[]{:S(2)}) collective-permute-start(bf16[32,32,128]{2,1,0:T(8,128)(2,1)S(1)} %get-tuple-element.63), channel_id=1, source_target_pairs={{0,1},{1,0},{2,3},{3,2},{4,5},{5,4},{6,7},{7,6},{8,9},{9,8},{10,11... | collective-permute-start | bytes 786440 | tf_op jit(solution)/shard_map/ppermute | solution.py:24
  22.9 8.7 %collective-permute-start.11 = (bf16[32,32,128]{2,1,0:T(8,128)(2,1)S(1)}, bf16[32,32,128]{2,1,0:T(8,128)(2,1)S(1)}, u32[]{:S(2)}, u32[]{:S(2)}) collective-permute-start(bf16[32,32,128]{2,1,0:T(8,128)(2,1)S(1)} %add_convert_fusion.1), channel_id=1, source_target_pairs={{0,2},{1,3},{2,0},{3,1},{4,6},{5,7},{6,4},{7,5},{8,10},{9,11},{10,... | collective-permute-start | bytes 786440 | tf_op jit(solution)/shard_map/ppermute | solution.py:24
  31.6 9.6 %copy-start.2 = (s32[4,4096]{1,0:T(4,128)S(1)}, s32[4,4096]{1,0:T(4,128)}, u32[]{:S(2)}) copy-start(s32[4,4096]{1,0:T(4,128)} %params) | copy-start | bytes 196612
  31.7 9.6 %copy-start.3 = (f32[4,4096]{1,0:T(4,128)S(1)}, f32[4,4096]{1,0:T(4,128)}, u32[]{:S(2)}) copy-start(f32[4,4096]{1,0:T(4,128)} %weights.1) | copy-start | bytes 196612
  31.7 9.6 %copy-start.4 = (s32[4096]{0:T(1024)S(1)}, s32[4096]{0:T(1024)}, u32[]{:S(2)}) copy-start(s32[4096]{0:T(1024)} %param.21) | copy-start | bytes 49156
  31.7 2.1 %collective-permute-start.14 = (f32[32,32,128]{2,1,0:T(8,128)S(1)}, f32[32,32,128]{2,1,0:T(8,128)S(1)}, u32[]{:S(2)}, u32[]{:S(2)}) collective-permute-start(f32[32,32,128]{2,1,0:T(8,128)S(1)} %pad_maximum_fusion.1), channel_id=1, source_target_pairs={{0,1},{1,0},{2,3},{3,2},{4,5},{5,4},{6,7},{7,6},{8,9},{9,8},{10,11... | collective-permute-start | bytes 1572872 | tf_op jit(solution)/shard_map/ppermute | solution.py:24
  32.0 9.1 %collective-permute-start.15 = (bf16[32,32,128]{2,1,0:T(8,128)(2,1)S(1)}, bf16[32,32,128]{2,1,0:T(8,128)(2,1)S(1)}, u32[]{:S(2)}, u32[]{:S(2)}) collective-permute-start(bf16[32,32,128]{2,1,0:T(8,128)(2,1)S(1)} %add_convert_fusion), channel_id=1, source_target_pairs={{0,4},{1,29},{2,6},{3,31},{4,8},{5,1},{6,10},{7,3},{8,12},{9,5},{1... | collective-permute-start | bytes 786440 | tf_op jit(solution)/shard_map/ppermute | solution.py:34
  33.8 7.2 %collective-permute-start.16 = (bf16[32,16,128]{2,1,0:T(8,128)(2,1)S(1)}, bf16[32,16,128]{2,1,0:T(8,128)(2,1)S(1)}, u32[]{:S(2)}, u32[]{:S(2)}) collective-permute-start(bf16[32,16,128]{2,1,0:T(8,128)(2,1)S(1)} %fusion), channel_id=1, source_target_pairs={{0,2},{1,3},{2,0},{3,1},{4,6},{5,7},{6,4},{7,5},{8,10},{9,11},{10,... | collective-permute-start | bytes 393224 | tf_op jit(solution)/shard_map/ppermute | solution.py:24
  35.5 7.0 %collective-permute-start.17 = (bf16[32,16,128]{2,1,0:T(8,128)(2,1)S(1)}, bf16[32,16,128]{2,1,0:T(8,128)(2,1)S(1)}, u32[]{:S(2)}, u32[]{:S(2)}) collective-permute-start(bf16[32,16,128]{2,1,0:T(8,128)(2,1)S(1)} %add_convert_fusion.2), channel_id=1, source_target_pairs={{0,2},{1,3},{2,0},{3,1},{4,6},{5,7},{6,4},{7,5},{8,10},{9,11},{10,... | collective-permute-start | bytes 393224 | tf_op jit(solution)/shard_map/ppermute | solution.py:24
  41.1 1.4 %collective-permute-start.18 = (bf16[32,16,128]{2,1,0:T(8,128)(2,1)S(1)}, bf16[32,16,128]{2,1,0:T(8,128)(2,1)S(1)}, u32[]{:S(2)}, u32[]{:S(2)}) collective-permute-start(bf16[32,16,128]{2,1,0:T(8,128)(2,1)S(1)} %slice.47), channel_id=1, source_target_pairs={{0,1},{1,0},{2,3},{3,2},{4,5},{5,4},{6,7},{7,6},{8,9},{9,8},{10,11... | collective-permute-start | bytes 393224 | tf_op jit(solution)/shard_map/ppermute | solution.py:24

commit v6 on v5

--- a/solution.py
+++ b/solution.py
@@ -24,10 +24,10 @@
     return lax.ppermute(x, AXES, pairs)
 
 
-def round_ring(x):
+def round_ring(x, mask=0):
     groups, members = lax.axis_size("clus"), lax.axis_size("sub")
     pairs = [
-        (g * members + s, ((g + 1 - 2 * (s % 2)) % groups) * members + s)
+        (g * members + s, ((g + 1 - 2 * (s % 2)) % groups) * members + (s ^ mask))
         for g in range(groups)
         for s in range(members)
     ]
@@ -228,17 +228,19 @@
 def final_kernel(column_total, n_fwd, n_adj, *refs):
     fwd_terms = refs[:n_fwd]
     adj_terms = refs[n_fwd : n_fwd + n_adj]
-    spread, places, fwd_out, adj_out, grad, scaled = refs[n_fwd + n_adj :]
+    spread, places, fwd_out, adj_out, grad, scaled, fwd_held, adj_held, sems = refs[n_fwd + n_adj :]
     clusters, height, _ = fwd_out.shape
     high, width = grad.shape
     entries = spread.shape[1] // clusters
     slots = entries // width
+    chunk = clusters // LOADS
+    copies = []
     for c in range(clusters):
         fwd = sum(t[c, : 2 * height].astype(jnp.float32) for t in fwd_terms)
         adj = sum(t[c, : 2 * height].astype(jnp.float32) for t in adj_terms)
-        for out, value in ((fwd_out, fwd), (adj_out, adj)):
-            out[c, :, :width] = value[:height]
-            out[c, :, width:] = value[height:]
+        for held, value in ((fwd_held, fwd), (adj_held, adj)):
+            held[c, :, :width] = value[:height]
+            held[c, :, width:] = value[height:]
         product = fwd * adj
         sens = jnp.sum(product[:height] - product[height:], axis=0, keepdims=True) / column_total
         at = slice(c * entries, (c + 1) * entries)
@@ -246,10 +248,18 @@
         top = value.astype(jnp.bfloat16)
         scaled[:high, at] = top
         scaled[high:, at] = (value - top.astype(jnp.float32)).astype(jnp.bfloat16)
+        if (c + 1) % chunk == 0:
+            k = c // chunk
+            part = pl.ds(k * chunk, chunk)
+            for i, (held, out) in enumerate(((fwd_held, fwd_out), (adj_held, adj_out))):
+                copies.append(pltpu.make_async_copy(held.at[part], out.at[part], sems.at[i, k]))
+                copies[-1].start()
     got = lax.dot_general(
-        scaled[...], places[...], (((1,), (1,)), ((), ())), preferred_element_type=jnp.float32
-    )
-    grad[...] = got[:high] + got[high:]
+        places[...], scaled[...], (((1,), (1,)), ((), ())), preferred_element_type=jnp.float32
+    )
+    grad[...] = jnp.transpose(got[:, :high] + got[:, high:])
+    for copy in copies:
+        copy.wait()
 
 
 def finish(column_total, shape, fwd_terms, adj_terms, spread, places):
@@ -260,9 +270,14 @@
     return pl.pallas_call(
         functools.partial(final_kernel, column_total, len(fwd_terms), len(adj_terms)),
         in_specs=[vmem] * (len(terms) + 2),
-        out_specs=[vmem] * 3,
+        out_specs=[pl.BlockSpec(memory_space=pl.ANY)] * 2 + [vmem],
         out_shape=[field, field, jax.ShapeDtypeStruct((high, width), jnp.float32)],
-        scratch_shapes=[pltpu.VMEM((2 * high, spread.shape[1]), jnp.bfloat16)],
+        scratch_shapes=[
+            pltpu.VMEM((2 * high, spread.shape[1]), jnp.bfloat16),
+            pltpu.VMEM(shape, jnp.float32),
+            pltpu.VMEM(shape, jnp.float32),
+            pltpu.SemaphoreType.DMA((2, LOADS)),
+        ],
         compiler_params=pltpu.CompilerParams(vmem_limit_bytes=VMEM_BYTES),
         cost_estimate=pl.CostEstimate(flops=200_000_000, bytes_accessed=3_000_000, transcendentals=0),
     )(*terms, spread, places)
@@ -344,13 +359,11 @@
         panel_params, panel_weights, panel_counts[None, :],
         PAR_DEV * groups * members // near_blocks.shape[-1], near_blocks.shape[-1],
     )
-    ring = round_ring(side)
+    ring = [round_ring(side[:, k * part : (k + 1) * part], k) for k in range(2)]
     own = [moved(own_sum(adj, adj_core, m).astype(jnp.bfloat16), 0, m) for m in evens[1:]]
     over = [moved(own_sum(fwd, fwd_core, m).astype(jnp.bfloat16), 0, m) for m in evens[1:]]
-    ring, over = tie((ring, over))
-    ring_core = moved(ring[:, part:], 0, 1)
     forward_field, adjoint_field, grad = finish(
-        column_total, forward_rhs.shape, [fwd, fwd_core, *over], [adj, adj_core, *own, ring, ring_core], spread, places
+        column_total, forward_rhs.shape, [fwd, fwd_core, *over], [adj, adj_core, *own, *ring], spread, places
     )
     devices = groups * members
     pieces = lax.all_to_all(grad.reshape(devices, PAR_DEV), AXES, 0, 0, tiled=True)

time: 57.1 us -> 56.3 us (0.986)
  blocking collectives: 11.8 us -> 10.5 us
    all_to_all x1, blocking collectives: 11.8 us -> 10.5 us  [shards(): lax.all_to_all(grad.reshape(devices, PAR_DEV), AXES, 0, 0, tiled=True)]
    ppermute x16 -> x15, waiting for transfers between devices: 6.51 us -> 6.93 us  [moved(): return lax.ppermute(x, AXES, pairs)]
    ppermute x16 -> x15, starting transfers between devices: 11.4 us -> 11.5 us  [moved(): return lax.ppermute(x, AXES, pairs)]
    ppermute x3 -> x4, starting transfers between devices: 5.94 us -> 5.96 us  [round_ring(): return lax.ppermute(x, AXES, pairs)]
    ppermute x3 -> x4, waiting for transfers between devices: 6.31 us -> 6.29 us  [round_ring(): return lax.ppermute(x, AXES, pairs)]
  transfers between devices with their start and end apart: 19 -> 19, of which waited for: 8 -> 10; matrix products, arithmetic and copies ran while one was open for 1% -> 1% of each run, Pallas kernels for 19% -> 19%
where the time goes in v6:
time: 56.3 us; the launch traced here: 56.1 us
  starting transfers between devices  17.4 us (31%)
  waiting for transfers between devices  13.2 us (23%)
  Pallas kernels  13 us (23%)
  blocking collectives  10.5 us (19%)
  other arithmetic  0.95 us (2%)
  between operations  0.85 us (2%)
    ppermute x15, starting transfers between devices, moved(): return lax.ppermute(x, AXES, pairs)  11.5 us
    all_to_all x1, blocking collectives, shards(): lax.all_to_all(grad.reshape(devices, PAR_DEV), AXES, 0, 0, tiled=True)  10.5 us
    ppermute x15, waiting for transfers between devices, moved(): return lax.ppermute(x, AXES, pairs)  6.93 us
    pallas_call x2, Pallas kernels, apply_blocks(): pl.pallas_call(functools.partial(block_kernel, transposed, total, members...  6.78 us
    ppermute x4, waiting for transfers between devices, round_ring(): return lax.ppermute(x, AXES, pairs)  6.29 us
    ppermute x4, starting transfers between devices, round_ring(): return lax.ppermute(x, AXES, pairs)  5.96 us
    pallas_call x1, Pallas kernels, loaded(): pl.pallas_call(functools.partial(load_kernel, LOADS), in_specs=[pl.BlockS...  2.87 us
    pallas_call x1, Pallas kernels, finish(): pl.pallas_call(functools.partial(final_kernel, column_total, len(fwd_term...  2.06 us
  transfers between devices with their start and end apart: 19, of which 10 were waited for; matrix products, arithmetic and copies ran while one was open for 1% of the time, Pallas kernels for 19%

profile of v6, /device:TPU:0, one launch (start us, length us, event | category | flops | bytes accessed | tf_op | source)
XLA Modules:
  0.0 56.1 jit_solution(9514400330638795738)
XLA Ops:
  0.6 0.0 copy-start.1
  0.6 0.0 copy-start.6
  0.7 0.0 copy-start.7
  0.7 0.0 copy-start.5
  0.7 0.5 collective-permute-start.3
  1.2 2.6 %collective-permute-start.4 = (bf16[32,8,256]{2,1,0:T(8,128)(2,1)}, bf16[32,8,256]{2,1,0:T(8,128)(2,1)S(1)}, u32[]{:S(2)}, u32[]{:S(2)}) collective-permute-start(bf16[32,8,256]{2,1,0:T(8,128)(2,1)} %refs_3_.1), channel_id=1, source_target_pairs={{0,4},{1,29},{2,6},{3,31},{4,8},{5,1},{6,10},{7,3},{8,12},{9,5},{1... | collective-permute-start | bytes 393224 | tf_op jit(solution)/shard_map/ppermute | solution.py:34
  3.7 0.0 collective-permute-done.3.refs_4_
  3.7 1.5 %collective-permute-start.5 = (bf16[32,8,256]{2,1,0:T(8,128)(2,1)S(1)}, bf16[32,8,256]{2,1,0:T(8,128)(2,1)S(1)}, u32[]{:S(2)}, u32[]{:S(2)}) collective-permute-start(bf16[32,8,256]{2,1,0:T(8,128)(2,1)S(1)} %collective-permute-done.3.refs_4_), channel_id=1, source_target_pairs={{0,4},{1,29},{2,6},{3,31},{4,8},{5,1},{6,10},{7,3},{8,12},{9,5},{1... | collective-permute-start | bytes 393224 | tf_op jit(solution)/shard_map/ppermute | solution.py:34
  5.3 1.5 %collective-permute-start.6 = (bf16[32,8,256]{2,1,0:T(8,128)(2,1)}, bf16[32,8,256]{2,1,0:T(8,128)(2,1)S(1)}, u32[]{:S(2)}, u32[]{:S(2)}) collective-permute-start(bf16[32,8,256]{2,1,0:T(8,128)(2,1)} %refs_3_.1), channel_id=1, source_target_pairs={{0,2},{1,3},{2,0},{3,1},{4,6},{5,7},{6,4},{7,5},{8,10},{9,11},{10,... | collective-permute-start | bytes 393224 | tf_op jit(solution)/shard_map/ppermute | solution.py:24
  6.8 0.5 collective-permute-start.1
  7.3 2.9 %shard_map.130 = (bf16[128,2,32,128]{3,2,1,0:T(8,128)(2,1)S(1)}, bf16[128,2,32,128]{3,2,1,0:T(8,128)(2,1)S(1)}, bf16[32,2,128,128]{3,2,1,0:T(8,128)(2,1)S(1)}) custom-call(bf16[128,2,32,128]{3,2,1,0:T(8,128)(2,1)} %refs_0_.3, bf16[128,2,32,128]{3,2,1,0:T(8,128)(2,1)} %refs_1_.3, bf16[32,2,128,128]{3,2,1,0:T(8,128)(2,1)} %refs_2_.3), custom_call_target="tpu_custom_call" | custom-call | bytes 12000000 | tf_op jit(solution)/shard_map/pallas_call | solution.py:182
  10.2 0.0 collective-permute-done.4
  10.2 1.3 %collective-permute-done.5 = bf16[32,8,256]{2,1,0:T(8,128)(2,1)S(1)} collective-permute-done((bf16[32,8,256]{2,1,0:T(8,128)(2,1)S(1)}, bf16[32,8,256]{2,1,0:T(8,128)(2,1)S(1)}, u32[]{:S(2)}, u32[]{:S(2)}) %collective-permute-start.5) | collective-permute-done | bytes 131104 | tf_op jit(solution)/shard_map/ppermute | solution.py:34
  11.5 0.0 collective-permute-done.6.refs_5_
  11.5 1.7 %collective-permute-start.8 = (bf16[64,8,256]{2,1,0:T(8,128)(2,1)S(1)}, bf16[64,8,256]{2,1,0:T(8,128)(2,1)S(1)}, u32[]{:S(2)}, u32[]{:S(2)}) collective-permute-start(bf16[64,8,256]{2,1,0:T(8,128)(2,1)S(1)} %pad_maximum_fusion.2), channel_id=1, source_target_pairs={{0,2},{1,3},{2,0},{3,1},{4,6},{5,7},{6,4},{7,5},{8,10},{9,11},{10,... | collective-permute-start | bytes 786440 | tf_op jit(solution)/shard_map/ppermute | solution.py:24
  13.3 0.0 copy-done.1
  13.3 1.1 %collective-permute-start = (bf16[32,8,256]{2,1,0:T(8,128)(2,1)S(1)}, bf16[32,8,256]{2,1,0:T(8,128)(2,1)S(1)}, u32[]{:S(2)}, u32[]{:S(2)}) collective-permute-start(bf16[32,8,256]{2,1,0:T(8,128)(2,1)S(1)} %copy-done.1), channel_id=1, source_target_pairs={{0,1},{1,0},{2,3},{3,2},{4,5},{5,4},{6,7},{7,6},{8,9},{9,8},{10,11... | collective-permute-start | bytes 393224 | tf_op jit(solution)/shard_map/ppermute | solution.py:24
  14.3 0.0 collective-permute-done.1.refs_5_
  14.4 0.3 collective-permute-start.2
  14.6 0.2 collective-permute-start.7
  14.9 0.5 collective-permute-done.refs_4_
  15.3 0.4 collective-permute-done.2.refs_6_
  15.7 0.3 collective-permute-done.7.refs_6_
  16.0 0.0 copy-done.6
  16.0 0.0 copy-done.7
  16.0 0.0 copy-done.5
  16.0 3.4 %shard_map.131 = (f32[96,64,128]{2,1,0:T(8,128)S(1)}, bf16[32,32,128]{2,1,0:T(8,128)(2,1)S(1)}, bf16[32,32,128]{2,1,0:T(8,128)(2,1)S(1)}) custom-call(s32[2,128]{1,0:T(2,128)S(1)} %copy-done.5, s32[128]{0:T(128)S(1)} %copy-done.7, s32[2,32]{1,0:T(2,128)S(1)} %copy-done.6, bf16[32,8,256]{2,1,0:T(8,128)(2,1)S(1)} %copy-done.1, ...), custom_call_target="tpu_custom_call" | custom-call | flops 671088640 | bytes 20000000 | tf_op jit(solution)/shard_map/pallas_call | solution.py:147
  19.4 0.7 %collective-permute-done.8 = bf16[64,8,256]{2,1,0:T(8,128)(2,1)S(1)} collective-permute-done((bf16[64,8,256]{2,1,0:T(8,128)(2,1)S(1)}, bf16[64,8,256]{2,1,0:T(8,128)(2,1)S(1)}, u32[]{:S(2)}, u32[]{:S(2)}) %collective-permute-start.8) | collective-permute-done | bytes 262176 | tf_op jit(solution)/shard_map/ppermute | solution.py:24
  20.1 0.5 collective-permute-start.9
  20.7 0.1 collective-permute-start.10
  20.8 1.4 %collective-permute-done.9.refs_8_ = bf16[128,8,256]{2,1,0:T(8,128)(2,1)S(1)} collective-permute-done((bf16[128,8,256]{2,1,0:T(8,128)(2,1)S(1)}, bf16[128,8,256]{2,1,0:T(8,128)(2,1)S(1)}, u32[]{:S(2)}, u32[]{:S(2)}) %collective-permute-start.9) | collective-permute-done | bytes 524320 | tf_op jit(solution)/shard_map/ppermute | solution.py:24
  22.2 0.1 pad_maximum_fusion
  22.3 0.4 collective-permute-start.12
  22.7 0.1 collective-permute-start.13
  22.9 0.0 collective-permute-done.10
  22.9 0.1 add_convert_fusion.1
  22.9 2.0 %collective-permute-start.11 = (bf16[32,32,128]{2,1,0:T(8,128)(2,1)S(1)}, bf16[32,32,128]{2,1,0:T(8,128)(2,1)S(1)}, u32[]{:S(2)}, u32[]{:S(2)}) collective-permute-start(bf16[32,32,128]{2,1,0:T(8,128)(2,1)S(1)} %add_convert_fusion.1), channel_id=1, source_target_pairs={{0,2},{1,3},{2,0},{3,1},{4,6},{5,7},{6,4},{7,5},{8,10},{9,11},{10,... | collective-permute-start | bytes 786440 | tf_op jit(solution)/shard_map/ppermute | solution.py:24
  24.9 0.0 copy-done
  24.9 3.4 %shard_map.132.refs_0_ = f32[32,64,128]{2,1,0:T(8,128)S(1)} custom-call(s32[2,128]{1,0:T(2,128)S(1)} %copy-done.5, s32[128]{0:T(128)S(1)} %copy-done.7, s32[2,32]{1,0:T(2,128)S(1)} %copy-done.6, bf16[32,8,256]{2,1,0:T(8,128)(2,1)S(1)} %copy-done, bf16[32,8,256]{2,1,0:T(8,128)(2,1)S(1)} %collective-permute-done.3.refs_4_, ...), custom_call_target="tpu_custom_call" | custom-call | flops 671088640 | bytes 20000000 | tf_op jit(solution)/shard_map/pallas_call | solution.py:147
  28.3 0.0 collective-permute-done.13
  28.3 3.3 %collective-permute-done.11 = bf16[32,32,128]{2,1,0:T(8,128)(2,1)S(1)} collective-permute-done((bf16[32,32,128]{2,1,0:T(8,128)(2,1)S(1)}, bf16[32,32,128]{2,1,0:T(8,128)(2,1)S(1)}, u32[]{:S(2)}, u32[]{:S(2)}) %collective-permute-start.11) | collective-permute-done | bytes 262176 | tf_op jit(solution)/shard_map/ppermute | solution.py:24
  31.6 0.0 collective-permute-done.12.refs_4_
  31.6 0.0 copy-start.2
  31.7 0.0 copy-start.3
  31.7 0.0 copy-start.4
  31.7 0.1 pad_maximum_fusion.1
  31.7 0.1 collective-permute-start.14
  31.8 0.1 add_convert_fusion
  32.0 1.8 %collective-permute-start.16 = (bf16[32,16,128]{2,1,0:T(8,128)(2,1)S(1)}, bf16[32,16,128]{2,1,0:T(8,128)(2,1)S(1)}, u32[]{:S(2)}, u32[]{:S(2)}) collective-permute-start(bf16[32,16,128]{2,1,0:T(8,128)(2,1)S(1)} %add_convert_fusion.2), channel_id=1, source_target_pairs={{0,2},{1,3},{2,0},{3,1},{4,6},{5,7},{6,4},{7,5},{8,10},{9,11},{10,... | collective-permute-start | bytes 393224 | tf_op jit(solution)/shard_map/ppermute | solution.py:24
  33.8 1.5 %collective-permute-start.18 = (bf16[32,16,128]{2,1,0:T(8,128)(2,1)S(1)}, bf16[32,16,128]{2,1,0:T(8,128)(2,1)S(1)}, u32[]{:S(2)}, u32[]{:S(2)}) collective-permute-start(bf16[32,16,128]{2,1,0:T(8,128)(2,1)S(1)} %get-tuple-element.77), channel_id=1, source_target_pairs={{0,5},{1,28},{2,7},{3,30},{4,9},{5,0},{6,11},{7,2},{8,13},{9,4},{1... | collective-permute-start | bytes 393224 | tf_op jit(solution)/shard_map/ppermute | solution.py:34
  35.3 0.4 collective-permute-start.17
  35.6 0.0 collective-permute-done.14.refs_1_
  35.7 0.6 %collective-permute-start.15 = (bf16[32,16,128]{2,1,0:T(8,128)(2,1)S(1)}, bf16[32,16,128]{2,1,0:T(8,128)(2,1)S(1)}, u32[]{:S(2)}, u32[]{:S(2)}) collective-permute-start(bf16[32,16,128]{2,1,0:T(8,128)(2,1)S(1)} %fusion), channel_id=1, source_target_pairs={{0,2},{1,3},{2,0},{3,1},{4,6},{5,7},{6,4},{7,5},{8,10},{9,11},{10,... | collective-permute-start | bytes 393224 | tf_op jit(solution)/shard_map/ppermute | solution.py:24
  36.2 0.0 copy-done.2
  36.2 0.0 copy-done.3
  36.2 0.0 copy-done.4
  36.2 1.3 %shard_map.133 = (f32[32,16384]{1,0:T(8,128)S(1)}, bf16[128,16384]{1,0:T(8,128)(2,1)S(1)}) custom-call(s32[4,4096]{1,0:T(4,128)S(1)} %copy-done.2, f32[4,4096]{1,0:T(4,128)S(1)} %copy-done.3, s32[1,4096]{1,0:T(1,128)S(1)} %bitcast.4), custom_call_target="tpu_custom_call" | custom-call | bytes 8000000 | tf_op jit(solution)/shard_map/pallas_call | solution.py:215
  37.5 0.4 collective-permute-done.16.refs_5_
  37.9 2.6 %collective-permute-done.18.refs_7_ = bf16[32,16,128]{2,1,0:T(8,128)(2,1)S(1)} collective-permute-done((bf16[32,16,128]{2,1,0:T(8,128)(2,1)S(1)}, bf16[32,16,128]{2,1,0:T(8,128)(2,1)S(1)}, u32[]{:S(2)}, u32[]{:S(2)}) %collective-permute-start.18) | collective-permute-done | bytes 131104 | tf_op jit(solution)/shard_map/ppermute | solution.py:34
  40.6 2.4 %collective-permute-done.17.refs_6_ = bf16[32,16,128]{2,1,0:T(8,128)(2,1)S(1)} collective-permute-done((bf16[32,16,128]{2,1,0:T(8,128)(2,1)S(1)}, bf16[32,16,128]{2,1,0:T(8,128)(2,1)S(1)}, u32[]{:S(2)}, u32[]{:S(2)}) %collective-permute-start.17) | collective-permute-done | bytes 131104 | tf_op jit(solution)/shard_map/ppermute | solution.py:34
  43.0 0.0 collective-permute-done.15.refs_2_
  43.0 2.1 %shard_map.134 = (f32[32,8,256]{2,1,0:T(8,128)}, f32[32,8,256]{2,1,0:T(8,128)}, f32[32,128]{1,0:T(8,128)S(1)}) custom-call(f32[32,64,128]{2,1,0:T(8,128)S(1)} %shard_map.132.refs_0_, f32[32,32,128]{2,1,0:T(8,128)S(1)} %collective-permute-done.14.refs_1_, bf16[32,16,128]{2,1,0:T(8,128)(2,1)S(1)} %collective-permute-done.15.refs_2_, ...), custom_call_target="tpu_custom_call" | custom-call | flops 200000000 | bytes 3000000 | tf_op jit(solution)/shard_map/pallas_call | solution.py:270
  45.1 10.5 %all_to_all.9 = f32[32,1,128]{2,1,0:T(1,128)S(1)} all-to-all(f32[32,1,128]{2,1,0:T(1,128)S(1)} %bitcast.5), channel_id=1, replica_groups=mesh['clus'=8,'sub'=4] {'clus','sub'}, dimensions={0} | all-to-all | bytes 32768 | tf_op jit(solution)/shard_map/all_to_all | solution.py:369
  55.5 0.6 reduce_sum.9
  (9 shorter events, 0.2 us)
Async XLA Ops:
  0.6 12.6 %copy-start.1 = (bf16[32,8,256]{2,1,0:T(8,128)(2,1)S(1)}, bf16[32,8,256]{2,1,0:T(8,128)(2,1)}, u32[]{:S(2)}) copy-start(bf16[32,8,256]{2,1,0:T(8,128)(2,1)} %refs_3_) | copy-start | bytes 393220
  0.6 15.3 %copy-start.6 = (s32[2,32]{1,0:T(2,128)S(1)}, s32[2,32]{1,0:T(2,128)}, u32[]{:S(2)}) copy-start(s32[2,32]{1,0:T(2,128)} %refs_2_.5) | copy-start | bytes 772
  0.7 15.3 %copy-start.7 = (s32[128]{0:T(128)S(1)}, s32[128]{0:T(128)}, u32[]{:S(2)}) copy-start(s32[128]{0:T(128)} %refs_1_.5) | copy-start | bytes 1540
  0.7 15.3 %copy-start.5 = (s32[2,128]{1,0:T(2,128)S(1)}, s32[2,128]{1,0:T(2,128)}, u32[]{:S(2)}) copy-start(s32[2,128]{1,0:T(2,128)} %refs_0_.5) | copy-start | bytes 3076
  0.7 3.1 %collective-permute-start.3 = (bf16[32,8,256]{2,1,0:T(8,128)(2,1)}, bf16[32,8,256]{2,1,0:T(8,128)(2,1)S(1)}, u32[]{:S(2)}, u32[]{:S(2)}) collective-permute-start(bf16[32,8,256]{2,1,0:T(8,128)(2,1)} %refs_3_.1), channel_id=1, source_target_pairs={{0,1},{1,0},{2,3},{3,2},{4,5},{5,4},{6,7},{7,6},{8,9},{9,8},{10,11... | collective-permute-start | bytes 393224 | tf_op jit(solution)/shard_map/ppermute | solution.py:24
  1.2 9.0 %collective-permute-start.4 = (bf16[32,8,256]{2,1,0:T(8,128)(2,1)}, bf16[32,8,256]{2,1,0:T(8,128)(2,1)S(1)}, u32[]{:S(2)}, u32[]{:S(2)}) collective-permute-start(bf16[32,8,256]{2,1,0:T(8,128)(2,1)} %refs_3_.1), channel_id=1, source_target_pairs={{0,4},{1,29},{2,6},{3,31},{4,8},{5,1},{6,10},{7,3},{8,12},{9,5},{1... | collective-permute-start | bytes 393224 | tf_op jit(solution)/shard_map/ppermute | solution.py:34
  3.7 7.7 %collective-permute-start.5 = (bf16[32,8,256]{2,1,0:T(8,128)(2,1)S(1)}, bf16[32,8,256]{2,1,0:T(8,128)(2,1)S(1)}, u32[]{:S(2)}, u32[]{:S(2)}) collective-permute-start(bf16[32,8,256]{2,1,0:T(8,128)(2,1)S(1)} %collective-permute-done.3.refs_4_), channel_id=1, source_target_pairs={{0,4},{1,29},{2,6},{3,31},{4,8},{5,1},{6,10},{7,3},{8,12},{9,5},{1... | collective-permute-start | bytes 393224 | tf_op jit(solution)/shard_map/ppermute | solution.py:34
  5.3 6.2 %collective-permute-start.6 = (bf16[32,8,256]{2,1,0:T(8,128)(2,1)}, bf16[32,8,256]{2,1,0:T(8,128)(2,1)S(1)}, u32[]{:S(2)}, u32[]{:S(2)}) collective-permute-start(bf16[32,8,256]{2,1,0:T(8,128)(2,1)} %refs_3_.1), channel_id=1, source_target_pairs={{0,2},{1,3},{2,0},{3,1},{4,6},{5,7},{6,4},{7,5},{8,10},{9,11},{10,... | collective-permute-start | bytes 393224 | tf_op jit(solution)/shard_map/ppermute | solution.py:24
  6.8 7.5 %collective-permute-start.1 = (bf16[32,8,256]{2,1,0:T(8,128)(2,1)}, bf16[32,8,256]{2,1,0:T(8,128)(2,1)S(1)}, u32[]{:S(2)}, u32[]{:S(2)}) collective-permute-start(bf16[32,8,256]{2,1,0:T(8,128)(2,1)} %refs_3_), channel_id=1, source_target_pairs={{0,2},{1,3},{2,0},{3,1},{4,6},{5,7},{6,4},{7,5},{8,10},{9,11},{10,... | collective-permute-start | bytes 393224 | tf_op jit(solution)/shard_map/ppermute | solution.py:24
  11.5 8.6 %collective-permute-start.8 = (bf16[64,8,256]{2,1,0:T(8,128)(2,1)S(1)}, bf16[64,8,256]{2,1,0:T(8,128)(2,1)S(1)}, u32[]{:S(2)}, u32[]{:S(2)}) collective-permute-start(bf16[64,8,256]{2,1,0:T(8,128)(2,1)S(1)} %pad_maximum_fusion.2), channel_id=1, source_target_pairs={{0,2},{1,3},{2,0},{3,1},{4,6},{5,7},{6,4},{7,5},{8,10},{9,11},{10,... | collective-permute-start | bytes 786440 | tf_op jit(solution)/shard_map/ppermute | solution.py:24
  13.3 2.1 %collective-permute-start = (bf16[32,8,256]{2,1,0:T(8,128)(2,1)S(1)}, bf16[32,8,256]{2,1,0:T(8,128)(2,1)S(1)}, u32[]{:S(2)}, u32[]{:S(2)}) collective-permute-start(bf16[32,8,256]{2,1,0:T(8,128)(2,1)S(1)} %copy-done.1), channel_id=1, source_target_pairs={{0,1},{1,0},{2,3},{3,2},{4,5},{5,4},{6,7},{7,6},{8,9},{9,8},{10,11... | collective-permute-start | bytes 393224 | tf_op jit(solution)/shard_map/ppermute | solution.py:24
  14.4 1.3 %collective-permute-start.2 = (bf16[32,8,256]{2,1,0:T(8,128)(2,1)S(1)}, bf16[32,8,256]{2,1,0:T(8,128)(2,1)S(1)}, u32[]{:S(2)}, u32[]{:S(2)}) collective-permute-start(bf16[32,8,256]{2,1,0:T(8,128)(2,1)S(1)} %collective-permute-done.1.refs_5_), channel_id=1, source_target_pairs={{0,1},{1,0},{2,3},{3,2},{4,5},{5,4},{6,7},{7,6},{8,9},{9,8},{10,11... | collective-permute-start | bytes 393224 | tf_op jit(solution)/shard_map/ppermute | solution.py:24
  14.6 1.3 %collective-permute-start.7 = (bf16[32,8,256]{2,1,0:T(8,128)(2,1)S(1)}, bf16[32,8,256]{2,1,0:T(8,128)(2,1)S(1)}, u32[]{:S(2)}, u32[]{:S(2)}) collective-permute-start(bf16[32,8,256]{2,1,0:T(8,128)(2,1)S(1)} %collective-permute-done.6.refs_5_), channel_id=1, source_target_pairs={{0,1},{1,0},{2,3},{3,2},{4,5},{5,4},{6,7},{7,6},{8,9},{9,8},{10,11... | collective-permute-start | bytes 393224 | tf_op jit(solution)/shard_map/ppermute | solution.py:24
  20.1 4.8 %copy-start = (bf16[32,8,256]{2,1,0:T(8,128)(2,1)S(1)}, bf16[32,8,256]{2,1,0:T(8,128)(2,1)}, u32[]{:S(2)}) copy-start(bf16[32,8,256]{2,1,0:T(8,128)(2,1)} %refs_3_.1) | copy-start | bytes 393220
  20.1 2.1 %collective-permute-start.9 = (bf16[128,8,256]{2,1,0:T(8,128)(2,1)S(1)}, bf16[128,8,256]{2,1,0:T(8,128)(2,1)S(1)}, u32[]{:S(2)}, u32[]{:S(2)}) collective-permute-start(bf16[128,8,256]{2,1,0:T(8,128)(2,1)S(1)} %constant_dynamic-update-slice_fusion.refs_7_), channel_id=1, source_target_pairs={{0,1},{1,0},{2,3},{3,2},{4,5},{5,4},{6,7},{7,6},{8,9},{9,8},{10,11... | collective-permute-start | bytes 1572872 | tf_op jit(solution)/shard_map/ppermute | solution.py:24
  20.7 2.2 %collective-permute-start.10 = (bf16[32,32,128]{2,1,0:T(8,128)(2,1)S(1)}, bf16[32,32,128]{2,1,0:T(8,128)(2,1)S(1)}, u32[]{:S(2)}, u32[]{:S(2)}) collective-permute-start(bf16[32,32,128]{2,1,0:T(8,128)(2,1)S(1)} %get-tuple-element.58), channel_id=1, source_target_pairs={{0,1},{1,0},{2,3},{3,2},{4,5},{5,4},{6,7},{7,6},{8,9},{9,8},{10,11... | collective-permute-start | bytes 786440 | tf_op jit(solution)/shard_map/ppermute | solution.py:24
  22.3 9.3 %collective-permute-start.12 = (f32[32,32,128]{2,1,0:T(8,128)S(1)}, f32[32,32,128]{2,1,0:T(8,128)S(1)}, u32[]{:S(2)}, u32[]{:S(2)}) collective-permute-start(f32[32,32,128]{2,1,0:T(8,128)S(1)} %pad_maximum_fusion), channel_id=1, source_target_pairs={{0,1},{1,0},{2,3},{3,2},{4,5},{5,4},{6,7},{7,6},{8,9},{9,8},{10,11... | collective-permute-start | bytes 1572872 | tf_op jit(solution)/shard_map/ppermute | solution.py:24
  22.7 5.6 %collective-permute-start.13 = (bf16[32,32,128]{2,1,0:T(8,128)(2,1)S(1)}, bf16[32,32,128]{2,1,0:T(8,128)(2,1)S(1)}, u32[]{:S(2)}, u32[]{:S(2)}) collective-permute-start(bf16[32,32,128]{2,1,0:T(8,128)(2,1)S(1)} %get-tuple-element.61), channel_id=1, source_target_pairs={{0,1},{1,0},{2,3},{3,2},{4,5},{5,4},{6,7},{7,6},{8,9},{9,8},{10,11... | collective-permute-start | bytes 786440 | tf_op jit(solution)/shard_map/ppermute | solution.py:24
  22.9 8.7 %collective-permute-start.11 = (bf16[32,32,128]{2,1,0:T(8,128)(2,1)S(1)}, bf16[32,32,128]{2,1,0:T(8,128)(2,1)S(1)}, u32[]{:S(2)}, u32[]{:S(2)}) collective-permute-start(bf16[32,32,128]{2,1,0:T(8,128)(2,1)S(1)} %add_convert_fusion.1), channel_id=1, source_target_pairs={{0,2},{1,3},{2,0},{3,1},{4,6},{5,7},{6,4},{7,5},{8,10},{9,11},{10,... | collective-permute-start | bytes 786440 | tf_op jit(solution)/shard_map/ppermute | solution.py:24
  31.6 4.6 %copy-start.2 = (s32[4,4096]{1,0:T(4,128)S(1)}, s32[4,4096]{1,0:T(4,128)}, u32[]{:S(2)}) copy-start(s32[4,4096]{1,0:T(4,128)} %params) | copy-start | bytes 196612
  31.7 4.6 %copy-start.3 = (f32[4,4096]{1,0:T(4,128)S(1)}, f32[4,4096]{1,0:T(4,128)}, u32[]{:S(2)}) copy-start(f32[4,4096]{1,0:T(4,128)} %weights.1) | copy-start | bytes 196612
  31.7 4.6 %copy-start.4 = (s32[4096]{0:T(1024)S(1)}, s32[4096]{0:T(1024)}, u32[]{:S(2)}) copy-start(s32[4096]{0:T(1024)} %param.21) | copy-start | bytes 49156
  31.7 3.9 %collective-permute-start.14 = (f32[32,32,128]{2,1,0:T(8,128)S(1)}, f32[32,32,128]{2,1,0:T(8,128)S(1)}, u32[]{:S(2)}, u32[]{:S(2)}) collective-permute-start(f32[32,32,128]{2,1,0:T(8,128)S(1)} %pad_maximum_fusion.1), channel_id=1, source_target_pairs={{0,1},{1,0},{2,3},{3,2},{4,5},{5,4},{6,7},{7,6},{8,9},{9,8},{10,11... | collective-permute-start | bytes 1572872 | tf_op jit(solution)/shard_map/ppermute | solution.py:24
  32.0 6.0 %collective-permute-start.16 = (bf16[32,16,128]{2,1,0:T(8,128)(2,1)S(1)}, bf16[32,16,128]{2,1,0:T(8,128)(2,1)S(1)}, u32[]{:S(2)}, u32[]{:S(2)}) collective-permute-start(bf16[32,16,128]{2,1,0:T(8,128)(2,1)S(1)} %add_convert_fusion.2), channel_id=1, source_target_pairs={{0,2},{1,3},{2,0},{3,1},{4,6},{5,7},{6,4},{7,5},{8,10},{9,11},{10,... | collective-permute-start | bytes 393224 | tf_op jit(solution)/shard_map/ppermute | solution.py:24
  33.8 6.8 %collective-permute-start.18 = (bf16[32,16,128]{2,1,0:T(8,128)(2,1)S(1)}, bf16[32,16,128]{2,1,0:T(8,128)(2,1)S(1)}, u32[]{:S(2)}, u32[]{:S(2)}) collective-permute-start(bf16[32,16,128]{2,1,0:T(8,128)(2,1)S(1)} %get-tuple-element.77), channel_id=1, source_target_pairs={{0,5},{1,28},{2,7},{3,30},{4,9},{5,0},{6,11},{7,2},{8,13},{9,4},{1... | collective-permute-start | bytes 393224 | tf_op jit(solution)/shard_map/ppermute | solution.py:34
  35.3 7.7 %collective-permute-start.17 = (bf16[32,16,128]{2,1,0:T(8,128)(2,1)S(1)}, bf16[32,16,128]{2,1,0:T(8,128)(2,1)S(1)}, u32[]{:S(2)}, u32[]{:S(2)}) collective-permute-start(bf16[32,16,128]{2,1,0:T(8,128)(2,1)S(1)} %get-tuple-element.78), channel_id=1, source_target_pairs={{0,4},{1,29},{2,6},{3,31},{4,8},{5,1},{6,10},{7,3},{8,12},{9,5},{1... | collective-permute-start | bytes 393224 | tf_op jit(solution)/shard_map/ppermute | solution.py:34
  35.7 7.3 %collective-permute-start.15 = (bf16[32,16,128]{2,1,0:T(8,128)(2,1)S(1)}, bf16[32,16,128]{2,1,0:T(8,128)(2,1)S(1)}, u32[]{:S(2)}, u32[]{:S(2)}) collective-permute-start(bf16[32,16,128]{2,1,0:T(8,128)(2,1)S(1)} %fusion), channel_id=1, source_target_pairs={{0,2},{1,3},{2,0},{3,1},{4,6},{5,7},{6,4},{7,5},{8,10},{9,11},{10,... | collective-permute-start | bytes 393224 | tf_op jit(solution)/shard_map/ppermute | solution.py:24

commit v7 on v6

--- a/solution.py
+++ b/solution.py
@@ -341,15 +341,15 @@
     x_there, odd_rows = tie((x_there, odd_rows))
     adj_core = moved(jnp.concatenate(odd_rows, axis=1), 0, 1)
     fwd, = apply(False, fields=[*x_pieces, x_here, x_there], first=right, second=left, near=near)
+    fwd_core = moved(
+        jnp.concatenate([fwd[:, m * part : (m + 1) * part] for m in range(1, members, 2)], axis=1), 0, 1
+    )
     fwd, sides, adj_core, given[0] = tie((fwd, sides, adj_core, given[0]))
 
     def own_sum(field, core_part, m):
         k = m // 2
         return field[:clusters, m * part : (m + 1) * part] + core_part[:, k * part : (k + 1) * part]
 
-    fwd_core = moved(
-        jnp.concatenate([fwd[:, m * part : (m + 1) * part] for m in range(1, members, 2)], axis=1), 0, 1
-    )
     side = chip_sums(0)
     for s in sides:
         side = side + s.astype(jnp.float32)

time: 56.3 us -> 56.2 us (level)
  waiting for transfers between devices: 13.2 us -> 12.1 us
  blocking collectives: 10.5 us -> 11.5 us
    ppermute x4, waiting for transfers between devices: 6.29 us -> 3.7 us  [round_ring(): return lax.ppermute(x, AXES, pairs)]
    ppermute x15, waiting for transfers between devices: 6.93 us -> 8.42 us  [moved(): return lax.ppermute(x, AXES, pairs)]
    all_to_all x1, blocking collectives: 10.5 us -> 11.5 us  [shards(): lax.all_to_all(grad.reshape(devices, PAR_DEV), AXES, 0, 0, tiled=True)]
  transfers between devices with their start and end apart: 19 -> 19, of which waited for: 10 -> 10; matrix products, arithmetic and copies ran while one was open for 1% -> 1% of each run, Pallas kernels for 19% -> 20%
where the time goes in v7:
time: 56.2 us; the launch traced here: 56 us
  starting transfers between devices  17.4 us (31%)
  Pallas kernels  13 us (23%)
  waiting for transfers between devices  12.1 us (22%)
  blocking collectives  11.5 us (20%)
  other arithmetic  0.95 us (2%)
  between operations  0.87 us (2%)
    all_to_all x1, blocking collectives, shards(): lax.all_to_all(grad.reshape(devices, PAR_DEV), AXES, 0, 0, tiled=True)  11.5 us
    ppermute x15, starting transfers between devices, moved(): return lax.ppermute(x, AXES, pairs)  11.5 us
    ppermute x15, waiting for transfers between devices, moved(): return lax.ppermute(x, AXES, pairs)  8.42 us
    pallas_call x2, Pallas kernels, apply_blocks(): pl.pallas_call(functools.partial(block_kernel, transposed, total, members...  6.78 us
    ppermute x4, starting transfers between devices, round_ring(): return lax.ppermute(x, AXES, pairs)  5.93 us
    ppermute x4, waiting for transfers between devices, round_ring(): return lax.ppermute(x, AXES, pairs)  3.7 us
    pallas_call x1, Pallas kernels, loaded(): pl.pallas_call(functools.partial(load_kernel, LOADS), in_specs=[pl.BlockS...  2.87 us
    pallas_call x1, Pallas kernels, finish(): pl.pallas_call(functools.partial(final_kernel, column_total, len(fwd_term...  2.07 us
  transfers between devices with their start and end apart: 19, of which 10 were waited for; matrix products, arithmetic and copies ran while one was open for 1% of the time, Pallas kernels for 20%

profile of v7, /device:TPU:0, one launch (start us, length us, event | category | flops | bytes accessed | tf_op | source)
XLA Modules:
  0.0 56.0 jit_solution(3364358880571863014)
XLA Ops:
  0.6 0.0 copy-start.1
  0.6 0.0 copy-start.6
  0.7 0.0 copy-start.7
  0.7 0.0 copy-start.5
  0.7 0.5 collective-permute-start.3
  1.2 2.6 %collective-permute-start.4 = (bf16[32,8,256]{2,1,0:T(8,128)(2,1)}, bf16[32,8,256]{2,1,0:T(8,128)(2,1)S(1)}, u32[]{:S(2)}, u32[]{:S(2)}) collective-permute-start(bf16[32,8,256]{2,1,0:T(8,128)(2,1)} %refs_3_.1), channel_id=1, source_target_pairs={{0,4},{1,29},{2,6},{3,31},{4,8},{5,1},{6,10},{7,3},{8,12},{9,5},{1... | collective-permute-start | bytes 393224 | tf_op jit(solution)/shard_map/ppermute | solution.py:34
  3.7 0.0 collective-permute-done.3.refs_4_
  3.7 1.5 %collective-permute-start.5 = (bf16[32,8,256]{2,1,0:T(8,128)(2,1)S(1)}, bf16[32,8,256]{2,1,0:T(8,128)(2,1)S(1)}, u32[]{:S(2)}, u32[]{:S(2)}) collective-permute-start(bf16[32,8,256]{2,1,0:T(8,128)(2,1)S(1)} %collective-permute-done.3.refs_4_), channel_id=1, source_target_pairs={{0,4},{1,29},{2,6},{3,31},{4,8},{5,1},{6,10},{7,3},{8,12},{9,5},{1... | collective-permute-start | bytes 393224 | tf_op jit(solution)/shard_map/ppermute | solution.py:34
  5.3 1.5 %collective-permute-start.6 = (bf16[32,8,256]{2,1,0:T(8,128)(2,1)}, bf16[32,8,256]{2,1,0:T(8,128)(2,1)S(1)}, u32[]{:S(2)}, u32[]{:S(2)}) collective-permute-start(bf16[32,8,256]{2,1,0:T(8,128)(2,1)} %refs_3_.1), channel_id=1, source_target_pairs={{0,2},{1,3},{2,0},{3,1},{4,6},{5,7},{6,4},{7,5},{8,10},{9,11},{10,... | collective-permute-start | bytes 393224 | tf_op jit(solution)/shard_map/ppermute | solution.py:24
  6.8 0.5 collective-permute-start.1
  7.3 2.9 %shard_map.130 = (bf16[128,2,32,128]{3,2,1,0:T(8,128)(2,1)S(1)}, bf16[128,2,32,128]{3,2,1,0:T(8,128)(2,1)S(1)}, bf16[32,2,128,128]{3,2,1,0:T(8,128)(2,1)S(1)}) custom-call(bf16[128,2,32,128]{3,2,1,0:T(8,128)(2,1)} %refs_0_.3, bf16[128,2,32,128]{3,2,1,0:T(8,128)(2,1)} %refs_1_.3, bf16[32,2,128,128]{3,2,1,0:T(8,128)(2,1)} %refs_2_.3), custom_call_target="tpu_custom_call" | custom-call | bytes 12000000 | tf_op jit(solution)/shard_map/pallas_call | solution.py:182
  10.2 0.0 collective-permute-done.4
  10.2 1.3 %collective-permute-done.5 = bf16[32,8,256]{2,1,0:T(8,128)(2,1)S(1)} collective-permute-done((bf16[32,8,256]{2,1,0:T(8,128)(2,1)S(1)}, bf16[32,8,256]{2,1,0:T(8,128)(2,1)S(1)}, u32[]{:S(2)}, u32[]{:S(2)}) %collective-permute-start.5) | collective-permute-done | bytes 131104 | tf_op jit(solution)/shard_map/ppermute | solution.py:34
  11.5 0.0 collective-permute-done.6.refs_5_
  11.5 1.7 %collective-permute-start.8 = (bf16[64,8,256]{2,1,0:T(8,128)(2,1)S(1)}, bf16[64,8,256]{2,1,0:T(8,128)(2,1)S(1)}, u32[]{:S(2)}, u32[]{:S(2)}) collective-permute-start(bf16[64,8,256]{2,1,0:T(8,128)(2,1)S(1)} %pad_maximum_fusion.2), channel_id=1, source_target_pairs={{0,2},{1,3},{2,0},{3,1},{4,6},{5,7},{6,4},{7,5},{8,10},{9,11},{10,... | collective-permute-start | bytes 786440 | tf_op jit(solution)/shard_map/ppermute | solution.py:24
  13.3 0.0 copy-done.1
  13.3 1.1 %collective-permute-start = (bf16[32,8,256]{2,1,0:T(8,128)(2,1)S(1)}, bf16[32,8,256]{2,1,0:T(8,128)(2,1)S(1)}, u32[]{:S(2)}, u32[]{:S(2)}) collective-permute-start(bf16[32,8,256]{2,1,0:T(8,128)(2,1)S(1)} %copy-done.1), channel_id=1, source_target_pairs={{0,1},{1,0},{2,3},{3,2},{4,5},{5,4},{6,7},{7,6},{8,9},{9,8},{10,11... | collective-permute-start | bytes 393224 | tf_op jit(solution)/shard_map/ppermute | solution.py:24
  14.3 0.0 collective-permute-done.1.refs_5_
  14.4 0.3 collective-permute-start.2
  14.6 0.2 collective-permute-start.7
  14.9 0.5 collective-permute-done.refs_4_
  15.3 0.4 collective-permute-done.2.refs_6_
  15.7 0.3 collective-permute-done.7.refs_6_
  16.0 0.0 copy-done.6
  16.0 0.0 copy-done.7
  16.0 0.0 copy-done.5
  16.0 3.4 %shard_map.131 = (f32[96,64,128]{2,1,0:T(8,128)S(1)}, bf16[32,32,128]{2,1,0:T(8,128)(2,1)S(1)}, bf16[32,32,128]{2,1,0:T(8,128)(2,1)S(1)}) custom-call(s32[2,128]{1,0:T(2,128)S(1)} %copy-done.5, s32[128]{0:T(128)S(1)} %copy-done.7, s32[2,32]{1,0:T(2,128)S(1)} %copy-done.6, bf16[32,8,256]{2,1,0:T(8,128)(2,1)S(1)} %copy-done.1, ...), custom_call_target="tpu_custom_call" | custom-call | flops 671088640 | bytes 20000000 | tf_op jit(solution)/shard_map/pallas_call | solution.py:147
  19.4 0.7 %collective-permute-done.8 = bf16[64,8,256]{2,1,0:T(8,128)(2,1)S(1)} collective-permute-done((bf16[64,8,256]{2,1,0:T(8,128)(2,1)S(1)}, bf16[64,8,256]{2,1,0:T(8,128)(2,1)S(1)}, u32[]{:S(2)}, u32[]{:S(2)}) %collective-permute-start.8) | collective-permute-done | bytes 262176 | tf_op jit(solution)/shard_map/ppermute | solution.py:24
  20.1 0.5 collective-permute-start.9
  20.7 0.1 collective-permute-start.10
  20.8 0.4 collective-permute-start.13
  21.2 1.0 %collective-permute-done.9.refs_8_ = bf16[128,8,256]{2,1,0:T(8,128)(2,1)S(1)} collective-permute-done((bf16[128,8,256]{2,1,0:T(8,128)(2,1)S(1)}, bf16[128,8,256]{2,1,0:T(8,128)(2,1)S(1)}, u32[]{:S(2)}, u32[]{:S(2)}) %collective-permute-start.9) | collective-permute-done | bytes 524320 | tf_op jit(solution)/shard_map/ppermute | solution.py:24
  22.2 0.1 pad_maximum_fusion
  22.3 0.4 collective-permute-start.12
  22.7 0.0 collective-permute-done.10
  22.7 0.1 add_convert_fusion.1
  22.8 1.9 %collective-permute-start.11 = (bf16[32,32,128]{2,1,0:T(8,128)(2,1)S(1)}, bf16[32,32,128]{2,1,0:T(8,128)(2,1)S(1)}, u32[]{:S(2)}, u32[]{:S(2)}) collective-permute-start(bf16[32,32,128]{2,1,0:T(8,128)(2,1)S(1)} %add_convert_fusion.1), channel_id=1, source_target_pairs={{0,2},{1,3},{2,0},{3,1},{4,6},{5,7},{6,4},{7,5},{8,10},{9,11},{10,... | collective-permute-start | bytes 786440 | tf_op jit(solution)/shard_map/ppermute | solution.py:24
  24.7 0.0 copy-done
  24.7 3.4 %shard_map.132.refs_0_ = f32[32,64,128]{2,1,0:T(8,128)S(1)} custom-call(s32[2,128]{1,0:T(2,128)S(1)} %copy-done.5, s32[128]{0:T(128)S(1)} %copy-done.7, s32[2,32]{1,0:T(2,128)S(1)} %copy-done.6, bf16[32,8,256]{2,1,0:T(8,128)(2,1)S(1)} %copy-done, bf16[32,8,256]{2,1,0:T(8,128)(2,1)S(1)} %collective-permute-done.3.refs_4_, ...), custom_call_target="tpu_custom_call" | custom-call | flops 671088640 | bytes 20000000 | tf_op jit(solution)/shard_map/pallas_call | solution.py:147
  28.1 0.0 copy-start.2
  28.1 0.0 copy-start.3
  28.1 0.0 copy-start.4
  28.1 0.1 pad_maximum_fusion.1
  28.2 0.1 collective-permute-start.14
  28.3 0.0 collective-permute-done.13
  28.3 3.1 %collective-permute-done.11 = bf16[32,32,128]{2,1,0:T(8,128)(2,1)S(1)} collective-permute-done((bf16[32,32,128]{2,1,0:T(8,128)(2,1)S(1)}, bf16[32,32,128]{2,1,0:T(8,128)(2,1)S(1)}, u32[]{:S(2)}, u32[]{:S(2)}) %collective-permute-start.11) | collective-permute-done | bytes 262176 | tf_op jit(solution)/shard_map/ppermute | solution.py:24
  31.4 0.0 collective-permute-done.12.refs_4_
  31.4 0.1 add_convert_fusion
  31.6 1.8 %collective-permute-start.16 = (bf16[32,16,128]{2,1,0:T(8,128)(2,1)S(1)}, bf16[32,16,128]{2,1,0:T(8,128)(2,1)S(1)}, u32[]{:S(2)}, u32[]{:S(2)}) collective-permute-start(bf16[32,16,128]{2,1,0:T(8,128)(2,1)S(1)} %add_convert_fusion.2), channel_id=1, source_target_pairs={{0,2},{1,3},{2,0},{3,1},{4,6},{5,7},{6,4},{7,5},{8,10},{9,11},{10,... | collective-permute-start | bytes 393224 | tf_op jit(solution)/shard_map/ppermute | solution.py:24
  33.4 0.0 collective-permute-done.14.refs_1_
  33.5 0.4 collective-permute-start.15
  33.8 0.3 collective-permute-start.18
  34.1 1.5 %collective-permute-start.17 = (bf16[32,16,128]{2,1,0:T(8,128)(2,1)S(1)}, bf16[32,16,128]{2,1,0:T(8,128)(2,1)S(1)}, u32[]{:S(2)}, u32[]{:S(2)}) collective-permute-start(bf16[32,16,128]{2,1,0:T(8,128)(2,1)S(1)} %get-tuple-element.78), channel_id=1, source_target_pairs={{0,4},{1,29},{2,6},{3,31},{4,8},{5,1},{6,10},{7,3},{8,12},{9,5},{1... | collective-permute-start | bytes 393224 | tf_op jit(solution)/shard_map/ppermute | solution.py:34
  35.6 0.0 copy-done.2
  35.6 0.0 copy-done.3
  35.7 0.0 copy-done.4
  35.7 1.3 %shard_map.133 = (f32[32,16384]{1,0:T(8,128)S(1)}, bf16[128,16384]{1,0:T(8,128)(2,1)S(1)}) custom-call(s32[4,4096]{1,0:T(4,128)S(1)} %copy-done.2, f32[4,4096]{1,0:T(4,128)S(1)} %copy-done.3, s32[1,4096]{1,0:T(1,128)S(1)} %bitcast.4), custom_call_target="tpu_custom_call" | custom-call | bytes 8000000 | tf_op jit(solution)/shard_map/pallas_call | solution.py:215
  36.9 1.0 %collective-permute-done.16.refs_5_ = bf16[32,16,128]{2,1,0:T(8,128)(2,1)S(1)} collective-permute-done((bf16[32,16,128]{2,1,0:T(8,128)(2,1)S(1)}, bf16[32,16,128]{2,1,0:T(8,128)(2,1)S(1)}, u32[]{:S(2)}, u32[]{:S(2)}) %collective-permute-start.16) | collective-permute-done | bytes 131104 | tf_op jit(solution)/shard_map/ppermute | solution.py:24
  37.9 1.5 %collective-permute-done.15.refs_2_ = bf16[32,16,128]{2,1,0:T(8,128)(2,1)S(1)} collective-permute-done((bf16[32,16,128]{2,1,0:T(8,128)(2,1)S(1)}, bf16[32,16,128]{2,1,0:T(8,128)(2,1)S(1)}, u32[]{:S(2)}, u32[]{:S(2)}) %collective-permute-start.15) | collective-permute-done | bytes 131104 | tf_op jit(solution)/shard_map/ppermute | solution.py:24
  39.4 0.0 collective-permute-done.18.refs_7_
  39.4 2.4 %collective-permute-done.17.refs_6_ = bf16[32,16,128]{2,1,0:T(8,128)(2,1)S(1)} collective-permute-done((bf16[32,16,128]{2,1,0:T(8,128)(2,1)S(1)}, bf16[32,16,128]{2,1,0:T(8,128)(2,1)S(1)}, u32[]{:S(2)}, u32[]{:S(2)}) %collective-permute-start.17) | collective-permute-done | bytes 131104 | tf_op jit(solution)/shard_map/ppermute | solution.py:34
  41.9 2.1 %shard_map.134 = (f32[32,8,256]{2,1,0:T(8,128)}, f32[32,8,256]{2,1,0:T(8,128)}, f32[32,128]{1,0:T(8,128)S(1)}) custom-call(f32[32,64,128]{2,1,0:T(8,128)S(1)} %shard_map.132.refs_0_, f32[32,32,128]{2,1,0:T(8,128)S(1)} %collective-permute-done.14.refs_1_, bf16[32,16,128]{2,1,0:T(8,128)(2,1)S(1)} %collective-permute-done.15.refs_2_, ...), custom_call_target="tpu_custom_call" | custom-call | flops 200000000 | bytes 3000000 | tf_op jit(solution)/shard_map/pallas_call | solution.py:270
  43.9 11.5 %all_to_all.9 = f32[32,1,128]{2,1,0:T(1,128)S(1)} all-to-all(f32[32,1,128]{2,1,0:T(1,128)S(1)} %bitcast.5), channel_id=1, replica_groups=mesh['clus'=8,'sub'=4] {'clus','sub'}, dimensions={0} | all-to-all | bytes 32768 | tf_op jit(solution)/shard_map/all_to_all | solution.py:369
  55.5 0.6 reduce_sum.9
  (9 shorter events, 0.2 us)
Async XLA Ops:
  0.6 12.6 %copy-start.1 = (bf16[32,8,256]{2,1,0:T(8,128)(2,1)S(1)}, bf16[32,8,256]{2,1,0:T(8,128)(2,1)}, u32[]{:S(2)}) copy-start(bf16[32,8,256]{2,1,0:T(8,128)(2,1)} %refs_3_) | copy-start | bytes 393220
  0.6 15.3 %copy-start.6 = (s32[2,32]{1,0:T(2,128)S(1)}, s32[2,32]{1,0:T(2,128)}, u32[]{:S(2)}) copy-start(s32[2,32]{1,0:T(2,128)} %refs_2_.5) | copy-start | bytes 772
  0.7 15.3 %copy-start.7 = (s32[128]{0:T(128)S(1)}, s32[128]{0:T(128)}, u32[]{:S(2)}) copy-start(s32[128]{0:T(128)} %refs_1_.5) | copy-start | bytes 1540
  0.7 15.3 %copy-start.5 = (s32[2,128]{1,0:T(2,128)S(1)}, s32[2,128]{1,0:T(2,128)}, u32[]{:S(2)}) copy-start(s32[2,128]{1,0:T(2,128)} %refs_0_.5) | copy-start | bytes 3076
  0.7 3.1 %collective-permute-start.3 = (bf16[32,8,256]{2,1,0:T(8,128)(2,1)}, bf16[32,8,256]{2,1,0:T(8,128)(2,1)S(1)}, u32[]{:S(2)}, u32[]{:S(2)}) collective-permute-start(bf16[32,8,256]{2,1,0:T(8,128)(2,1)} %refs_3_.1), channel_id=1, source_target_pairs={{0,1},{1,0},{2,3},{3,2},{4,5},{5,4},{6,7},{7,6},{8,9},{9,8},{10,11... | collective-permute-start | bytes 393224 | tf_op jit(solution)/shard_map/ppermute | solution.py:24
  1.2 9.0 %collective-permute-start.4 = (bf16[32,8,256]{2,1,0:T(8,128)(2,1)}, bf16[32,8,256]{2,1,0:T(8,128)(2,1)S(1)}, u32[]{:S(2)}, u32[]{:S(2)}) collective-permute-start(bf16[32,8,256]{2,1,0:T(8,128)(2,1)} %refs_3_.1), channel_id=1, source_target_pairs={{0,4},{1,29},{2,6},{3,31},{4,8},{5,1},{6,10},{7,3},{8,12},{9,5},{1... | collective-permute-start | bytes 393224 | tf_op jit(solution)/shard_map/ppermute | solution.py:34
  3.7 7.7 %collective-permute-start.5 = (bf16[32,8,256]{2,1,0:T(8,128)(2,1)S(1)}, bf16[32,8,256]{2,1,0:T(8,128)(2,1)S(1)}, u32[]{:S(2)}, u32[]{:S(2)}) collective-permute-start(bf16[32,8,256]{2,1,0:T(8,128)(2,1)S(1)} %collective-permute-done.3.refs_4_), channel_id=1, source_target_pairs={{0,4},{1,29},{2,6},{3,31},{4,8},{5,1},{6,10},{7,3},{8,12},{9,5},{1... | collective-permute-start | bytes 393224 | tf_op jit(solution)/shard_map/ppermute | solution.py:34
  5.3 6.2 %collective-permute-start.6 = (bf16[32,8,256]{2,1,0:T(8,128)(2,1)}, bf16[32,8,256]{2,1,0:T(8,128)(2,1)S(1)}, u32[]{:S(2)}, u32[]{:S(2)}) collective-permute-start(bf16[32,8,256]{2,1,0:T(8,128)(2,1)} %refs_3_.1), channel_id=1, source_target_pairs={{0,2},{1,3},{2,0},{3,1},{4,6},{5,7},{6,4},{7,5},{8,10},{9,11},{10,... | collective-permute-start | bytes 393224 | tf_op jit(solution)/shard_map/ppermute | solution.py:24
  6.8 7.5 %collective-permute-start.1 = (bf16[32,8,256]{2,1,0:T(8,128)(2,1)}, bf16[32,8,256]{2,1,0:T(8,128)(2,1)S(1)}, u32[]{:S(2)}, u32[]{:S(2)}) collective-permute-start(bf16[32,8,256]{2,1,0:T(8,128)(2,1)} %refs_3_), channel_id=1, source_target_pairs={{0,2},{1,3},{2,0},{3,1},{4,6},{5,7},{6,4},{7,5},{8,10},{9,11},{10,... | collective-permute-start | bytes 393224 | tf_op jit(solution)/shard_map/ppermute | solution.py:24
  11.5 8.6 %collective-permute-start.8 = (bf16[64,8,256]{2,1,0:T(8,128)(2,1)S(1)}, bf16[64,8,256]{2,1,0:T(8,128)(2,1)S(1)}, u32[]{:S(2)}, u32[]{:S(2)}) collective-permute-start(bf16[64,8,256]{2,1,0:T(8,128)(2,1)S(1)} %pad_maximum_fusion.2), channel_id=1, source_target_pairs={{0,2},{1,3},{2,0},{3,1},{4,6},{5,7},{6,4},{7,5},{8,10},{9,11},{10,... | collective-permute-start | bytes 786440 | tf_op jit(solution)/shard_map/ppermute | solution.py:24
  13.3 2.1 %collective-permute-start = (bf16[32,8,256]{2,1,0:T(8,128)(2,1)S(1)}, bf16[32,8,256]{2,1,0:T(8,128)(2,1)S(1)}, u32[]{:S(2)}, u32[]{:S(2)}) collective-permute-start(bf16[32,8,256]{2,1,0:T(8,128)(2,1)S(1)} %copy-done.1), channel_id=1, source_target_pairs={{0,1},{1,0},{2,3},{3,2},{4,5},{5,4},{6,7},{7,6},{8,9},{9,8},{10,11... | collective-permute-start | bytes 393224 | tf_op jit(solution)/shard_map/ppermute | solution.py:24
  14.4 1.3 %collective-permute-start.2 = (bf16[32,8,256]{2,1,0:T(8,128)(2,1)S(1)}, bf16[32,8,256]{2,1,0:T(8,128)(2,1)S(1)}, u32[]{:S(2)}, u32[]{:S(2)}) collective-permute-start(bf16[32,8,256]{2,1,0:T(8,128)(2,1)S(1)} %collective-permute-done.1.refs_5_), channel_id=1, source_target_pairs={{0,1},{1,0},{2,3},{3,2},{4,5},{5,4},{6,7},{7,6},{8,9},{9,8},{10,11... | collective-permute-start | bytes 393224 | tf_op jit(solution)/shard_map/ppermute | solution.py:24
  14.6 1.3 %collective-permute-start.7 = (bf16[32,8,256]{2,1,0:T(8,128)(2,1)S(1)}, bf16[32,8,256]{2,1,0:T(8,128)(2,1)S(1)}, u32[]{:S(2)}, u32[]{:S(2)}) collective-permute-start(bf16[32,8,256]{2,1,0:T(8,128)(2,1)S(1)} %collective-permute-done.6.refs_5_), channel_id=1, source_target_pairs={{0,1},{1,0},{2,3},{3,2},{4,5},{5,4},{6,7},{7,6},{8,9},{9,8},{10,11... | collective-permute-start | bytes 393224 | tf_op jit(solution)/shard_map/ppermute | solution.py:24
  20.1 4.6 %copy-start = (bf16[32,8,256]{2,1,0:T(8,128)(2,1)S(1)}, bf16[32,8,256]{2,1,0:T(8,128)(2,1)}, u32[]{:S(2)}) copy-start(bf16[32,8,256]{2,1,0:T(8,128)(2,1)} %refs_3_.1) | copy-start | bytes 393220
  20.1 2.1 %collective-permute-start.9 = (bf16[128,8,256]{2,1,0:T(8,128)(2,1)S(1)}, bf16[128,8,256]{2,1,0:T(8,128)(2,1)S(1)}, u32[]{:S(2)}, u32[]{:S(2)}) collective-permute-start(bf16[128,8,256]{2,1,0:T(8,128)(2,1)S(1)} %constant_dynamic-update-slice_fusion.refs_7_), channel_id=1, source_target_pairs={{0,1},{1,0},{2,3},{3,2},{4,5},{5,4},{6,7},{7,6},{8,9},{9,8},{10,11... | collective-permute-start | bytes 1572872 | tf_op jit(solution)/shard_map/ppermute | solution.py:24
  20.7 2.0 %collective-permute-start.10 = (bf16[32,32,128]{2,1,0:T(8,128)(2,1)S(1)}, bf16[32,32,128]{2,1,0:T(8,128)(2,1)S(1)}, u32[]{:S(2)}, u32[]{:S(2)}) collective-permute-start(bf16[32,32,128]{2,1,0:T(8,128)(2,1)S(1)} %get-tuple-element.58), channel_id=1, source_target_pairs={{0,1},{1,0},{2,3},{3,2},{4,5},{5,4},{6,7},{7,6},{8,9},{9,8},{10,11... | collective-permute-start | bytes 786440 | tf_op jit(solution)/shard_map/ppermute | solution.py:24
  20.8 7.5 %collective-permute-start.13 = (bf16[32,32,128]{2,1,0:T(8,128)(2,1)S(1)}, bf16[32,32,128]{2,1,0:T(8,128)(2,1)S(1)}, u32[]{:S(2)}, u32[]{:S(2)}) collective-permute-start(bf16[32,32,128]{2,1,0:T(8,128)(2,1)S(1)} %get-tuple-element.61), channel_id=1, source_target_pairs={{0,1},{1,0},{2,3},{3,2},{4,5},{5,4},{6,7},{7,6},{8,9},{9,8},{10,11... | collective-permute-start | bytes 786440 | tf_op jit(solution)/shard_map/ppermute | solution.py:24
  22.3 9.1 %collective-permute-start.12 = (f32[32,32,128]{2,1,0:T(8,128)S(1)}, f32[32,32,128]{2,1,0:T(8,128)S(1)}, u32[]{:S(2)}, u32[]{:S(2)}) collective-permute-start(f32[32,32,128]{2,1,0:T(8,128)S(1)} %pad_maximum_fusion), channel_id=1, source_target_pairs={{0,1},{1,0},{2,3},{3,2},{4,5},{5,4},{6,7},{7,6},{8,9},{9,8},{10,11... | collective-permute-start | bytes 1572872 | tf_op jit(solution)/shard_map/ppermute | solution.py:24
  22.8 8.6 %collective-permute-start.11 = (bf16[32,32,128]{2,1,0:T(8,128)(2,1)S(1)}, bf16[32,32,128]{2,1,0:T(8,128)(2,1)S(1)}, u32[]{:S(2)}, u32[]{:S(2)}) collective-permute-start(bf16[32,32,128]{2,1,0:T(8,128)(2,1)S(1)} %add_convert_fusion.1), channel_id=1, source_target_pairs={{0,2},{1,3},{2,0},{3,1},{4,6},{5,7},{6,4},{7,5},{8,10},{9,11},{10,... | collective-permute-start | bytes 786440 | tf_op jit(solution)/shard_map/ppermute | solution.py:24
  28.1 7.6 %copy-start.2 = (s32[4,4096]{1,0:T(4,128)S(1)}, s32[4,4096]{1,0:T(4,128)}, u32[]{:S(2)}) copy-start(s32[4,4096]{1,0:T(4,128)} %params) | copy-start | bytes 196612
  28.1 7.5 %copy-start.3 = (f32[4,4096]{1,0:T(4,128)S(1)}, f32[4,4096]{1,0:T(4,128)}, u32[]{:S(2)}) copy-start(f32[4,4096]{1,0:T(4,128)} %weights.1) | copy-start | bytes 196612
  28.1 7.5 %copy-start.4 = (s32[4096]{0:T(1024)S(1)}, s32[4096]{0:T(1024)}, u32[]{:S(2)}) copy-start(s32[4096]{0:T(1024)} %param.21) | copy-start | bytes 49156
  28.2 5.2 %collective-permute-start.14 = (f32[32,32,128]{2,1,0:T(8,128)S(1)}, f32[32,32,128]{2,1,0:T(8,128)S(1)}, u32[]{:S(2)}, u32[]{:S(2)}) collective-permute-start(f32[32,32,128]{2,1,0:T(8,128)S(1)} %pad_maximum_fusion.1), channel_id=1, source_target_pairs={{0,1},{1,0},{2,3},{3,2},{4,5},{5,4},{6,7},{7,6},{8,9},{9,8},{10,11... | collective-permute-start | bytes 1572872 | tf_op jit(solution)/shard_map/ppermute | solution.py:24
  31.6 6.4 %collective-permute-start.16 = (bf16[32,16,128]{2,1,0:T(8,128)(2,1)S(1)}, bf16[32,16,128]{2,1,0:T(8,128)(2,1)S(1)}, u32[]{:S(2)}, u32[]{:S(2)}) collective-permute-start(bf16[32,16,128]{2,1,0:T(8,128)(2,1)S(1)} %add_convert_fusion.2), channel_id=1, source_target_pairs={{0,2},{1,3},{2,0},{3,1},{4,6},{5,7},{6,4},{7,5},{8,10},{9,11},{10,... | collective-permute-start | bytes 393224 | tf_op jit(solution)/shard_map/ppermute | solution.py:24
  33.5 6.0 %collective-permute-start.15 = (bf16[32,16,128]{2,1,0:T(8,128)(2,1)S(1)}, bf16[32,16,128]{2,1,0:T(8,128)(2,1)S(1)}, u32[]{:S(2)}, u32[]{:S(2)}) collective-permute-start(bf16[32,16,128]{2,1,0:T(8,128)(2,1)S(1)} %fusion), channel_id=1, source_target_pairs={{0,2},{1,3},{2,0},{3,1},{4,6},{5,7},{6,4},{7,5},{8,10},{9,11},{10,... | collective-permute-start | bytes 393224 | tf_op jit(solution)/shard_map/ppermute | solution.py:24
  33.8 5.6 %collective-permute-start.18 = (bf16[32,16,128]{2,1,0:T(8,128)(2,1)S(1)}, bf16[32,16,128]{2,1,0:T(8,128)(2,1)S(1)}, u32[]{:S(2)}, u32[]{:S(2)}) collective-permute-start(bf16[32,16,128]{2,1,0:T(8,128)(2,1)S(1)} %get-tuple-element.77), channel_id=1, source_target_pairs={{0,5},{1,28},{2,7},{3,30},{4,9},{5,0},{6,11},{7,2},{8,13},{9,4},{1... | collective-permute-start | bytes 393224 | tf_op jit(solution)/shard_map/ppermute | solution.py:34
  34.1 7.7 %collective-permute-start.17 = (bf16[32,16,128]{2,1,0:T(8,128)(2,1)S(1)}, bf16[32,16,128]{2,1,0:T(8,128)(2,1)S(1)}, u32[]{:S(2)}, u32[]{:S(2)}) collective-permute-start(bf16[32,16,128]{2,1,0:T(8,128)(2,1)S(1)} %get-tuple-element.78), channel_id=1, source_target_pairs={{0,4},{1,29},{2,6},{3,31},{4,8},{5,1},{6,10},{7,3},{8,12},{9,5},{1... | collective-permute-start | bytes 393224 | tf_op jit(solution)/shard_map/ppermute | solution.py:34
